TPU v7x, 32 devices: a whole 2x2x4 slice. The times are simulated.
32 devices in a mesh: ctx: 16 (over z, x, core), tp: 2 (over y).
Axes of the slice: x: 2, y: 2, z: 4, core: 2. Of those that a mesh axis runs over, the one named last changes fastest.
Arguments:
- light_query: bfloat16 [4096, 8192], P('ctx', 'tp'), may hold values from -6 to 6
- light_key: bfloat16 [4096, 8192], P('ctx', 'tp'), may hold values from -6 to 6
- light_value: bfloat16 [4096, 8192], P('ctx', 'tp'), may hold values from -400 to 400
- log_decay: float32 [4096, 64], P('ctx', 'tp'), may hold values from -1 to 0
- out_gate: bfloat16 [4096, 8192], P('ctx', 'tp'), may hold values from -6 to 6
- norm_gain: float32 [8192], P('tp'), may hold values from 0.1 to 1.9
- soft_query: bfloat16 [4096, 8192], P('ctx', 'tp'), may hold values from -6 to 6
- soft_key: bfloat16 [4096, 1024], P('ctx', 'tp'), may hold values from -6 to 6
- soft_value: bfloat16 [4096, 1024], P('ctx', 'tp'), may hold values from -6 to 6
Outputs:
- light_out: bfloat16 [4096, 8192], P('ctx', 'tp')
- soft_out: bfloat16 [4096, 8192], P('ctx', 'tp')
All inputs are finite; a program needn't handle non-finite values.
Results may differ from a plain program's by a relative error of at most 0.0075.
Values may be sent and summed in bfloat16 or wider, within the bound.
No kernel may reach another device: no remote copies, remote signals or barrier semaphores. Data moves between devices by JAX's collectives and lax.ppermute only.
A program may use at most 384 MiB of HBM per device.

v0:
```python
import jax
import jax.numpy as jnp
from jax import lax
from jax.sharding import PartitionSpec as P

HEADS = 64
HD = 128
KV_HEADS = 8


def entering(value, axis, join, neutral):
    place = lax.axis_index(axis)
    gathered = jax.tree.map(
        lambda a, kind: lax.all_gather(a.astype(kind), axis), value, (jnp.bfloat16, jnp.bfloat16)
    )
    state = jax.tree.map(lambda a, e: jnp.zeros_like(a) + jnp.asarray(e, a.dtype), value, neutral)

    def one(lap, state):
        return join(
            state,
            jax.tree.map(
                lambda a, own: lax.dynamic_index_in_dim(a, lap, 0, False).astype(own.dtype),
                gathered,
                value,
            ),
        )

    return lax.fori_loop(0, place, one, state)


def local(
    light_query,
    light_key,
    light_value,
    log_decay,
    out_gate,
    norm_gain,
    soft_query,
    soft_key,
    soft_value,
):
    rows = light_query.shape[0]
    heads = log_decay.shape[1]
    query = light_query.reshape(rows, heads, HD)
    keyed = light_key.reshape(rows, heads, HD)
    valued = light_value.reshape(rows, heads, HD)
    cumulative = jnp.cumsum(log_decay, axis=0)
    final = cumulative[-1]
    causal = jnp.arange(rows)[:, None] >= jnp.arange(rows)[None, :]
    scores = jnp.einsum("thd,shd->hts", query, keyed, preferred_element_type=jnp.float32)
    ctime = cumulative.T
    spread = jnp.where(causal[None], ctime[:, :, None] - ctime[:, None, :], 0.0)
    weights = jnp.where(causal[None], scores * jnp.exp(spread), 0.0).astype(jnp.bfloat16)
    inner = jnp.einsum("hts,shd->thd", weights, valued, preferred_element_type=jnp.float32)
    decayed = keyed.astype(jnp.float32) * jnp.exp(final[None, :] - cumulative)[:, :, None]
    local_state = jnp.einsum(
        "shd,she->hde", decayed, valued.astype(jnp.float32), precision=lax.Precision.HIGHEST
    )
    empty_state = jnp.zeros((heads, HD, HD), jnp.float32)

    def combine(earlier, later):
        return (earlier[0] + later[0], jnp.exp(later[0])[:, None, None] * earlier[1] + later[1])

    identity = (jnp.zeros((heads,), jnp.float32), empty_state)
    _, incoming = entering((final, local_state), "ctx", combine, identity)
    carried = jnp.einsum(
        "thd,hde->the", query.astype(jnp.float32), incoming, precision=lax.Precision.HIGHEST
    )
    light_raw = (inner + jnp.exp(cumulative)[:, :, None] * carried).reshape(rows, heads * HD)
    square_sum = jnp.sum(light_raw * light_raw, axis=1)
    square_sum = lax.psum(square_sum, "tp")
    mean_square = square_sum / (HEADS * HD)
    light_out = (
        light_raw
        * lax.rsqrt(mean_square + 1e-06)[:, None]
        * norm_gain[None, :]
        * jax.nn.sigmoid(out_gate.astype(jnp.float32))
    )
    groups = HEADS // KV_HEADS
    kv_count = soft_key.shape[1] // HD
    soft_rows = soft_query.reshape(rows, kv_count, groups, HD)
    scale = HD ** (-0.5)
    own_start = lax.axis_index("ctx") * rows
    query_pos = own_start + jnp.arange(rows)
    top = jnp.full((kv_count, groups, rows), -1e30, jnp.float32)
    key_piece = lax.all_gather(soft_key, "ctx", axis=0, tiled=True)
    value_piece = lax.all_gather(soft_value, "ctx", axis=0, tiled=True)
    length = key_piece.shape[0]
    key_pos = jnp.arange(length)
    allowed = (key_pos[None, :] <= query_pos[:, None]) & (key_pos[None, :] >= 0)
    tile = (
        jnp.einsum(
            "tkgd,skd->kgts",
            soft_rows,
            key_piece.reshape(length, kv_count, HD),
            preferred_element_type=jnp.float32,
        )
        * scale
    )
    tile = jnp.where(allowed, tile, -1e30)
    new_top = jnp.maximum(top, jnp.max(tile, axis=-1))
    probs = jnp.where(allowed, jnp.exp(tile - new_top[..., None]), 0.0)
    total = jnp.sum(probs, axis=-1)
    update = jnp.einsum(
        "kgts,skd->kgtd",
        probs.astype(jnp.bfloat16),
        value_piece.reshape(length, kv_count, HD),
        preferred_element_type=jnp.float32,
    )
    accum = update
    top, total, accum = (new_top, total, accum)
    soft_out = (accum / total[..., None]).transpose(2, 0, 1, 3).reshape(rows, heads * HD)
    return (light_out.astype(jnp.bfloat16), soft_out.astype(jnp.bfloat16))


def solution(mesh):
    placed = (
        P("ctx", "tp"),
        P("ctx", "tp"),
        P("ctx", "tp"),
        P("ctx", "tp"),
        P("ctx", "tp"),
        P("tp"),
        P("ctx", "tp"),
        P("ctx", "tp"),
        P("ctx", "tp"),
    )
    return jax.shard_map(
        local,
        mesh=mesh,
        in_specs=placed,
        out_specs=(P("ctx", "tp"), P("ctx", "tp")),
        check_vma=False,
    )
```

profile of v0, /device:TPU:27, one launch (start us, length us, event | category | flops | bytes accessed | tf_op | source)
XLA Modules:
  0.0 352.7 jit_solution(15617582696315091476)
XLA Ops:
  11.4 4.1 %copy.79 = bf16[256,4096]{0,1:T(8,128)(2,1)} copy(bf16[256,4096]{1,0:T(8,128)(2,1)} %param.12) | data formatting | bytes 4194304 | tf_op jit(solution)/shard_map/reshape | solution.py:45
  16.4 5.7 %fusion.33 = bf16[32,128,128]{2,1,0:T(8,128)(2,1)} fusion(bf16[256,32,128]{0,2,1:T(8,128)(2,1)} %bitcast.113, f32[256,32]{0,1:T(8,128)S(1)} %get-tuple-element.66, bf16[256,4096]{1,0:T(8,128)(2,1)} %param.13), kind=kOutput, calls=%fused_computation.37 | convolution fusion | flops 1613234176 | bytes 5275648 | tf_op jit(solution)/shard_map/shd,she->hde/dot_general | solution.py:56
  22.3 6.4 %fusion.6 = f32[32,256,128]{1,2,0:T(8,128)} fusion(f32[32,256]{1,0:T(8,128)S(1)} %get-tuple-element.68, pred[256,256]{1,0:T(8,128)(4,1)S(1)} %iota_compare_fusion.1, bf16[256,32,128]{0,2,1:T(8,128)(2,1)} %bitcast.114, bf16[256,4096]{1,0:T(8,128)(2,1)} %param.13, bf16[256,4096]{1,0:T(8,128)(2,1)S(1)} %copy-done), kind=kOutput, calls=%fused_computation.10 | convolution fusion | flops 1084227584 | bytes 10584064 | tf_op jit(solution)/shard_map/hts,shd->thd/dot_general | solution.py:54
  28.7 17.0 %all-gather.1 = bf16[16,1,32]{2,1,0:T(2,128)(2,1)S(1)} all-gather(bf16[1,1,32]{2,1,0:T(2,128)(2,1)S(1)} %bitcast.120), channel_id=1, replica_groups=mesh['ctx'=16,'tp'=2] {'ctx'}, dimensions={0}, use_global_device_ids=true | all-gather | bytes 1088 | tf_op jit(solution)/shard_map/all_gather | solution.py:14
  50.4 9.4 %all-gather.8.cloned.1.call-done = bf16[4096,512]{1,0:T(8,128)(2,1)} async-done(((bf16[256,512]{1,0:T(8,128)(2,1)}), bf16[4096,512]{1,0:T(8,128)(2,1)}) %all-gather.8.cloned.1.call-update) | async-done | bytes 4194320 | tf_op jit(solution)/shard_map/all_gather | solution.py:87
  59.8 6.4 %copy.69 = bf16[4096,512]{0,1:T(8,128)(2,1)} copy(bf16[4096,512]{1,0:T(8,128)(2,1)} %all-gather.8.cloned.1.call-done) | data formatting | bytes 8388608 | tf_op jit(solution)/shard_map/all_gather | solution.py:87
  66.1 47.9 %all-gather.6.cloned.1.call-done = bf16[4096,512]{0,1:T(8,128)(2,1)} async-done(((bf16[256,512]{0,1:T(8,128)(2,1)}), bf16[4096,512]{0,1:T(8,128)(2,1)}) %all-gather.6.cloned.1.call-update) | async-done | bytes 4194320 | tf_op jit(solution)/shard_map/all_gather | solution.py:86
  114.0 50.7 %fusion = (f32[4,8,256]{2,1,0:T(8,128)S(1)}, f32[4,4096,256,8]{2,1,3,0:T(8,128)}) fusion(pred[256,4096]{0,1:T(8,128)(4,1)S(1)} %iota_compare_fusion, bf16[4096,4,128,1]{0,2,3,1:T(8,128)(2,1)} %bitcast.121, bf16[256,4,8,128]{3,2,1,0:T(8,128)(2,1)} %bitcast.115), kind=kOutput, calls=%fused_computation.4 | convolution fusion | flops 8690589696 | bytes 141590528 | tf_op jit(solution)/shard_map/tkgd,skd->kgts/dot_general | solution.py:92
  164.7 43.9 %fusion.1 = f32[4,8,256]{2,1,0:T(8,128)S(1)} fusion(f32[4,4096,256,8]{2,1,3,0:T(8,128)} %get-tuple-element.72, f32[4,8,256]{2,1,0:T(8,128)S(1)} %broadcast_maximum_fusion, pred[256,4096]{0,1:T(8,128)(4,1)S(1)} %iota_compare_fusion), kind=kLoop, calls=%fused_computation.5 | loop fusion | flops 167763968 | bytes 135331840 | tf_op jit(solution)/shard_map/reduce_sum | solution.py:103
  208.5 48.4 %fusion.7 = bf16[256,4,8,128]{0,3,2,1:T(8,128)(2,1)} fusion(bf16[4096,4,128,1]{0,2,3,1:T(8,128)(2,1)} %bitcast.111, f32[4,4096,256,8]{2,1,3,0:T(8,128)} %get-tuple-element.72, f32[4,8,256]{2,1,0:T(8,128)S(1)} %broadcast_maximum_fusion, pred[256,4096]{0,1:T(8,128)(4,1)S(1)} %iota_compare_fusion, f32[256,4,8]{0,2,1:T(8,128)S(1)} %bitcast.118), kind=kOutput, calls=%fused_computation.12 | convolution fusion | flops 8759803904 | bytes 141623296 | tf_op jit(solution)/shard_map/kgts,skd->kgtd/dot_general | solution.py:104
  257.0 4.1 %copy.71 = bf16[256,4096]{1,0:T(8,128)(2,1)} copy(bf16[256,4096]{0,1:T(8,128)(2,1)} %bitcast.116) | data formatting | bytes 4194304
  262.6 61.7 %while.12 = (s32[]{:T(128)}, f32[32,128,128]{2,1,0:T(8,128)}, s32[]{:T(128)}, bf16[16,32]{1,0:T(8,128)(2,1)}, bf16[16,32,128,128]{3,2,1,0:T(8,128)(2,1)}, /*index=5*/s32[]{:T(128)}, s32[]{:T(128)}, s32[]{:T(128)}) while((s32[]{:T(128)}, f32[32,128,128]{2,1,0:T(8,128)}, s32[]{:T(128)}, bf16[16,32]{1,0:T(8,128)(2,1)}, ...), condition=%wide.region_3.4_spmd, body=%wide.region_2.3_spmd.sunk | while | flops 1572901 | bytes 5243327 | solution.py:28
  263.3 3.5 convert_add_fusion.2
  267.3 3.5 convert_add_fusion.2
  271.4 3.5 convert_add_fusion.2
  275.5 3.5 convert_add_fusion.2
  279.6 3.5 convert_add_fusion.2
  283.7 3.5 convert_add_fusion.2
  287.8 3.5 convert_add_fusion.2
  291.9 3.5 convert_add_fusion.2
  324.3 7.1 %multiply_reduce_fusion = (f32[256]{0:T(256)S(1)}, f32[256,32,128]{0,2,1:T(8,128)}) fusion(f32[32,128,128]{2,1,0:T(8,128)} %get-tuple-element.46, f32[256,32]{0,1:T(8,128)S(1)} %copy-done.1, f32[32,256,128]{1,2,0:T(8,128)} %fusion.6, bf16[256,4096]{1,0:T(8,128)(2,1)S(1)} %copy-done), kind=kOutput, calls=%fused_computation.17 | convolution fusion | flops 1614806784 | bytes 12616704 | tf_op jit(solution)/shard_map/thd,hde->the/dot_general | solution.py:66
  331.4 5.6 %copy.65 = f32[256,4096]{1,0:T(8,128)} copy(f32[256,4096]{0,1:T(8,128)} %bitcast.110) | data formatting | bytes 8388608 | tf_op jit(solution)/shard_map/reshape | solution.py:69
  337.0 3.8 %psum.7 = f32[256]{0:T(256)S(1)} all-reduce(f32[256]{0:T(256)S(1)} %get-tuple-element.69), channel_id=1, replica_groups=mesh['ctx'=16,'tp'=2] {'tp'}, use_global_device_ids=true, to_apply=%region_5.6 | all-reduce | flops 256 | bytes 2048 | tf_op jit(solution)/shard_map/psum | solution.py:71
  340.8 5.4 %multiply_convert_fusion = bf16[256,4096]{1,0:T(8,128)(2,1)} fusion(bf16[256,4096]{1,0:T(8,128)(2,1)} %param.15, f32[256,4096]{1,0:T(8,128)} %copy.65, f32[4096]{0:T(1024)S(1)} %copy-done.2, f32[256]{0:T(256)S(1)} %add_rsqrt_fusion), kind=kLoop, calls=%fused_computation.16 | loop fusion | flops 8388608 | bytes 8406016 | tf_op jit(solution)/shard_map/convert_element_type | solution.py:113
  (53 shorter events, 45.7 us)
Async XLA Ops:
  7.2 15.1 %copy-start = (bf16[256,4096]{1,0:T(8,128)(2,1)S(1)}, bf16[256,4096]{1,0:T(8,128)(2,1)}, u32[]{:S(2)}) copy-start(bf16[256,4096]{1,0:T(8,128)(2,1)} %param.11) | copy-start | bytes 6291460
  7.2 52.6 %all-gather.8.cloned.1.call-start = ((), (), s32[]{:S(2)}) async-start(), calls=%async_computation.1 | async-start | bytes 4456448 | tf_op jit(solution)/shard_map/all_gather | solution.py:87
  7.9 106.1 %all-gather.6.cloned.1.call-start = ((), (), s32[]{:S(2)}) async-start(), calls=%async_computation | async-start | bytes 4456448 | tf_op jit(solution)/shard_map/all_gather | solution.py:86
  9.8 251.3 %all-gather.10.cloned.1.call-start = ((), (), s32[]{:S(2)}) async-start(), calls=%async_computation.2 | async-start | bytes 17825792 | tf_op jit(solution)/shard_map/all_gather | solution.py:14
  262.6 61.7 %copy-start.1 = (f32[256,32]{0,1:T(8,128)S(1)}, f32[256,32]{0,1:T(8,128)}, u32[]{:S(2)}) copy-start(f32[256,32]{0,1:T(8,128)} %get-tuple-element.65) | copy-start | bytes 98308
  331.4 9.4 %copy-start.2 = (f32[4096]{0:T(1024)S(1)}, f32[4096]{0:T(1024)}, u32[]{:S(2)}) copy-start(f32[4096]{0:T(1024)} %param.16) | copy-start | bytes 49156
Sparse Core Ops, SparseCore 0:
  10.2 49.5 all-gather.7
  62.5 51.4 all-gather.5
  116.2 124.7 all-gather.9
where the time goes:
time: 354 us; the launch traced here: 353 us
  matrix products  118 us (33%)
  other arithmetic  113 us (32%)
  waiting for transfers between devices  57.9 us (16%)
  local copies, waits for them, and re-layouts  28.8 us (8%)
  blocking collectives  20.8 us (6%)
  between operations  13.8 us (4%)
    add x15, other arithmetic, combine(): jnp.exp(later[0])[:, None, None] * earlier[1] + later[1]  51.8 us
    dot_general x1, matrix products, local(): jnp.einsum('tkgd,skd->kgts', soft_rows, key_piece.reshape(length, kv_coun...  50.7 us
    dot_general x1, matrix products, local(): jnp.einsum('kgts,skd->kgtd', probs.astype(jnp.bfloat16), value_piece.resh...  48.4 us
    all_gather x1, waiting for transfers between devices, local(): key_piece = lax.all_gather(soft_key, 'ctx', axis=0, tiled=True)  47.9 us
    reduce_sum x1, other arithmetic, local(): total = jnp.sum(probs, axis=-1)  43.9 us
    all_gather x1, blocking collectives, entering(): lax.all_gather(a.astype(kind), axis)  17 us
    exp x15, other arithmetic, combine(): jnp.exp(later[0])[:, None, None] * earlier[1] + later[1]  9.94 us
    unnamed x10, local copies, waits for them, and re-layouts  9.86 us
  transfers between devices with their start and end apart: 3, of which 2 were waited for; matrix products, arithmetic and copies ran while one was open for 51% of the time, Pallas kernels for 0%

commit v1 on v0

v1 whole, which is shorter than its diff:
```python
import functools
import math

import jax
import jax.numpy as jnp
from jax import lax
from jax.experimental import pallas as pl
from jax.experimental.pallas import tpu as pltpu
from jax.sharding import PartitionSpec as P

HD = 128
EPS = 1e-06
LOW = -1e30
PLANE = 4
TAIL = 16
VMEM = 60 * 2**20
F32 = jnp.float32
BF16 = jnp.bfloat16
HIGH = lax.Precision.HIGHEST
SCALE2 = HD ** (-0.5) * math.log2(math.e)


def params(**more):
    return pltpu.CompilerParams(vmem_limit_bytes=VMEM, **more)


def mm(a, b):
    return lax.dot_general(a, b, (((1,), (0,)), ((), ())), preferred_element_type=F32)


def mm_bt(a, b):
    return lax.dot_general(a, b, (((1,), (1,)), ((), ())), preferred_element_type=F32)


def mm_at(a, b):
    return lax.dot_general(a, b, (((0,), (0,)), ((), ())), preferred_element_type=F32)


def iota(shape, dim):
    return lax.broadcasted_iota(jnp.int32, shape, dim)


def state_kernel(pos, k_ref, v_ref, ld_ref, send_ref, keep_ref, cum_ref, cumt_ref, fin, *, qh, heads):
    step = pl.program_id(0)
    rows = ld_ref.shape[0]

    @pl.when(step == 0)
    def _():
        tri = (iota((rows, rows), 0) >= iota((rows, rows), 1)).astype(F32)
        ld = ld_ref[...]
        cum = lax.dot_general(tri, ld, (((1,), (0,)), ((), ())), precision=HIGH, preferred_element_type=F32)
        cumt = lax.dot_general(ld, tri, (((0,), (1,)), ((), ())), precision=HIGH, preferred_element_type=F32)
        ends = lax.dot_general(
            ld, jnp.ones((rows, HD), F32), (((0,), (0,)), ((), ())), precision=HIGH, preferred_element_type=F32
        )
        cum_ref[...] = jnp.zeros_like(cum_ref)
        cumt_ref[...] = jnp.zeros_like(cumt_ref)
        fin[...] = jnp.zeros_like(fin)
        for i in range(4):
            cum_ref[i, :, 0:qh] = cum[:, i * qh : (i + 1) * qh]
            cumt_ref[i, 0:qh, :] = cumt[i * qh : (i + 1) * qh, :]
            fin[i, 0:qh, :] = ends[i * qh : (i + 1) * qh, :]

    core = pos[2]
    kept = step // 2
    part = step % 2
    quarter = part * 2 + jnp.where(kept == 1, core, 1 - core)
    cum = cum_ref[quarter]
    weight = jnp.exp(cum[rows - 1 : rows, :] - cum)
    tail = fin[quarter]
    high = tail.astype(BF16).astype(F32)
    tail = jnp.concatenate([high, tail - high], axis=0).astype(BF16)
    states = []
    for i in range(qh):
        cols = slice(i * HD, (i + 1) * HD)
        keyed = (k_ref[:, cols].astype(F32) * weight[:, i : i + 1]).astype(BF16)
        states.append(mm_at(keyed, v_ref[:, cols]).astype(BF16))

    def put(ref):
        for i in range(qh):
            ref[part, i * HD : (i + 1) * HD, :] = states[i]
        ref[part, qh * HD : qh * HD + TAIL, :] = tail

    @pl.when(kept == 0)
    def _():
        put(send_ref)

    @pl.when(kept == 1)
    def _():
        put(keep_ref)


def local_state(pos, key, value, log_decay):
    rows, heads = log_decay.shape
    qh = heads // 4
    length = qh * HD + TAIL

    def columns(step, pos):
        core = pos[2]
        return (0, (step % 2) * 2 + jnp.where(step // 2 == 1, core, 1 - core))

    whole = lambda *shape: pl.BlockSpec(shape, lambda step, pos: (0,) * len(shape))
    return pl.pallas_call(
        functools.partial(state_kernel, qh=qh, heads=heads),
        grid_spec=pltpu.PrefetchScalarGridSpec(
            num_scalar_prefetch=1,
            grid=(4,),
            in_specs=[
                pl.BlockSpec((rows, qh * HD), columns),
                pl.BlockSpec((rows, qh * HD), columns),
                whole(rows, heads),
            ],
            out_specs=[
                whole(2, length, HD),
                whole(2, length, HD),
                whole(4, rows, HD),
                whole(4, 8, rows),
            ],
            scratch_shapes=[pltpu.VMEM((4, 8, HD), F32)],
        ),
        out_shape=[
            jax.ShapeDtypeStruct((2, length, HD), BF16),
            jax.ShapeDtypeStruct((2, length, HD), BF16),
            jax.ShapeDtypeStruct((4, rows, HD), F32),
            jax.ShapeDtypeStruct((4, 8, rows), F32),
        ],
        compiler_params=params(),
        cost_estimate=pl.CostEstimate(
            flops=2 * heads * rows * HD * HD * 4, bytes_accessed=rows * heads * HD * 4 + heads * HD * HD * 2, transcendentals=0
        ),
        name="local_state",
    )(pos, key, value, log_decay)


def spread(item, qh):
    tail = item[qh * HD : qh * HD + TAIL, :].astype(F32)
    return item[0 : qh * HD, :].astype(F32), tail[0:8, :] + tail[8:16, :]


def pack(states, logs):
    high = logs.astype(BF16).astype(F32)
    return states.astype(BF16), jnp.concatenate([high, logs - high], axis=0).astype(BF16)


def decay(states, logs, qh):
    factor = jnp.exp(logs)
    return jnp.concatenate(
        [states[i * HD : (i + 1) * HD, :] * factor[i : i + 1, :] for i in range(qh)], axis=0
    )


def joined(early, late, qh):
    return decay(early[0], late[1], qh) + late[0], early[1] + late[1]


def store(ref, item, qh):
    states, tail = pack(*item)
    ref[0 : qh * HD, :] = states
    ref[qh * HD : qh * HD + TAIL, :] = tail


def chip_kernel(pos, keep_ref, recv_ref, send_out, keep_out, *, qh):
    first = pos[2] == 0
    for out, part in ((send_out, 1 - pos[1]), (keep_out, pos[1])):
        own, other = keep_ref[part], recv_ref[part]
        early = spread(jnp.where(first, own, other), qh)
        late = spread(jnp.where(first, other, own), qh)
        store(out, joined(early, late, qh), qh)


def plane_kernel(pos, keep_ref, recv_ref, out, *, qh):
    first = pos[1] == 0
    own, other = keep_ref[...], recv_ref[...]
    early = spread(jnp.where(first, own, other), qh)
    late = spread(jnp.where(first, other, own), qh)
    store(out, joined(early, late, qh), qh)


def enter_kernel(pos, keep_ref, recv_ref, *refs, qh):
    planes, (send_out, keep_out) = refs[:-2], refs[-2:]
    total = None
    for ref in reversed(planes):
        item = spread(ref[...], qh)
        total = item if total is None else joined(total, item, qh)
    first = pos[1] == 0
    early = spread(jnp.where(first, keep_ref[...], recv_ref[...]), qh)
    if total is None:
        total = (jnp.zeros_like(early[0]), jnp.zeros_like(early[1]))
    later = joined(total, early, qh)
    zero, one = pack(*total), pack(*later)
    for out, take in ((send_out, first), (keep_out, jnp.logical_not(first))):
        out[0 : qh * HD, :] = jnp.where(take, one[0], zero[0])
        out[qh * HD : qh * HD + TAIL, :] = jnp.where(take, one[1], zero[1])


def core_kernel(pos, enter_keep, enter_recv, keep_ref, recv_ref, send_out, keep_out, *, qh):
    first = pos[2] == 0
    for part in range(2):
        entering = spread(jnp.where(pos[1] == part, enter_keep[...], enter_recv[...]), qh)
        own = spread(jnp.where(first, keep_ref[part], recv_ref[part]), qh)
        later = joined(entering, own, qh)[0].astype(BF16)
        now = entering[0].astype(BF16)
        send_out[part] = jnp.where(first, later, now)
        keep_out[part] = jnp.where(first, now, later)


def small(kernel, pos, arrays, outs, qh, name):
    nbytes = sum(a.size * 2 for a in arrays) + sum(math.prod(s) * 2 for s in outs)
    return pl.pallas_call(
        functools.partial(kernel, qh=qh),
        in_specs=[pl.BlockSpec(memory_space=pltpu.SMEM)] + [pl.BlockSpec(memory_space=pltpu.VMEM)] * len(arrays),
        out_specs=[pl.BlockSpec(memory_space=pltpu.VMEM)] * len(outs),
        out_shape=[jax.ShapeDtypeStruct(s, BF16) for s in outs],
        compiler_params=params(),
        cost_estimate=pl.CostEstimate(flops=nbytes, bytes_accessed=nbytes, transcendentals=0),
        name=name,
    )(pos, *arrays)


def intra_kernel(q_ref, k_ref, v_ref, cum_ref, cumt_ref, out_ref, *, qh):
    rows = q_ref.shape[0]
    causal = iota((rows, rows), 0) >= iota((rows, rows), 1)
    cum, cumt = cum_ref[0], cumt_ref[0]
    for i in range(qh):
        cols = slice(i * HD, (i + 1) * HD)
        scores = mm_bt(q_ref[:, cols], k_ref[:, cols])
        gap = jnp.where(causal, cum[:, i : i + 1] - cumt[i : i + 1, :], LOW)
        weights = (scores * jnp.exp(gap)).astype(BF16)
        out_ref[:, cols] = mm(weights, v_ref[:, cols])


def intra(query, key, value, cum, cumt):
    rows, width = query.shape
    wide = width // 4
    block = pl.BlockSpec((rows, wide), lambda i: (0, i))
    return pl.pallas_call(
        functools.partial(intra_kernel, qh=wide // HD),
        grid=(4,),
        in_specs=[
            block,
            block,
            block,
            pl.BlockSpec((1, rows, HD), lambda i: (i, 0, 0)),
            pl.BlockSpec((1, 8, rows), lambda i: (i, 0, 0)),
        ],
        out_specs=block,
        out_shape=jax.ShapeDtypeStruct((rows, width), F32),
        compiler_params=params(),
        cost_estimate=pl.CostEstimate(
            flops=8 * rows * rows * width, bytes_accessed=rows * width * 10, transcendentals=rows * rows * width // HD
        ),
        name="intra",
    )(query, key, value, cum, cumt)


def carry_kernel(pos, q_ref, intra_ref, cum_ref, keep_ref, recv_ref, out_ref, ss_ref, *, qh):
    quarter = pl.program_id(0)
    part = quarter // 2
    mine = quarter % 2 == pos[2]
    factor = jnp.exp(cum_ref[0])
    state = jnp.where(mine, keep_ref[part], recv_ref[part])
    total = jnp.zeros((q_ref.shape[0], HD), F32)
    for i in range(qh):
        cols = slice(i * HD, (i + 1) * HD)
        carried = mm(q_ref[:, cols], state[i * HD : (i + 1) * HD, :])
        raw = intra_ref[:, cols] + factor[:, i : i + 1] * carried
        out_ref[:, cols] = raw
        total = total + raw * raw

    @pl.when(quarter == 0)
    def _():
        ss_ref[...] = total

    @pl.when(quarter > 0)
    def _():
        ss_ref[...] += total


def carry(pos, query, inner, cum, keep, recv):
    rows, width = query.shape
    wide = width // 4
    block = pl.BlockSpec((rows, wide), lambda i: (0, i))
    whole = pl.BlockSpec(keep.shape, lambda i: (0, 0, 0))
    return pl.pallas_call(
        functools.partial(carry_kernel, qh=wide // HD),
        grid=(4,),
        in_specs=[
            pl.BlockSpec(memory_space=pltpu.SMEM),
            block,
            block,
            pl.BlockSpec((1, rows, HD), lambda i: (i, 0, 0)),
            whole,
            whole,
        ],
        out_specs=[block, pl.BlockSpec((rows, HD), lambda i: (0, 0))],
        out_shape=[jax.ShapeDtypeStruct((rows, width), F32), jax.ShapeDtypeStruct((rows, HD), F32)],
        input_output_aliases={2: 0},
        compiler_params=params(),
        cost_estimate=pl.CostEstimate(flops=4 * rows * width * HD, bytes_accessed=rows * width * 10, transcendentals=0),
        name="carry",
    )(pos, query, inner, cum, keep, recv)


def finish_kernel(raw_ref, ss_ref, gain_ref, gate_ref, out_ref, *, features):
    mean = jnp.sum(ss_ref[...], axis=1, keepdims=True) / features
    factor = lax.rsqrt(mean + EPS)
    gate = jax.nn.sigmoid(gate_ref[...].astype(F32))
    out_ref[...] = (raw_ref[...] * factor * gain_ref[...] * gate).astype(BF16)


def finish(raw, square, gain, gate, features):
    rows, width = raw.shape
    wide = width // 4
    block = pl.BlockSpec((rows, wide), lambda i: (0, i))
    return pl.pallas_call(
        functools.partial(finish_kernel, features=features),
        grid=(4,),
        in_specs=[
            block,
            pl.BlockSpec((rows, HD), lambda i: (0, 0)),
            pl.BlockSpec((1, wide), lambda i: (0, i)),
            block,
        ],
        out_specs=block,
        out_shape=jax.ShapeDtypeStruct((rows, width), BF16),
        compiler_params=params(),
        cost_estimate=pl.CostEstimate(flops=10 * rows * width, bytes_accessed=rows * width * 8, transcendentals=rows * width),
        name="finish",
    )(raw, square, gain.reshape(1, width), gate)


def soft_kernel(pos, q_ref, *refs, group, first, last, distance):
    keys, values, refs = refs[:PLANE], refs[PLANE : 2 * PLANE], refs[2 * PLANE :]
    if not first:
        acc_in, stat_in, refs = refs[0], refs[1], refs[2:]
    acc_out = refs[0]
    stat_out = None if last else refs[1]
    rows = q_ref.shape[0]
    lane = iota((rows, HD), 1)

    def attend():
        ones = jnp.ones((rows, HD), BF16)
        wide = [jnp.concatenate([v[...], ones], axis=1) for v in values]
        keyed = [k[...] for k in keys]
        if first:
            causal = iota((rows, rows), 0) >= iota((rows, rows), 1)
            x_later, core_later = pos[1] == 1, pos[2] == 1
            bias = [jnp.where(flag, 0.0, LOW).astype(F32) for flag in (x_later, core_later, x_later)]
        stat = jnp.zeros((rows, HD), F32)
        for g in range(group):
            cols = slice(g * HD, (g + 1) * HD)
            query = q_ref[:, cols]
            scores = [mm_bt(query, k) for k in keyed]
            if first:
                scores = [jnp.where(causal, scores[0], LOW)] + [s + b for s, b in zip(scores[1:], bias)]
            top = jnp.maximum(jnp.maximum(scores[0], scores[1]), jnp.maximum(scores[2], scores[3]))
            top = jnp.max(top, axis=1, keepdims=True)
            if not first:
                before = stat_in[0, :, g : g + 1]
                top = jnp.maximum(top, before)
            shift = top * SCALE2
            out = None
            for s, v in zip(scores, wide):
                probs = jnp.exp2(s * SCALE2 - shift).astype(BF16)
                piece = mm(probs, v)
                out = piece if out is None else out + piece
            summed, total = out[:, :HD], out[:, HD:]
            if not first:
                keep = jnp.exp2(before * SCALE2 - shift)
                summed = summed + keep * acc_in[:, cols]
                total = total + keep * stat_in[0, :, group + g : group + g + 1]
            if last:
                acc_out[:, cols] = (summed / total).astype(BF16)
            else:
                acc_out[:, cols] = summed
                stat = jnp.where(lane == g, top, stat)
                stat = jnp.where(lane == group + g, total, stat)
        if not last:
            stat_out[0] = stat

    def passing():
        for g in range(group):
            cols = slice(g * HD, (g + 1) * HD)
            if last:
                acc_out[:, cols] = (acc_in[:, cols] / stat_in[0, :, group + g : group + g + 1]).astype(BF16)
            else:
                acc_out[:, cols] = acc_in[:, cols]
        if not last:
            stat_out[0] = stat_in[0]

    if first:
        attend()
    else:
        pl.when(pos[0] >= distance)(attend)
        pl.when(pos[0] < distance)(passing)


def soft_step(pos, query, pieces, state, kv_count, distance, last):
    rows, width = query.shape
    halves = 2
    group = width // HD // kv_count // halves
    first = state is None
    block = pl.BlockSpec((rows, group * HD), lambda k, h: (0, k * halves + h))
    stat = pl.BlockSpec((1, rows, HD), lambda k, h: (k * halves + h, 0, 0))
    keys = pl.BlockSpec((rows, HD), lambda k, h: (0, k))
    values = pl.BlockSpec((rows, HD), lambda k, h: (0, kv_count + k))
    in_specs = [pl.BlockSpec(memory_space=pltpu.SMEM), block] + [keys] * PLANE + [values] * PLANE
    operands = [pos, query] + pieces + pieces
    aliases = {}
    if not first:
        if not last:
            aliases = {len(operands): 0, len(operands) + 1: 1}
        in_specs += [block, stat]
        operands += list(state)
    out_specs = [block]
    out_shape = [jax.ShapeDtypeStruct((rows, width), BF16 if last else F32)]
    if not last:
        out_specs.append(stat)
        out_shape.append(jax.ShapeDtypeStruct((kv_count * halves, rows, HD), F32))
    return pl.pallas_call(
        functools.partial(soft_kernel, group=group, first=first, last=last, distance=distance),
        grid=(kv_count, halves),
        in_specs=in_specs,
        out_specs=out_specs,
        out_shape=out_shape,
        input_output_aliases=aliases,
        compiler_params=params(),
        cost_estimate=pl.CostEstimate(
            flops=8 * rows * rows * PLANE * width, bytes_accessed=rows * width * 12, transcendentals=rows * rows * PLANE * width // HD
        ),
        name="softmax",
    )(*operands)


def local(
    light_query,
    light_key,
    light_value,
    log_decay,
    out_gate,
    norm_gain,
    soft_query,
    soft_key,
    soft_value,
    *,
    ctx,
    tp,
):
    rows, heads = log_decay.shape
    qh = heads // 4
    length = qh * HD + TAIL
    planes = ctx // PLANE
    kv_count = soft_key.shape[1] // HD
    place = lax.axis_index("ctx")
    pos = jnp.stack([place // 4, (place // 2) % 2, place % 2]).astype(jnp.int32)

    def over_core(a):
        return lax.ppermute(a, "ctx", [(i, i ^ 1) for i in range(ctx)])

    def over_x(a):
        return lax.ppermute(a, "ctx", [(i, i ^ 2) for i in range(ctx)])

    def over_z(a, d):
        return lax.ppermute(a, "ctx", [(i, i + PLANE * d) for i in range(ctx - PLANE * d)])

    paired = jnp.concatenate([soft_key, soft_value], axis=1)
    arrived = [paired] + [over_z(paired, d) for d in range(1, planes)]
    pieces = []
    for a in arrived:
        b = over_x(a)
        pieces.append([a, b, over_core(a), over_core(b)])

    send, keep, cum, cumt = local_state(pos, light_key, light_value, log_decay)
    other = over_core(send)
    quarter = (length, HD)
    chip_send, chip_keep = small(chip_kernel, pos, [keep, other], [quarter, quarter], qh, "chip")
    chip_other = over_x(chip_send)
    (plane,) = small(plane_kernel, pos, [chip_keep, chip_other], [quarter], qh, "plane")
    earlier = [over_z(plane, d) for d in range(1, planes)]
    enter_send, enter_keep = small(
        enter_kernel, pos, [chip_keep, chip_other] + earlier, [quarter, quarter], qh, "enter"
    )
    enter_other = over_x(enter_send)
    half = (2, qh * HD, HD)
    state_send, state_keep = small(
        core_kernel, pos, [enter_keep, enter_other, keep, other], [half, half], qh, "core"
    )
    state_other = over_core(state_send)

    inner = intra(light_query, light_key, light_value, cum, cumt)
    raw, square = carry(pos, light_query, inner, cum, state_keep, state_other)
    step = 1
    while step < tp:
        square = square + lax.ppermute(square, "tp", [(i, i ^ step) for i in range(tp)])
        step *= 2
    light_out = finish(raw, square, norm_gain, out_gate, heads * HD * tp)

    state = None
    for d, piece in enumerate(pieces):
        state = soft_step(pos, soft_query, piece, state, kv_count, d, d == planes - 1)
    return (light_out, state[0])


def solution(mesh):
    both = P("ctx", "tp")
    return jax.shard_map(
        functools.partial(local, ctx=mesh.shape["ctx"], tp=mesh.shape["tp"]),
        mesh=mesh,
        in_specs=(both, both, both, both, both, P("tp"), both, both, both),
        out_specs=(both, both),
        check_vma=False,
    )
```

time: 354 us -> 203 us (0.57)
  matrix products: 118 us -> 0 us
  Pallas kernels: 0 us -> 112 us
  other arithmetic: 113 us -> 1.29 us
  local copies, waits for them, and re-layouts: 28.8 us -> 4.7 us
  starting transfers between devices: 0.12 us -> 22.8 us
  blocking collectives: 20.8 us -> 0 us
  between operations: 13.8 us -> 0.89 us
    dot_general x5 -> x0, matrix products: 118 us -> none  [the longest x1 50.7 us: local(): jnp.einsum('tkgd,skd->kgts', soft_rows, key_piece.reshape(length, kv_coun...]
    pallas_call x0 -> x12, Pallas kernels: none -> 112 us  [the longest x4 75.5 us: soft_step(): pl.pallas_call(functools.partial(soft_kernel, group=group, first=first, l...]
    ppermute x0 -> x23, waiting for transfers between devices: none -> 59.6 us  [the longest x6 38.1 us: over_z(): lax.ppermute(a, 'ctx', [(i, i + PLANE * d) for i in range(ctx - PLANE * d)])]
    all_gather x3 -> x0, waiting for transfers between devices: 57.2 us -> none  [the longest x1 47.9 us: local(): key_piece = lax.all_gather(soft_key, 'ctx', axis=0, tiled=True)]
    add x16 -> x1, other arithmetic: 51.8 us -> 0.67 us  [local(): square + lax.ppermute(square, 'tp', [(i, i ^ step) for i in range(tp)])]
    reduce_sum x1 -> x0, other arithmetic: 43.9 us -> none  [local(): total = jnp.sum(probs, axis=-1)]
    ppermute x0 -> x23, starting transfers between devices: none -> 22.8 us  [the longest x10 9.2 us: over_core(): return lax.ppermute(a, 'ctx', [(i, i ^ 1) for i in range(ctx)])]
    all_gather x1 -> x0, blocking collectives: 17 us -> none  [entering(): lax.all_gather(a.astype(kind), axis)]
  transfers between devices with their start and end apart: 3 -> 23, of which waited for: 2 -> 6; matrix products, arithmetic and copies ran while one was open for 51% -> 0% of each run, Pallas kernels for 0% -> 48%
where the time goes in v1:
time: 203 us; the launch traced here: 201 us
  Pallas kernels  112 us (55%)
  waiting for transfers between devices  59.6 us (29%)
  starting transfers between devices  22.8 us (11%)
  local copies, waits for them, and re-layouts  4.7 us (2%)
    pallas_call x4, Pallas kernels, soft_step(): pl.pallas_call(functools.partial(soft_kernel, group=group, first=first, l...  75.5 us
    ppermute x6, waiting for transfers between devices, over_z(): lax.ppermute(a, 'ctx', [(i, i + PLANE * d) for i in range(ctx - PLANE * d)])  38.1 us
    ppermute x6, waiting for transfers between devices, over_x(): return lax.ppermute(a, 'ctx', [(i, i ^ 2) for i in range(ctx)])  19.8 us
    ppermute x10, starting transfers between devices, over_core(): return lax.ppermute(a, 'ctx', [(i, i ^ 1) for i in range(ctx)])  9.2 us
    pallas_call x4, Pallas kernels, small(): pl.pallas_call(functools.partial(kernel, qh=qh), in_specs=[pl.BlockSpec(m...  9.09 us
    pallas_call x1, Pallas kernels, local_state(): pl.pallas_call(functools.partial(state_kernel, qh=qh, heads=heads), grid_...  7.98 us
    ppermute x6, starting transfers between devices, over_z(): lax.ppermute(a, 'ctx', [(i, i + PLANE * d) for i in range(ctx - PLANE * d)])  7.89 us
    pallas_call x1, Pallas kernels, intra(): pl.pallas_call(functools.partial(intra_kernel, qh=wide // HD), grid=(4,),...  7.15 us
  transfers between devices with their start and end apart: 23, of which 6 were waited for; matrix products, arithmetic and copies ran while one was open for 0% of the time, Pallas kernels for 48%

profile of v1, /device:TPU:27, one launch (start us, length us, event | category | flops | bytes accessed | tf_op | source)
XLA Modules:
  0.0 200.8 jit_solution(3651879909600897423)
XLA Ops:
  0.7 1.5 copy.16.ld_ref
  2.8 8.0 %local_state.1 = (bf16[2,1040,128]{2,1,0:T(8,128)(2,1)}, bf16[2,1040,128]{2,1,0:T(8,128)(2,1)}, f32[4,256,128]{2,1,0:T(8,128)}, f32[4,8,256]{2,1,0:T(8,128)}) custom-call(s32[3]{0:T(128)} %pad_add_fusion.pos, bf16[256,4096]{1,0:T(8,128)(2,1)} %k_ref.3, bf16[256,4096]{1,0:T(8,128)(2,1)} %v_ref.3, f32[256,32]{1,0:T(8,128)} %copy.16.ld_ref), custom_call_target="tpu_custom_call" | custom-call | flops 1073741824 | bytes 5242880 | tf_op jit(solution)/shard_map/local_state/pallas_call | solution.py:103
  11.5 1.7 collective-permute-done.recv_ref
  14.0 2.1 %chip.1 = (bf16[1040,128]{1,0:T(8,128)(2,1)}, bf16[1040,128]{1,0:T(8,128)(2,1)}) custom-call(s32[3]{0:T(128)} %pad_add_fusion.pos, bf16[2,1040,128]{2,1,0:T(8,128)(2,1)} %get-tuple-element.22.keep_ref, bf16[2,1040,128]{2,1,0:T(8,128)(2,1)} %copy-done), custom_call_target="tpu_custom_call" | custom-call | flops 1597440 | bytes 1597440 | tf_op jit(solution)/shard_map/chip/pallas_call | solution.py:209
  17.7 1.3 collective-permute-start.16
  19.0 5.0 %collective-permute-done.1.recv_ref = bf16[1040,128]{1,0:T(8,128)(2,1)S(1)} collective-permute-done((bf16[1040,128]{1,0:T(8,128)(2,1)}, bf16[1040,128]{1,0:T(8,128)(2,1)S(1)}, u32[]{:S(2)}, u32[]{:S(2)}) %collective-permute-start.1) | collective-permute-done | bytes 266272 | tf_op jit(solution)/shard_map/ppermute | solution.py:461
  24.7 1.9 plane.1
  27.8 1.3 collective-permute-start.3
  29.1 1.3 collective-permute-start.4
  30.4 4.8 %collective-permute-done.20.refs_1_.refs_5_ = bf16[256,1024]{1,0:T(8,128)(2,1)S(1)} collective-permute-done((bf16[256,1024]{1,0:T(8,128)(2,1)S(1)}, bf16[256,1024]{1,0:T(8,128)(2,1)S(1)}, u32[]{:S(2)}, u32[]{:S(2)}) %collective-permute-start.20) | collective-permute-done | bytes 524320 | tf_op jit(solution)/shard_map/ppermute | solution.py:461
  36.4 1.3 collective-permute-start.12
  37.8 1.5 collective-permute-start.8
  39.3 38.0 %collective-permute-done.3.refs_1_ = bf16[1040,128]{1,0:T(8,128)(2,1)S(1)} collective-permute-done((bf16[1040,128]{1,0:T(8,128)(2,1)}, bf16[1040,128]{1,0:T(8,128)(2,1)S(1)}, u32[]{:S(2)}, u32[]{:S(2)}) %collective-permute-start.3) | collective-permute-done | bytes 266272 | tf_op jit(solution)/shard_map/ppermute | solution.py:464
  77.6 3.6 %collective-permute-start.22 = (bf16[256,1024]{1,0:T(8,128)(2,1)S(1)}, bf16[256,1024]{1,0:T(8,128)(2,1)}, u32[]{:S(2)}, u32[]{:S(2)}) collective-permute-start(bf16[256,1024]{1,0:T(8,128)(2,1)S(1)} %collective-permute-done.20.refs_1_.refs_5_), channel_id=1, source_target_pairs={{0,2},{2,0},{4,6},{6,4},{8,10},{10,8},{12,14},{14,12},{16,18},{18,... | collective-permute-start | bytes 1572872 | tf_op jit(solution)/shard_map/ppermute | solution.py:458
  81.1 7.2 %intra.1.intra_ref = f32[256,4096]{1,0:T(8,128)} custom-call(bf16[256,4096]{1,0:T(8,128)(2,1)} %q_ref.7, bf16[256,4096]{1,0:T(8,128)(2,1)} %k_ref.3, bf16[256,4096]{1,0:T(8,128)(2,1)} %v_ref.3, f32[4,256,128]{2,1,0:T(8,128)} %get-tuple-element.20.cum_ref, f32[4,8,256]{2,1,0:T(8,128)} %get-tuple-element.21.cumt_ref), custom_call_target="tpu_custom_call" | custom-call | flops 2147483648 | bytes 10485760 | tf_op jit(solution)/shard_map/intra/pallas_call | solution.py:236
  88.3 2.4 %enter.1 = (bf16[1040,128]{1,0:T(8,128)(2,1)}, bf16[1040,128]{1,0:T(8,128)(2,1)}) custom-call(s32[3]{0:T(128)} %pad_add_fusion.pos, bf16[1040,128]{1,0:T(8,128)(2,1)} %get-tuple-element.24.keep_ref, bf16[1040,128]{1,0:T(8,128)(2,1)} %copy-done.1, bf16[1040,128]{1,0:T(8,128)(2,1)} %copy-done.3, bf16[1040,128]{1,0:T(8,128)(2,1)} %copy-done.4, ...), custom_call_target="tpu_custom_call" | custom-call | flops 1863680 | bytes 1863680 | tf_op jit(solution)/shard_map/enter/pallas_call | solution.py:209
  94.5 16.3 %softmax.4 = (f32[256,4096]{1,0:T(8,128)}, f32[8,256,128]{2,1,0:T(8,128)}) custom-call(s32[3]{0:T(128)} %pad_add_fusion.pos, bf16[256,4096]{1,0:T(8,128)(2,1)} %q_ref.11, bf16[256,1024]{1,0:T(8,128)(2,1)} %copy-done.10, bf16[256,1024]{1,0:T(8,128)(2,1)} %copy-done.16, bf16[256,1024]{1,0:T(8,128)(2,1)} %collective-permute-done.21.refs_2_.refs_6_, ...), custom_call_target="tpu_custom_call" | custom-call | flops 8589934592 | bytes 12582912 | tf_op jit(solution)/shard_map/softmax/pallas_call | solution.py:420
  110.9 10.0 %collective-permute-done.5.enter_recv = bf16[1040,128]{1,0:T(8,128)(2,1)S(1)} collective-permute-done((bf16[1040,128]{1,0:T(8,128)(2,1)}, bf16[1040,128]{1,0:T(8,128)(2,1)S(1)}, u32[]{:S(2)}, u32[]{:S(2)}) %collective-permute-start.5) | collective-permute-done | bytes 266272 | tf_op jit(solution)/shard_map/ppermute | solution.py:461
  122.2 2.7 %core.1 = (bf16[2,1024,128]{2,1,0:T(8,128)(2,1)}, bf16[2,1024,128]{2,1,0:T(8,128)(2,1)}) custom-call(s32[3]{0:T(128)} %pad_add_fusion.pos, bf16[1040,128]{1,0:T(8,128)(2,1)} %get-tuple-element.26.enter_keep, bf16[1040,128]{1,0:T(8,128)(2,1)} %copy-done.6, bf16[2,1040,128]{2,1,0:T(8,128)(2,1)} %get-tuple-element.22.keep_ref, bf16[2,1040,128]{2,1,0:T(8,128)(2,1)} %copy-done), custom_call_target="tpu_custom_call" | custom-call | flops 2646016 | bytes 2646016 | tf_op jit(solution)/shard_map/core/pallas_call | solution.py:209
  126.3 20.0 %softmax.5 = (f32[256,4096]{1,0:T(8,128)}, f32[8,256,128]{2,1,0:T(8,128)}) custom-call(s32[3]{0:T(128)} %pad_add_fusion.pos, bf16[256,4096]{1,0:T(8,128)(2,1)} %q_ref.11, bf16[256,1024]{1,0:T(8,128)(2,1)} %copy-done.12, bf16[256,1024]{1,0:T(8,128)(2,1)} %copy-done.15, ...), custom_call_target="tpu_custom_call", output_to_operand_aliasing={{0}: (10, {}), {1}: (11, {})} | custom-call | flops 8589934592 | bytes 12582912 | tf_op jit(solution)/shard_map/softmax/pallas_call | solution.py:420
  146.4 20.1 %softmax.6 = (f32[256,4096]{1,0:T(8,128)}, f32[8,256,128]{2,1,0:T(8,128)}) custom-call(s32[3]{0:T(128)} %pad_add_fusion.pos, bf16[256,4096]{1,0:T(8,128)(2,1)} %q_ref.11, bf16[256,1024]{1,0:T(8,128)(2,1)} %copy-done.13, bf16[256,1024]{1,0:T(8,128)(2,1)} %copy-done.17, ...), custom_call_target="tpu_custom_call", output_to_operand_aliasing={{0}: (10, {}), {1}: (11, {})} | custom-call | flops 8589934592 | bytes 12582912 | tf_op jit(solution)/shard_map/softmax/pallas_call | solution.py:420
  167.2 6.6 %carry.1 = (f32[256,4096]{1,0:T(8,128)}, f32[256,128]{1,0:T(8,128)}) custom-call(s32[3]{0:T(128)} %pad_add_fusion.pos, bf16[256,4096]{1,0:T(8,128)(2,1)} %q_ref.7, f32[256,4096]{1,0:T(8,128)} %intra.1.intra_ref, f32[4,256,128]{2,1,0:T(8,128)} %get-tuple-element.20.cum_ref, ...), custom_call_target="tpu_custom_call", output_to_operand_aliasing={{0}: (2, {})} | custom-call | flops 536870912 | bytes 10485760 | tf_op jit(solution)/shard_map/carry/pallas_call | solution.py:284
  175.9 19.1 %softmax.7 = bf16[256,4096]{1,0:T(8,128)(2,1)} custom-call(s32[3]{0:T(128)} %pad_add_fusion.pos, bf16[256,4096]{1,0:T(8,128)(2,1)} %q_ref.11, bf16[256,1024]{1,0:T(8,128)(2,1)} %copy-done.11, bf16[256,1024]{1,0:T(8,128)(2,1)} %copy-done.14, bf16[256,1024]{1,0:T(8,128)(2,1)} %copy-done.18, bf16[256,1024]{1,0:T(8,128)(2,1)} %collective-permute-done.11.refs_3_.refs_7_, ...), custom_call_target="tpu_custom_call" | custom-call | flops 8589934592 | bytes 12582912 | tf_op jit(solution)/shard_map/softmax/pallas_call | solution.py:420
  195.6 5.2 %finish.1 = bf16[256,4096]{1,0:T(8,128)(2,1)} custom-call(f32[256,4096]{1,0:T(8,128)} %get-tuple-element.30.raw_ref, f32[256,128]{1,0:T(8,128)} %add.14.ss_ref, f32[1,4096]{1,0:T(1,128)} %bitcast.4, bf16[256,4096]{1,0:T(8,128)(2,1)} %gate_ref.1), custom_call_target="tpu_custom_call" | custom-call | flops 10485760 | bytes 8388608 | tf_op jit(solution)/shard_map/finish/pallas_call | solution.py:315
  (77 shorter events, 17.3 us)
Async XLA Ops:
  10.8 2.4 %collective-permute-start = (bf16[2,1040,128]{2,1,0:T(8,128)(2,1)}, bf16[2,1040,128]{2,1,0:T(8,128)(2,1)S(1)}, u32[]{:S(2)}, u32[]{:S(2)}) collective-permute-start(bf16[2,1040,128]{2,1,0:T(8,128)(2,1)} %get-tuple-element.23), channel_id=1, source_target_pairs={{0,2},{2,0},{4,6},{6,4},{8,10},{10,8},{12,14},{14,12},{16,18},{18,... | collective-permute-start | bytes 1597448 | tf_op jit(solution)/shard_map/ppermute | solution.py:458
  16.2 7.8 %collective-permute-start.1 = (bf16[1040,128]{1,0:T(8,128)(2,1)}, bf16[1040,128]{1,0:T(8,128)(2,1)S(1)}, u32[]{:S(2)}, u32[]{:S(2)}) collective-permute-start(bf16[1040,128]{1,0:T(8,128)(2,1)} %get-tuple-element.25), channel_id=1, source_target_pairs={{0,4},{2,6},{4,0},{6,2},{8,12},{10,14},{12,8},{14,10},{16,20},{18,... | collective-permute-start | bytes 798728 | tf_op jit(solution)/shard_map/ppermute | solution.py:461
  16.5 74.2 %copy-start.10 = (bf16[256,1024]{1,0:T(8,128)(2,1)}, bf16[256,1024]{1,0:T(8,128)(2,1)S(1)}, u32[]{:S(2)}) copy-start(bf16[256,1024]{1,0:T(8,128)(2,1)S(1)} %constant_dynamic-update-slice_fusion.refs_0_.refs_4_) | copy-start | bytes 1572868
  16.5 18.8 %collective-permute-start.20 = (bf16[256,1024]{1,0:T(8,128)(2,1)S(1)}, bf16[256,1024]{1,0:T(8,128)(2,1)S(1)}, u32[]{:S(2)}, u32[]{:S(2)}) collective-permute-start(bf16[256,1024]{1,0:T(8,128)(2,1)S(1)} %constant_dynamic-update-slice_fusion.refs_0_.refs_4_), channel_id=1, source_target_pairs={{0,4},{2,6},{4,0},{6,2},{8,12},{10,14},{12,8},{14,10},{16,20},{18,... | collective-permute-start | bytes 1572872 | tf_op jit(solution)/shard_map/ppermute | solution.py:461
  17.7 18.7 %collective-permute-start.16 = (bf16[256,1024]{1,0:T(8,128)(2,1)S(1)}, bf16[256,1024]{1,0:T(8,128)(2,1)S(1)}, u32[]{:S(2)}, u32[]{:S(2)}) collective-permute-start(bf16[256,1024]{1,0:T(8,128)(2,1)S(1)} %constant_dynamic-update-slice_fusion.refs_0_.refs_4_), channel_id=1, source_target_pairs={{0,8},{2,10},{4,12},{6,14},{8,16},{10,18},{12,20},{14,22},{16,24},... | collective-permute-start | bytes 1572872 | tf_op jit(solution)/shard_map/ppermute | solution.py:464
  26.6 11.3 %collective-permute-start.2 = (bf16[1040,128]{1,0:T(8,128)(2,1)}, bf16[1040,128]{1,0:T(8,128)(2,1)S(1)}, u32[]{:S(2)}, u32[]{:S(2)}) collective-permute-start(bf16[1040,128]{1,0:T(8,128)(2,1)} %plane.1), channel_id=1, source_target_pairs={{0,8},{2,10},{4,12},{6,14},{8,16},{10,18},{12,20},{14,22},{16,24},... | collective-permute-start | bytes 798728 | tf_op jit(solution)/shard_map/ppermute | solution.py:464
  27.8 49.4 %collective-permute-start.3 = (bf16[1040,128]{1,0:T(8,128)(2,1)}, bf16[1040,128]{1,0:T(8,128)(2,1)S(1)}, u32[]{:S(2)}, u32[]{:S(2)}) collective-permute-start(bf16[1040,128]{1,0:T(8,128)(2,1)} %plane.1), channel_id=1, source_target_pairs={{0,16},{2,18},{4,20},{6,22},{8,24},{10,26},{12,28},{14,30},{1,17},... | collective-permute-start | bytes 798728 | tf_op jit(solution)/shard_map/ppermute | solution.py:464
  29.1 48.4 %collective-permute-start.4 = (bf16[1040,128]{1,0:T(8,128)(2,1)}, bf16[1040,128]{1,0:T(8,128)(2,1)S(1)}, u32[]{:S(2)}, u32[]{:S(2)}) collective-permute-start(bf16[1040,128]{1,0:T(8,128)(2,1)} %plane.1), channel_id=1, source_target_pairs={{0,24},{2,26},{4,28},{6,30},{1,25},{3,27},{5,29},{7,31}} | collective-permute-start | bytes 798728 | tf_op jit(solution)/shard_map/ppermute | solution.py:464
  35.2 55.4 %collective-permute-start.21 = (bf16[256,1024]{1,0:T(8,128)(2,1)S(1)}, bf16[256,1024]{1,0:T(8,128)(2,1)}, u32[]{:S(2)}, u32[]{:S(2)}) collective-permute-start(bf16[256,1024]{1,0:T(8,128)(2,1)S(1)} %constant_dynamic-update-slice_fusion.refs_0_.refs_4_), channel_id=1, source_target_pairs={{0,2},{2,0},{4,6},{6,4},{8,10},{10,8},{12,14},{14,12},{16,18},{18,... | collective-permute-start | bytes 1572872 | tf_op jit(solution)/shard_map/ppermute | solution.py:458
  36.4 54.4 %collective-permute-start.12 = (bf16[256,1024]{1,0:T(8,128)(2,1)S(1)}, bf16[256,1024]{1,0:T(8,128)(2,1)S(1)}, u32[]{:S(2)}, u32[]{:S(2)}) collective-permute-start(bf16[256,1024]{1,0:T(8,128)(2,1)S(1)} %constant_dynamic-update-slice_fusion.refs_0_.refs_4_), channel_id=1, source_target_pairs={{0,16},{2,18},{4,20},{6,22},{8,24},{10,26},{12,28},{14,30},{1,17},... | collective-permute-start | bytes 1572872 | tf_op jit(solution)/shard_map/ppermute | solution.py:464
  37.8 54.3 %collective-permute-start.8 = (bf16[256,1024]{1,0:T(8,128)(2,1)S(1)}, bf16[256,1024]{1,0:T(8,128)(2,1)S(1)}, u32[]{:S(2)}, u32[]{:S(2)}) collective-permute-start(bf16[256,1024]{1,0:T(8,128)(2,1)S(1)} %constant_dynamic-update-slice_fusion.refs_0_.refs_4_), channel_id=1, source_target_pairs={{0,24},{2,26},{4,28},{6,30},{1,25},{3,27},{5,29},{7,31}} | collective-permute-start | bytes 1572872 | tf_op jit(solution)/shard_map/ppermute | solution.py:464
  77.3 15.0 %collective-permute-start.17 = (bf16[256,1024]{1,0:T(8,128)(2,1)S(1)}, bf16[256,1024]{1,0:T(8,128)(2,1)S(1)}, u32[]{:S(2)}, u32[]{:S(2)}) collective-permute-start(bf16[256,1024]{1,0:T(8,128)(2,1)S(1)} %collective-permute-done.16.refs_0_.refs_4_), channel_id=1, source_target_pairs={{0,4},{2,6},{4,0},{6,2},{8,12},{10,14},{12,8},{14,10},{16,20},{18,... | collective-permute-start | bytes 1572872 | tf_op jit(solution)/shard_map/ppermute | solution.py:461
  77.6 15.7 %collective-permute-start.22 = (bf16[256,1024]{1,0:T(8,128)(2,1)S(1)}, bf16[256,1024]{1,0:T(8,128)(2,1)}, u32[]{:S(2)}, u32[]{:S(2)}) collective-permute-start(bf16[256,1024]{1,0:T(8,128)(2,1)S(1)} %collective-permute-done.20.refs_1_.refs_5_), channel_id=1, source_target_pairs={{0,2},{2,0},{4,6},{6,4},{8,10},{10,8},{12,14},{14,12},{16,18},{18,... | collective-permute-start | bytes 1572872 | tf_op jit(solution)/shard_map/ppermute | solution.py:458
  90.7 34.2 %collective-permute-start.18 = (bf16[256,1024]{1,0:T(8,128)(2,1)S(1)}, bf16[256,1024]{1,0:T(8,128)(2,1)}, u32[]{:S(2)}, u32[]{:S(2)}) collective-permute-start(bf16[256,1024]{1,0:T(8,128)(2,1)S(1)} %collective-permute-done.16.refs_0_.refs_4_), channel_id=1, source_target_pairs={{0,2},{2,0},{4,6},{6,4},{8,10},{10,8},{12,14},{14,12},{16,18},{18,... | collective-permute-start | bytes 1572872 | tf_op jit(solution)/shard_map/ppermute | solution.py:458
  90.9 34.8 %collective-permute-start.13 = (bf16[256,1024]{1,0:T(8,128)(2,1)S(1)}, bf16[256,1024]{1,0:T(8,128)(2,1)S(1)}, u32[]{:S(2)}, u32[]{:S(2)}) collective-permute-start(bf16[256,1024]{1,0:T(8,128)(2,1)S(1)} %collective-permute-done.12.refs_0_.refs_4_), channel_id=1, source_target_pairs={{0,4},{2,6},{4,0},{6,2},{8,12},{10,14},{12,8},{14,10},{16,20},{18,... | collective-permute-start | bytes 1572872 | tf_op jit(solution)/shard_map/ppermute | solution.py:461
  92.1 33.7 %collective-permute-start.9 = (bf16[256,1024]{1,0:T(8,128)(2,1)S(1)}, bf16[256,1024]{1,0:T(8,128)(2,1)S(1)}, u32[]{:S(2)}, u32[]{:S(2)}) collective-permute-start(bf16[256,1024]{1,0:T(8,128)(2,1)S(1)} %collective-permute-done.8.refs_0_.refs_4_), channel_id=1, source_target_pairs={{0,4},{2,6},{4,0},{6,2},{8,12},{10,14},{12,8},{14,10},{16,20},{18,... | collective-permute-start | bytes 1572872 | tf_op jit(solution)/shard_map/ppermute | solution.py:461
  92.3 33.8 %collective-permute-start.19 = (bf16[256,1024]{1,0:T(8,128)(2,1)S(1)}, bf16[256,1024]{1,0:T(8,128)(2,1)}, u32[]{:S(2)}, u32[]{:S(2)}) collective-permute-start(bf16[256,1024]{1,0:T(8,128)(2,1)S(1)} %collective-permute-done.17.refs_1_.refs_5_), channel_id=1, source_target_pairs={{0,2},{2,0},{4,6},{6,4},{8,10},{10,8},{12,14},{14,12},{16,18},{18,... | collective-permute-start | bytes 1572872 | tf_op jit(solution)/shard_map/ppermute | solution.py:458
  93.3 27.6 %collective-permute-start.5 = (bf16[1040,128]{1,0:T(8,128)(2,1)}, bf16[1040,128]{1,0:T(8,128)(2,1)S(1)}, u32[]{:S(2)}, u32[]{:S(2)}) collective-permute-start(bf16[1040,128]{1,0:T(8,128)(2,1)} %get-tuple-element.27), channel_id=1, source_target_pairs={{0,4},{2,6},{4,0},{6,2},{8,12},{10,14},{12,8},{14,10},{16,20},{18,... | collective-permute-start | bytes 798728 | tf_op jit(solution)/shard_map/ppermute | solution.py:461
  120.9 25.4 %collective-permute-start.14 = (bf16[256,1024]{1,0:T(8,128)(2,1)S(1)}, bf16[256,1024]{1,0:T(8,128)(2,1)}, u32[]{:S(2)}, u32[]{:S(2)}) collective-permute-start(bf16[256,1024]{1,0:T(8,128)(2,1)S(1)} %collective-permute-done.12.refs_0_.refs_4_), channel_id=1, source_target_pairs={{0,2},{2,0},{4,6},{6,4},{8,10},{10,8},{12,14},{14,12},{16,18},{18,... | collective-permute-start | bytes 1572872 | tf_op jit(solution)/shard_map/ppermute | solution.py:458
  124.9 50.2 %collective-permute-start.10 = (bf16[256,1024]{1,0:T(8,128)(2,1)S(1)}, bf16[256,1024]{1,0:T(8,128)(2,1)S(1)}, u32[]{:S(2)}, u32[]{:S(2)}) collective-permute-start(bf16[256,1024]{1,0:T(8,128)(2,1)S(1)} %collective-permute-done.8.refs_0_.refs_4_), channel_id=1, source_target_pairs={{0,2},{2,0},{4,6},{6,4},{8,10},{10,8},{12,14},{14,12},{16,18},{18,... | collective-permute-start | bytes 1572872 | tf_op jit(solution)/shard_map/ppermute | solution.py:458
  125.7 20.7 %collective-permute-start.15 = (bf16[256,1024]{1,0:T(8,128)(2,1)S(1)}, bf16[256,1024]{1,0:T(8,128)(2,1)}, u32[]{:S(2)}, u32[]{:S(2)}) collective-permute-start(bf16[256,1024]{1,0:T(8,128)(2,1)S(1)} %collective-permute-done.13.refs_1_.refs_5_), channel_id=1, source_target_pairs={{0,2},{2,0},{4,6},{6,4},{8,10},{10,8},{12,14},{14,12},{16,18},{18,... | collective-permute-start | bytes 1572872 | tf_op jit(solution)/shard_map/ppermute | solution.py:458
  125.8 49.3 %collective-permute-start.11 = (bf16[256,1024]{1,0:T(8,128)(2,1)S(1)}, bf16[256,1024]{1,0:T(8,128)(2,1)}, u32[]{:S(2)}, u32[]{:S(2)}) collective-permute-start(bf16[256,1024]{1,0:T(8,128)(2,1)S(1)} %collective-permute-done.9.refs_1_.refs_5_), channel_id=1, source_target_pairs={{0,2},{2,0},{4,6},{6,4},{8,10},{10,8},{12,14},{14,12},{16,18},{18,... | collective-permute-start | bytes 1572872 | tf_op jit(solution)/shard_map/ppermute | solution.py:458
  126.2 40.3 %collective-permute-start.6 = (bf16[2,1024,128]{2,1,0:T(8,128)(2,1)}, bf16[2,1024,128]{2,1,0:T(8,128)(2,1)S(1)}, u32[]{:S(2)}, u32[]{:S(2)}) collective-permute-start(bf16[2,1024,128]{2,1,0:T(8,128)(2,1)} %get-tuple-element.29), channel_id=1, source_target_pairs={{0,2},{2,0},{4,6},{6,4},{8,10},{10,8},{12,14},{14,12},{16,18},{18,... | collective-permute-start | bytes 1572872 | tf_op jit(solution)/shard_map/ppermute | solution.py:458
  173.8 21.2 %collective-permute-start.7 = (f32[256,128]{1,0:T(8,128)}, f32[256,128]{1,0:T(8,128)S(1)}, u32[]{:S(2)}, u32[]{:S(2)}) collective-permute-start(f32[256,128]{1,0:T(8,128)} %get-tuple-element.31), channel_id=1, source_target_pairs={{0,1},{1,0},{2,3},{3,2},{4,5},{5,4},{6,7},{7,6},{8,9},{9,8},{10,11... | collective-permute-start | bytes 393224 | tf_op jit(solution)/shard_map/ppermute | solution.py:494
  (18 other events, 354.2 us)

commit v2 on v1

v2 whole, which is shorter than its diff:
```python
import functools
import math

import jax
import jax.numpy as jnp
from jax import lax
from jax.experimental import pallas as pl
from jax.experimental.pallas import tpu as pltpu
from jax.sharding import PartitionSpec as P

HD = 128
EPS = 1e-06
LOW = -1e30
PLANE = 4
TAIL = 16
VMEM = 60 * 2**20
F32 = jnp.float32
BF16 = jnp.bfloat16
HIGH = lax.Precision.HIGHEST
SCALAR = pl.BlockSpec(memory_space=pltpu.SMEM)
ANY = pl.BlockSpec(memory_space=pl.ANY)
NEXT = jax.ShapeDtypeStruct((1,), jnp.int32)
COST = pl.CostEstimate(flops=1000, bytes_accessed=2**20, transcendentals=0)
SCALE2 = HD ** (-0.5) * math.log2(math.e)


def params(**more):
    return pltpu.CompilerParams(vmem_limit_bytes=VMEM, **more)


def mm(a, b):
    return lax.dot_general(a, b, (((1,), (0,)), ((), ())), preferred_element_type=F32)


def mm_bt(a, b):
    return lax.dot_general(a, b, (((1,), (1,)), ((), ())), preferred_element_type=F32)


def mm_at(a, b):
    return lax.dot_general(a, b, (((0,), (0,)), ((), ())), preferred_element_type=F32)


def z_of(pos):
    return pos[0] // PLANE


def x_of(pos):
    return (pos[0] // 2) % 2


def core_of(pos):
    return pos[0] % 2


def iota(shape, dim):
    return lax.broadcasted_iota(jnp.int32, shape, dim)


def state_kernel(pos, k_ref, v_ref, ld_ref, send_ref, keep_ref, cum_ref, cumt_ref, after, fin, *, qh, heads):
    after[0] = pos[0]
    step = pl.program_id(0)
    rows = ld_ref.shape[1]

    @pl.when(step == 0)
    def _():
        upper = (iota((rows, rows), 0) <= iota((rows, rows), 1)).astype(F32).astype(BF16)
        ld = ld_ref[...]
        high = ld.astype(BF16)
        rest = ld - high.astype(F32)
        middle = rest.astype(BF16)
        low = (rest - middle.astype(F32)).astype(BF16)
        cumt = mm(high, upper) + (mm(middle, upper) + mm(low, upper))
        full = jnp.concatenate([cumt, jnp.zeros((HD - heads, rows), F32)], axis=0)
        cum = jnp.transpose(full)
        ends = jnp.broadcast_to(cumt[:, rows - 1 : rows], (heads, HD))
        fin[...] = jnp.zeros_like(fin)
        cumt_ref[...] = jnp.zeros_like(cumt_ref)
        cum_ref[...] = jnp.zeros_like(cum_ref)
        for i in range(4):
            cum_ref[i, :, 0:qh] = cum[:, i * qh : (i + 1) * qh]
            cumt_ref[i, 0:qh, :] = cumt[i * qh : (i + 1) * qh, :]
            fin[i, 0:qh, :] = ends[i * qh : (i + 1) * qh, :]

    core = pos[0] & 1
    kept = step // 2
    part = step % 2
    quarter = part * 2 + jnp.where(kept == 1, core, 1 - core)
    cum = cum_ref[quarter]
    weight = jnp.exp(cum[rows - 1 : rows, :] - cum)
    tail = fin[quarter]
    high = tail.astype(BF16).astype(F32)
    tail = jnp.concatenate([high, tail - high], axis=0).astype(BF16)
    states = []
    for i in range(qh):
        cols = slice(i * HD, (i + 1) * HD)
        keyed = (k_ref[:, cols].astype(F32) * weight[:, i : i + 1]).astype(BF16)
        states.append(mm_at(keyed, v_ref[:, cols]).astype(BF16))

    def put(ref):
        for i in range(qh):
            ref[part, i * HD : (i + 1) * HD, :] = states[i]
        ref[part, qh * HD : qh * HD + TAIL, :] = tail

    @pl.when(kept == 0)
    def _():
        put(send_ref)

    @pl.when(kept == 1)
    def _():
        put(keep_ref)


def local_state(pos, key, value, log_decay):
    heads, rows = log_decay.shape
    qh = heads // 4
    length = qh * HD + TAIL

    def columns(step, pos):
        core = pos[0] & 1
        return (0, (step % 2) * 2 + jnp.where(step // 2 == 1, core, 1 - core))

    whole = lambda *shape: pl.BlockSpec(shape, lambda step, pos: (0,) * len(shape))
    return pl.pallas_call(
        functools.partial(state_kernel, qh=qh, heads=heads),
        grid_spec=pltpu.PrefetchScalarGridSpec(
            num_scalar_prefetch=1,
            grid=(4,),
            in_specs=[
                pl.BlockSpec((rows, qh * HD), columns),
                pl.BlockSpec((rows, qh * HD), columns),
                whole(heads, rows),
            ],
            out_specs=[
                whole(2, length, HD),
                whole(2, length, HD),
                whole(4, rows, HD),
                whole(4, 8, rows),
                SCALAR,
            ],
            scratch_shapes=[pltpu.VMEM((4, 8, HD), F32)],
        ),
        out_shape=[
            jax.ShapeDtypeStruct((2, length, HD), BF16),
            jax.ShapeDtypeStruct((2, length, HD), BF16),
            jax.ShapeDtypeStruct((4, rows, HD), F32),
            jax.ShapeDtypeStruct((4, 8, rows), F32),
            NEXT,
        ],
        compiler_params=params(),
        cost_estimate=COST,
        name="local_state",
    )(pos, key, value, log_decay)


def spread(item, qh):
    tail = item[qh * HD : qh * HD + TAIL, :].astype(F32)
    return item[0 : qh * HD, :].astype(F32), tail[0:8, :] + tail[8:16, :]


def pack(states, logs):
    high = logs.astype(BF16).astype(F32)
    return states.astype(BF16), jnp.concatenate([high, logs - high], axis=0).astype(BF16)


def decay(states, logs, qh):
    factor = jnp.exp(logs)
    return jnp.concatenate(
        [states[i * HD : (i + 1) * HD, :] * factor[i : i + 1, :] for i in range(qh)], axis=0
    )


def joined(early, late, qh):
    return decay(early[0], late[1], qh) + late[0], early[1] + late[1]


def store(ref, item, qh):
    states, tail = pack(*item)
    ref[0 : qh * HD, :] = states
    ref[qh * HD : qh * HD + TAIL, :] = tail


def chip_kernel(pos, keep_ref, recv_ref, send_out, keep_out, *, qh):
    first = core_of(pos) == 0
    for out, part in ((send_out, 1 - x_of(pos)), (keep_out, x_of(pos))):
        own, other = keep_ref[part], recv_ref[part]
        early = spread(jnp.where(first, own, other), qh)
        late = spread(jnp.where(first, other, own), qh)
        store(out, joined(early, late, qh), qh)


def plane_kernel(pos, keep_ref, recv_ref, out, *, qh):
    first = x_of(pos) == 0
    own, other = keep_ref[...], recv_ref[...]
    early = spread(jnp.where(first, own, other), qh)
    late = spread(jnp.where(first, other, own), qh)
    store(out, joined(early, late, qh), qh)


def enter_kernel(pos, keep_ref, recv_ref, *refs, qh):
    planes, (send_out, keep_out) = refs[:-2], refs[-2:]
    total = None
    for ref in reversed(planes):
        item = spread(ref[...], qh)
        total = item if total is None else joined(total, item, qh)
    first = x_of(pos) == 0
    early = spread(jnp.where(first, keep_ref[...], recv_ref[...]), qh)
    if total is None:
        total = (jnp.zeros_like(early[0]), jnp.zeros_like(early[1]))
    later = joined(total, early, qh)
    zero, one = pack(*total), pack(*later)
    for out, take in ((send_out, first), (keep_out, jnp.logical_not(first))):
        out[0 : qh * HD, :] = jnp.where(take, one[0], zero[0])
        out[qh * HD : qh * HD + TAIL, :] = jnp.where(take, one[1], zero[1])


def core_kernel(pos, enter_keep, enter_recv, keep_ref, recv_ref, send_out, keep_out, *, qh):
    first = core_of(pos) == 0
    for part in range(2):
        entering = spread(jnp.where(x_of(pos) == part, enter_keep[...], enter_recv[...]), qh)
        own = spread(jnp.where(first, keep_ref[part], recv_ref[part]), qh)
        later = joined(entering, own, qh)[0].astype(BF16)
        now = entering[0].astype(BF16)
        send_out[part] = jnp.where(first, later, now)
        keep_out[part] = jnp.where(first, now, later)


def with_token(kernel, pos, token, *refs):
    refs[-1][0] = token[0]
    kernel(pos, *refs[:-1])


def small(kernel, pos, arrays, outs, qh, name, token):
    return pl.pallas_call(
        functools.partial(with_token, functools.partial(kernel, qh=qh)),
        in_specs=[SCALAR, SCALAR] + [pl.BlockSpec(memory_space=pltpu.VMEM)] * len(arrays),
        out_specs=[pl.BlockSpec(memory_space=pltpu.VMEM)] * len(outs) + [SCALAR],
        out_shape=[jax.ShapeDtypeStruct(s, BF16) for s in outs] + [NEXT],
        compiler_params=pltpu.CompilerParams(vmem_limit_bytes=24 * 2**20),
        cost_estimate=COST,
        name=name,
    )(pos, token, *arrays)


def light_kernel(pos, q_ref, k_ref, v_ref, cum_ref, cumt_ref, keep_ref, recv_ref, token, out_ref, ss_ref, after, *, qh):
    after[0] = token[0]
    rows = q_ref.shape[0]
    quarter = pl.program_id(0)
    part = quarter // 2
    mine = quarter % 2 == core_of(pos)
    causal = iota((rows, rows), 0) >= iota((rows, rows), 1)
    cum, cumt = cum_ref[0], cumt_ref[0]
    factor = jnp.exp(cum)
    state = jnp.where(mine, keep_ref[part], recv_ref[part])
    total = jnp.zeros((rows, HD), F32)
    for i in range(qh):
        cols = slice(i * HD, (i + 1) * HD)
        query = q_ref[:, cols]
        scores = mm_bt(query, k_ref[:, cols])
        gap = jnp.where(causal, cum[:, i : i + 1] - cumt[i : i + 1, :], LOW)
        weights = (scores * jnp.exp(gap)).astype(BF16)
        carried = mm(query, state[i * HD : (i + 1) * HD, :])
        raw = mm(weights, v_ref[:, cols]) + factor[:, i : i + 1] * carried
        out_ref[:, cols] = raw.astype(BF16)
        total = total + raw * raw

    @pl.when(quarter == 0)
    def _():
        ss_ref[...] = total

    @pl.when(quarter > 0)
    def _():
        ss_ref[...] += total


def light(pos, query, key, value, cum, cumt, keep, recv, token):
    rows, width = query.shape
    wide = width // 4
    block = pl.BlockSpec((rows, wide), lambda i: (0, i))
    whole = pl.BlockSpec(keep.shape, lambda i: (0, 0, 0))
    return pl.pallas_call(
        functools.partial(light_kernel, qh=wide // HD),
        grid=(4,),
        in_specs=[
            SCALAR,
            block,
            block,
            block,
            pl.BlockSpec((1, rows, HD), lambda i: (i, 0, 0)),
            pl.BlockSpec((1, 8, rows), lambda i: (i, 0, 0)),
            whole,
            whole,
            SCALAR,
        ],
        out_specs=[block, pl.BlockSpec((rows, HD), lambda i: (0, 0)), SCALAR],
        out_shape=[jax.ShapeDtypeStruct((rows, width), BF16), jax.ShapeDtypeStruct((rows, HD), F32), NEXT],
        compiler_params=params(),
        cost_estimate=COST,
        name="light",
    )(pos, query, key, value, cum, cumt, keep, recv, token)


def finish_kernel(raw_ref, ss_ref, gain_ref, gate_ref, token, out_ref, *, features):
    mean = jnp.sum(ss_ref[...], axis=1, keepdims=True) / features
    factor = lax.rsqrt(mean + EPS)
    gate = 0.5 * jnp.tanh(0.5 * gate_ref[...].astype(F32)) + 0.5
    out_ref[...] = (raw_ref[...].astype(F32) * factor * gain_ref[...] * gate).astype(BF16)


def finish(raw, square, gain, gate, features, token):
    rows, width = raw.shape
    wide = min(width, 512)
    block = pl.BlockSpec((rows, wide), lambda i: (0, i))
    return pl.pallas_call(
        functools.partial(finish_kernel, features=features),
        grid=(width // wide,),
        in_specs=[
            block,
            pl.BlockSpec((rows, HD), lambda i: (0, 0)),
            pl.BlockSpec((1, wide), lambda i: (0, i)),
            block,
            SCALAR,
        ],
        out_specs=block,
        out_shape=jax.ShapeDtypeStruct((rows, width), BF16),
        compiler_params=params(),
        cost_estimate=COST,
        name="finish",
    )(raw, square, gain.reshape(1, width), gate, token)


def soft_kernel(pos, q_ref, *refs, group, distances, last, passed):
    chunks = []
    for _ in distances:
        chunks.append((refs[:PLANE], refs[PLANE : 2 * PLANE]))
        refs = refs[2 * PLANE :]
    first = distances[0] == 0
    if not first:
        acc_in, stat_in, refs = refs[0], refs[1], refs[2:]
    token, refs = refs[0], refs[passed:]
    if last:
        out_ref, after, acc, stat = refs
    else:
        acc, stat, after = refs
        stat = stat.at[0]
    after[0] = token[0]
    rows = q_ref.shape[0]
    lane = iota((rows, HD), 1)
    pair = min(group, 2)

    if not first:
        acc[...] = acc_in[...]
        stat[...] = stat_in[0]

    def attend(keys, values, fresh):
        keyed = jnp.concatenate([k[...] for k in keys], axis=0)
        valued = jnp.concatenate([v[...] for v in values], axis=0)
        valued = jnp.concatenate([valued, jnp.ones_like(valued)], axis=1)
        if fresh:
            causal = iota((rows, rows), 0) >= iota((rows, rows), 1)
            part = iota((1, (PLANE - 1) * rows), 1) // rows
            shown = jnp.where(part == 1, core_of(pos), x_of(pos))
            bias = jnp.where(shown == 1, 0.0, LOW).astype(F32)

        def scored(i):
            query = jnp.concatenate([q_ref[:, g * HD : (g + 1) * HD] for g in range(i, i + pair)], axis=0)
            return mm_bt(query, keyed)

        def masked(s):
            return jnp.concatenate([jnp.where(causal, s[:, :rows], LOW), s[:, rows:] + bias], axis=1)

        scores = scored(0)
        for i in range(0, group, pair):
            ahead = scored(i + pair) if i + pair < group else None
            if fresh:
                scores = jnp.concatenate(
                    [masked(scores[n * rows : (n + 1) * rows]) for n in range(pair)], axis=0
                )
            top = jnp.max(scores, axis=1, keepdims=True)
            if not fresh:
                before = jnp.concatenate([stat[:, g : g + 1] for g in range(i, i + pair)], axis=0)
                top = jnp.maximum(top, before)
            shift = top * SCALE2
            probs = jnp.exp2(scores * SCALE2 - shift).astype(BF16)
            out = mm(probs, valued)
            for n in range(pair):
                g = i + n
                cols = slice(g * HD, (g + 1) * HD)
                band = slice(n * rows, (n + 1) * rows)
                summed, total = out[band, :HD], out[band, HD:]
                if not fresh:
                    keep = jnp.exp2(before[band] * SCALE2 - shift[band])
                    summed = summed + keep * acc[:, cols]
                    total = total + keep * stat[:, group + g : group + g + 1]
                acc[:, cols] = summed
                now = jnp.where(lane == g, top[band], stat[...])
                stat[...] = jnp.where(lane == group + g, total, now)
            scores = ahead

    for (keys, values), distance in zip(chunks, distances):
        if distance == 0:
            attend(keys, values, True)
        else:
            pl.when(z_of(pos) >= distance)(functools.partial(attend, keys, values, False))
    if last:
        for g in range(group):
            cols = slice(g * HD, (g + 1) * HD)
            out_ref[:, cols] = (acc[:, cols] / stat[:, group + g : group + g + 1]).astype(BF16)


def soft_step(pos, query, pieces, distances, state, into, span, kv_count, last, token):
    rows, width = query.shape
    group = width // HD // kv_count
    first = distances[0] == 0
    begin, count = span
    block = pl.BlockSpec((rows, group * HD), lambda k: (0, begin + k))
    stat = pl.BlockSpec((1, rows, HD), lambda k: (begin + k, 0, 0))
    keys = pl.BlockSpec((rows, HD), lambda k: (0, begin + k))
    values = pl.BlockSpec((rows, HD), lambda k: (0, kv_count + begin + k))
    in_specs = [SCALAR, block]
    operands = [pos, query]
    for d in distances:
        in_specs += [keys] * PLANE + [values] * PLANE
        operands += pieces[d] + pieces[d]
    aliases = {}
    if not first:
        if not last:
            aliases = {len(operands): 0, len(operands) + 1: 1}
        in_specs += [block, stat]
        operands += list(state)
    passed = 1
    in_specs.append(SCALAR)
    operands.append(token)
    if into is not None:
        passed += len(into)
        for i, a in enumerate(into):
            aliases[len(operands)] = i
            in_specs.append(ANY)
            operands.append(a)
    if last:
        out_specs = [block, SCALAR]
        out_shape = [jax.ShapeDtypeStruct((rows, width), BF16), NEXT]
        scratch = [pltpu.VMEM((rows, group * HD), F32), pltpu.VMEM((rows, HD), F32)]
    else:
        out_specs = [block, stat, SCALAR]
        out_shape = [
            jax.ShapeDtypeStruct((rows, width), F32),
            jax.ShapeDtypeStruct((kv_count, rows, HD), F32),
            NEXT,
        ]
        scratch = []
    return pl.pallas_call(
        functools.partial(soft_kernel, group=group, distances=distances, last=last, passed=passed),
        grid=(count,),
        in_specs=in_specs,
        out_specs=out_specs,
        out_shape=out_shape,
        scratch_shapes=scratch,
        input_output_aliases=aliases,
        compiler_params=params(),
        cost_estimate=COST,
        name="softmax",
    )(*operands)


def local(
    light_query,
    light_key,
    light_value,
    log_decay,
    out_gate,
    norm_gain,
    soft_query,
    soft_key,
    soft_value,
    *,
    ctx,
    tp,
):
    rows, heads = log_decay.shape
    qh = heads // 4
    length = qh * HD + TAIL
    planes = ctx // PLANE
    kv_count = soft_key.shape[1] // HD
    place = lax.axis_index("ctx")
    pos = place.astype(jnp.int32).reshape(1)

    def over_core(a):
        return lax.ppermute(a, "ctx", [(i, i ^ 1) for i in range(ctx)])

    def over_x(a):
        return lax.ppermute(a, "ctx", [(i, i ^ 2) for i in range(ctx)])

    def over_z(a, d):
        return lax.ppermute(a, "ctx", [(i, i + PLANE * d) for i in range(ctx - PLANE * d)])

    def after(a, token):
        return lax.optimization_barrier((a, token))[0]

    paired = jnp.concatenate([soft_key, soft_value], axis=1)
    crossed = over_x(paired)
    arrived = [paired]
    for _ in range(1, planes):
        arrived.append(over_z(arrived[-1], 1))
    pieces = [[paired, crossed, over_core(paired), over_core(crossed)]]

    half = max(kv_count // 2, 1)
    spans = [(0, half), (half, kv_count - half)] if kv_count > 1 else [(0, 1)]

    def soft(distances, state, last, token, span=None, into=None):
        *state, token = soft_step(
            pos, soft_query, pieces, distances, state, into, span or (0, kv_count), kv_count, last, token
        )
        return state, token

    send, keep, cum, cumt, token = local_state(
        pos, light_key, light_value, after(log_decay.T, pieces[0][2])
    )
    other = over_core(send)
    quarter = (length, HD)

    def cross(d, token):
        a = after(arrived[d], token)
        pieces.append([a, over_x(a)])

    def spread_core(d, token):
        pieces[d] += [over_core(after(a, token)) for a in pieces[d]]

    cross(1, token)
    state, token = soft((0,), None, False, token, spans[0])
    chip_send, chip_keep, token = small(chip_kernel, pos, [keep, other], [quarter, quarter], qh, "chip", token)
    chip_other = over_x(chip_send)
    cross(2, token)
    if len(spans) > 1:
        state, token = soft((0,), None, False, token, spans[1], state)
    plane, token = small(plane_kernel, pos, [chip_keep, chip_other], [quarter], qh, "plane", token)
    earlier = [over_z(plane, d) for d in range(1, planes)]
    spread_core(1, token)
    spread_core(2, token)
    for d in range(1, planes - 2):
        cross(d + 2, token)
        state, token = soft((d,), state, False, token)
        if d > 1:
            spread_core(d + 1, token)
    state, token = soft((planes - 2,), state, False, token, spans[0])
    enter_send, enter_keep, token = small(
        enter_kernel, pos, [chip_keep, chip_other] + earlier, [quarter, quarter], qh, "enter", token
    )
    enter_other = over_x(enter_send)
    if len(spans) > 1:
        state, token = soft((planes - 2,), state, False, token, spans[1])
    spread_core(planes - 1, token)
    both = (2, qh * HD, HD)
    state_send, state_keep, token = small(
        core_kernel, pos, [enter_keep, enter_other, keep, other], [both, both], qh, "core", token
    )
    state_other = over_core(state_send)
    soft_out, token = soft((planes - 1,), state, True, token, spans[0])
    raw, square, token = light(
        pos, light_query, light_key, light_value, cum, cumt, state_keep, state_other, token
    )
    step = 1
    while step < tp:
        square = square + lax.ppermute(square, "tp", [(i, i ^ step) for i in range(tp)])
        step *= 2
    if len(spans) > 1:
        soft_out, token = soft((planes - 1,), state, True, token, spans[1], soft_out)
    light_out = finish(raw, square, norm_gain, out_gate, heads * HD * tp, token)
    return (light_out, soft_out[0])


def solution(mesh):
    both = P("ctx", "tp")
    return jax.shard_map(
        functools.partial(local, ctx=mesh.shape["ctx"], tp=mesh.shape["tp"]),
        mesh=mesh,
        in_specs=(both, both, both, both, both, P("tp"), both, both, both),
        out_specs=(both, both),
        check_vma=False,
    )
```

time: 203 us -> 156 us (0.77)
  waiting for transfers between devices: 59.6 us -> 7.03 us
  Pallas kernels: 112 us -> 117 us
  local copies, waits for them, and re-layouts: 4.7 us -> 7.08 us
    ppermute x6, waiting for transfers between devices: 38.1 us -> 1.2 us  [over_z(): lax.ppermute(a, 'ctx', [(i, i + PLANE * d) for i in range(ctx - PLANE * d)])]
    ppermute x6, waiting for transfers between devices: 19.8 us -> 5.8 us  [over_x(): return lax.ppermute(a, 'ctx', [(i, i ^ 2) for i in range(ctx)])]
    pallas_call x10 -> x12, Pallas kernels: 98.4 us -> 103 us  [the longest x7 88.9 us: soft_step(): pl.pallas_call(functools.partial(soft_kernel, group=group, distances=dist...]
    pallas_call x1, Pallas kernels: 5.17 us -> 7.55 us  [finish(): pl.pallas_call(functools.partial(finish_kernel, features=features), grid=...]
    unnamed x40 -> x37, local copies, waits for them, and re-layouts: 4.68 us -> 6.1 us
  transfers between devices with their start and end apart: 23 -> 23, of which waited for: 6 -> 4; matrix products, arithmetic and copies ran while one was open for 0% -> 0% of each run, Pallas kernels for 48% -> 65%
where the time goes in v2:
time: 156 us; the launch traced here: 155 us
  Pallas kernels  117 us (75%)
  starting transfers between devices  22.3 us (14%)
  local copies, waits for them, and re-layouts  7.08 us (5%)
  waiting for transfers between devices  7.03 us (5%)
    pallas_call x7, Pallas kernels, soft_step(): pl.pallas_call(functools.partial(soft_kernel, group=group, distances=dist...  88.9 us
    pallas_call x1, Pallas kernels, light(): pl.pallas_call(functools.partial(light_kernel, qh=wide // HD), grid=(4,),...  8.81 us
    ppermute x10, starting transfers between devices, over_core(): return lax.ppermute(a, 'ctx', [(i, i ^ 1) for i in range(ctx)])  8.41 us
    ppermute x6, starting transfers between devices, over_z(): lax.ppermute(a, 'ctx', [(i, i + PLANE * d) for i in range(ctx - PLANE * d)])  7.89 us
    pallas_call x1, Pallas kernels, finish(): pl.pallas_call(functools.partial(finish_kernel, features=features), grid=...  7.55 us
    pallas_call x1, Pallas kernels, local_state(): pl.pallas_call(functools.partial(state_kernel, qh=qh, heads=heads), grid_...  7.15 us
    unnamed x37, local copies, waits for them, and re-layouts  6.1 us
    ppermute x6, waiting for transfers between devices, over_x(): return lax.ppermute(a, 'ctx', [(i, i ^ 2) for i in range(ctx)])  5.8 us
  transfers between devices with their start and end apart: 23, of which 4 were waited for; matrix products, arithmetic and copies ran while one was open for 0% of the time, Pallas kernels for 65%

profile of v2, /device:TPU:27, one launch (start us, length us, event | category | flops | bytes accessed | tf_op | source)
XLA Modules:
  0.0 155.4 jit_solution(11161336739568352256)
XLA Ops:
  3.6 1.3 collective-permute-start.1
  4.9 7.2 %local_state.1 = (bf16[2,1040,128]{2,1,0:T(8,128)(2,1)}, bf16[2,1040,128]{2,1,0:T(8,128)(2,1)}, f32[4,256,128]{2,1,0:T(8,128)}, f32[4,8,256]{2,1,0:T(8,128)}, s32[1]{0:T(128)}) custom-call(s32[1]{0:T(128)} %bitcast.pos, bf16[256,4096]{1,0:T(8,128)(2,1)} %k_ref.3, bf16[256,4096]{1,0:T(8,128)(2,1)} %v_ref.3, f32[32,256]{1,0:T(8,128)} %bitcast.3), custom_call_target="tpu_custom_call" | custom-call | flops 1000 | bytes 1048576 | tf_op jit(solution)/shard_map/local_state/pallas_call | solution.py:123
  12.5 4.3 %collective-permute-done.3.refs_1_.refs_5_ = bf16[256,1024]{1,0:T(8,128)(2,1)S(1)} collective-permute-done((bf16[256,1024]{1,0:T(8,128)(2,1)S(1)}, bf16[256,1024]{1,0:T(8,128)(2,1)S(1)}, u32[]{:S(2)}, u32[]{:S(2)}) %collective-permute-start.3) | collective-permute-done | bytes 524320 | tf_op jit(solution)/shard_map/ppermute | solution.py:491
  18.7 1.3 collective-permute-start.2
  20.0 1.3 collective-permute-start.10
  22.1 8.9 %softmax.7 = (f32[256,4096]{1,0:T(8,128)}, f32[4,256,128]{2,1,0:T(8,128)}, s32[1]{0:T(128)}) custom-call(s32[1]{0:T(128)} %bitcast.pos, bf16[256,4096]{1,0:T(8,128)(2,1)} %q_ref.15, bf16[256,1024]{1,0:T(8,128)(2,1)} %copy-done.2, bf16[256,1024]{1,0:T(8,128)(2,1)} %copy-done.7, bf16[256,1024]{1,0:T(8,128)(2,1)} %copy-done.6, bf16[256,1024]{1,0:T(8,128)(2,1)} %copy-done.8, ...), custom_call_target="tpu_custom_call" | custom-call | flops 1000 | bytes 1048576 | tf_op jit(solution)/shard_map/softmax/pallas_call | solution.py:451
  31.0 1.3 chip.1
  34.1 1.3 collective-permute-start.18
  35.4 9.1 %softmax.8 = (f32[256,4096]{1,0:T(8,128)}, f32[4,256,128]{2,1,0:T(8,128)}, s32[1]{0:T(128)}) custom-call(s32[1]{0:T(128)} %bitcast.pos, bf16[256,4096]{1,0:T(8,128)(2,1)} %q_ref.15, bf16[256,1024]{1,0:T(8,128)(2,1)} %copy-done.2, bf16[256,1024]{1,0:T(8,128)(2,1)} %copy-done.7, ...), custom_call_target="tpu_custom_call", output_to_operand_aliasing={{0}: (11, {}), {1}: (12, {})} | custom-call | flops 1000 | bytes 1048576 | tf_op jit(solution)/shard_map/softmax/pallas_call | solution.py:451
  45.7 2.3 %collective-permute-start.12 = (bf16[256,1024]{1,0:T(8,128)(2,1)}, bf16[256,1024]{1,0:T(8,128)(2,1)S(1)}, u32[]{:S(2)}, u32[]{:S(2)}) collective-permute-start(bf16[256,1024]{1,0:T(8,128)(2,1)} %collective-permute-done.10.refs_1_.refs_5_), channel_id=1, source_target_pairs={{0,2},{2,0},{4,6},{6,4},{8,10},{10,8},{12,14},{14,12},{16,18},{18,... | collective-permute-start | bytes 1572872 | tf_op jit(solution)/shard_map/ppermute | solution.py:488
  48.6 1.5 collective-permute-done.6.refs_1_.refs_5_
  50.1 2.4 %collective-permute-start.9 = (bf16[256,1024]{1,0:T(8,128)(2,1)S(1)}, bf16[256,1024]{1,0:T(8,128)(2,1)}, u32[]{:S(2)}, u32[]{:S(2)}) collective-permute-start(bf16[256,1024]{1,0:T(8,128)(2,1)S(1)} %collective-permute-done.6.refs_1_.refs_5_), channel_id=1, source_target_pairs={{0,2},{2,0},{4,6},{6,4},{8,10},{10,8},{12,14},{14,12},{16,18},{18,... | collective-permute-start | bytes 1572872 | tf_op jit(solution)/shard_map/ppermute | solution.py:488
  53.2 1.3 collective-permute-start.13
  54.6 1.3 collective-permute-start.14
  55.9 1.5 collective-permute-start.15
  58.4 21.0 %softmax.9 = (f32[256,4096]{1,0:T(8,128)}, f32[4,256,128]{2,1,0:T(8,128)}, s32[1]{0:T(128)}) custom-call(s32[1]{0:T(128)} %bitcast.pos, bf16[256,4096]{1,0:T(8,128)(2,1)} %q_ref.15, bf16[256,1024]{1,0:T(8,128)(2,1)} %copy-done.13, bf16[256,1024]{1,0:T(8,128)(2,1)} %collective-permute-done.10.refs_1_.refs_5_, ...), custom_call_target="tpu_custom_call", output_to_operand_aliasing={{0}: (10, {}), {1}: (11, {})} | custom-call | flops 1000 | bytes 1048576 | tf_op jit(solution)/shard_map/softmax/pallas_call | solution.py:451
  79.4 12.1 %softmax.10 = (f32[256,4096]{1,0:T(8,128)}, f32[4,256,128]{2,1,0:T(8,128)}, s32[1]{0:T(128)}) custom-call(s32[1]{0:T(128)} %bitcast.pos, bf16[256,4096]{1,0:T(8,128)(2,1)} %q_ref.15, bf16[256,1024]{1,0:T(8,128)(2,1)} %copy-done.3, bf16[256,1024]{1,0:T(8,128)(2,1)} %copy-done.4, ...), custom_call_target="tpu_custom_call", output_to_operand_aliasing={{0}: (10, {}), {1}: (11, {})} | custom-call | flops 1000 | bytes 1048576 | tf_op jit(solution)/shard_map/softmax/pallas_call | solution.py:451
  92.8 1.3 collective-permute-start.16
  94.1 12.4 %softmax.11 = (f32[256,4096]{1,0:T(8,128)}, f32[4,256,128]{2,1,0:T(8,128)}, s32[1]{0:T(128)}) custom-call(s32[1]{0:T(128)} %bitcast.pos, bf16[256,4096]{1,0:T(8,128)(2,1)} %q_ref.15, bf16[256,1024]{1,0:T(8,128)(2,1)} %copy-done.3, bf16[256,1024]{1,0:T(8,128)(2,1)} %copy-done.4, ...), custom_call_target="tpu_custom_call", output_to_operand_aliasing={{0}: (10, {}), {1}: (11, {})} | custom-call | flops 1000 | bytes 1048576 | tf_op jit(solution)/shard_map/softmax/pallas_call | solution.py:451
  110.8 12.5 %softmax.12 = (bf16[256,4096]{1,0:T(8,128)(2,1)}, s32[1]{0:T(128)}) custom-call(s32[1]{0:T(128)} %bitcast.pos, bf16[256,4096]{1,0:T(8,128)(2,1)} %q_ref.15, bf16[256,1024]{1,0:T(8,128)(2,1)} %copy-done.9, bf16[256,1024]{1,0:T(8,128)(2,1)} %collective-permute-done.19.refs_1_.refs_5_, bf16[256,1024]{1,0:T(8,128)(2,1)} %copy-done.12, ...), custom_call_target="tpu_custom_call" | custom-call | flops 1000 | bytes 1048576 | tf_op jit(solution)/shard_map/softmax/pallas_call | solution.py:451
  124.1 8.8 %light.1 = (bf16[256,4096]{1,0:T(8,128)(2,1)}, f32[256,128]{1,0:T(8,128)}, s32[1]{0:T(128)}) custom-call(s32[1]{0:T(128)} %bitcast.pos, bf16[256,4096]{1,0:T(8,128)(2,1)} %q_ref.14, bf16[256,4096]{1,0:T(8,128)(2,1)} %k_ref.3, bf16[256,4096]{1,0:T(8,128)(2,1)} %v_ref.3, f32[4,256,128]{2,1,0:T(8,128)} %get-tuple-element.51.cum_ref, ...), custom_call_target="tpu_custom_call" | custom-call | flops 1000 | bytes 1048576 | tf_op jit(solution)/shard_map/light/pallas_call | solution.py:280
  132.9 1.4 collective-permute-start.22
  134.3 12.9 %softmax.13 = (bf16[256,4096]{1,0:T(8,128)(2,1)}, s32[1]{0:T(128)}) custom-call(s32[1]{0:T(128)} %bitcast.pos, bf16[256,4096]{1,0:T(8,128)(2,1)} %q_ref.15, bf16[256,1024]{1,0:T(8,128)(2,1)} %copy-done.9, bf16[256,1024]{1,0:T(8,128)(2,1)} %collective-permute-done.19.refs_1_.refs_5_, bf16[256,1024]{1,0:T(8,128)(2,1)} %copy-done.12, ...), custom_call_target="tpu_custom_call", output_to_operand_aliasing={{0}: (13, {})} | custom-call | flops 1000 | bytes 1048576 | tf_op jit(solution)/shard_map/softmax/pallas_call | solution.py:451
  147.8 7.5 %finish.1 = bf16[256,4096]{1,0:T(8,128)(2,1)} custom-call(bf16[256,4096]{1,0:T(8,128)(2,1)} %get-tuple-element.92.raw_ref, f32[256,128]{1,0:T(8,128)} %add.3.ss_ref, f32[1,4096]{1,0:T(1,128)} %bitcast.4, bf16[256,4096]{1,0:T(8,128)(2,1)} %gate_ref.1, s32[1]{0:T(128)} %get-tuple-element.96.token), custom_call_target="tpu_custom_call" | custom-call | flops 1000 | bytes 1048576 | tf_op jit(solution)/shard_map/finish/pallas_call | solution.py:313
  (75 shorter events, 18.5 us)
Async XLA Ops:
  2.6 2.3 %collective-permute-start = (bf16[256,1024]{1,0:T(8,128)(2,1)S(1)}, bf16[256,1024]{1,0:T(8,128)(2,1)S(1)}, u32[]{:S(2)}, u32[]{:S(2)}) collective-permute-start(bf16[256,1024]{1,0:T(8,128)(2,1)S(1)} %constant_dynamic-update-slice_fusion.refs_0_.refs_4_), channel_id=1, source_target_pairs={{0,2},{2,0},{4,6},{6,4},{8,10},{10,8},{12,14},{14,12},{16,18},{18,... | collective-permute-start | bytes 1572872 | tf_op jit(solution)/shard_map/ppermute | solution.py:488
  3.3 13.5 %collective-permute-start.3 = (bf16[256,1024]{1,0:T(8,128)(2,1)S(1)}, bf16[256,1024]{1,0:T(8,128)(2,1)S(1)}, u32[]{:S(2)}, u32[]{:S(2)}) collective-permute-start(bf16[256,1024]{1,0:T(8,128)(2,1)S(1)} %constant_dynamic-update-slice_fusion.refs_0_.refs_4_), channel_id=1, source_target_pairs={{0,4},{2,6},{4,0},{6,2},{8,12},{10,14},{12,8},{14,10},{16,20},{18,... | collective-permute-start | bytes 1572872 | tf_op jit(solution)/shard_map/ppermute | solution.py:491
  3.6 15.0 %collective-permute-start.1 = (bf16[256,1024]{1,0:T(8,128)(2,1)S(1)}, bf16[256,1024]{1,0:T(8,128)(2,1)S(1)}, u32[]{:S(2)}, u32[]{:S(2)}) collective-permute-start(bf16[256,1024]{1,0:T(8,128)(2,1)S(1)} %constant_dynamic-update-slice_fusion.refs_0_.refs_4_), channel_id=1, source_target_pairs={{0,8},{2,10},{4,12},{6,14},{8,16},{10,18},{12,20},{14,22},{16,24},... | collective-permute-start | bytes 1572872 | tf_op jit(solution)/shard_map/ppermute | solution.py:494
  12.1 18.9 %collective-permute-start.5 = (bf16[2,1040,128]{2,1,0:T(8,128)(2,1)}, bf16[2,1040,128]{2,1,0:T(8,128)(2,1)S(1)}, u32[]{:S(2)}, u32[]{:S(2)}) collective-permute-start(bf16[2,1040,128]{2,1,0:T(8,128)(2,1)} %get-tuple-element.56), channel_id=1, source_target_pairs={{0,2},{2,0},{4,6},{6,4},{8,10},{10,8},{12,14},{14,12},{16,18},{18,... | collective-permute-start | bytes 1597448 | tf_op jit(solution)/shard_map/ppermute | solution.py:488
  16.9 4.4 %collective-permute-start.4 = (bf16[256,1024]{1,0:T(8,128)(2,1)S(1)}, bf16[256,1024]{1,0:T(8,128)(2,1)S(1)}, u32[]{:S(2)}, u32[]{:S(2)}) collective-permute-start(bf16[256,1024]{1,0:T(8,128)(2,1)S(1)} %collective-permute-done.3.refs_1_.refs_5_), channel_id=1, source_target_pairs={{0,2},{2,0},{4,6},{6,4},{8,10},{10,8},{12,14},{14,12},{16,18},{18,... | collective-permute-start | bytes 1572872 | tf_op jit(solution)/shard_map/ppermute | solution.py:488
  18.7 29.4 %copy-start.13 = (bf16[256,1024]{1,0:T(8,128)(2,1)}, bf16[256,1024]{1,0:T(8,128)(2,1)S(1)}, u32[]{:S(2)}) copy-start(bf16[256,1024]{1,0:T(8,128)(2,1)S(1)} %collective-permute-done.1.refs_0_.refs_4_) | copy-start | bytes 1572868
  18.7 14.2 %collective-permute-start.2 = (bf16[256,1024]{1,0:T(8,128)(2,1)S(1)}, bf16[256,1024]{1,0:T(8,128)(2,1)S(1)}, u32[]{:S(2)}, u32[]{:S(2)}) collective-permute-start(bf16[256,1024]{1,0:T(8,128)(2,1)S(1)} %collective-permute-done.1.refs_0_.refs_4_), channel_id=1, source_target_pairs={{0,8},{2,10},{4,12},{6,14},{8,16},{10,18},{12,20},{14,22},{16,24},... | collective-permute-start | bytes 1572872 | tf_op jit(solution)/shard_map/ppermute | solution.py:494
  20.0 25.8 %collective-permute-start.10 = (bf16[256,1024]{1,0:T(8,128)(2,1)S(1)}, bf16[256,1024]{1,0:T(8,128)(2,1)}, u32[]{:S(2)}, u32[]{:S(2)}) collective-permute-start(bf16[256,1024]{1,0:T(8,128)(2,1)S(1)} %collective-permute-done.1.refs_0_.refs_4_), channel_id=1, source_target_pairs={{0,4},{2,6},{4,0},{6,2},{8,12},{10,14},{12,8},{14,10},{16,20},{18,... | collective-permute-start | bytes 1572872 | tf_op jit(solution)/shard_map/ppermute | solution.py:491
  32.3 12.2 %collective-permute-start.7 = (bf16[1040,128]{1,0:T(8,128)(2,1)S(1)}, bf16[1040,128]{1,0:T(8,128)(2,1)S(1)}, u32[]{:S(2)}, u32[]{:S(2)}) collective-permute-start(bf16[1040,128]{1,0:T(8,128)(2,1)S(1)} %get-tuple-element.63), channel_id=1, source_target_pairs={{0,4},{2,6},{4,0},{6,2},{8,12},{10,14},{12,8},{14,10},{16,20},{18,... | collective-permute-start | bytes 798728 | tf_op jit(solution)/shard_map/ppermute | solution.py:491
  32.9 17.2 %collective-permute-start.6 = (bf16[256,1024]{1,0:T(8,128)(2,1)S(1)}, bf16[256,1024]{1,0:T(8,128)(2,1)S(1)}, u32[]{:S(2)}, u32[]{:S(2)}) collective-permute-start(bf16[256,1024]{1,0:T(8,128)(2,1)S(1)} %collective-permute-done.2.refs_0_.refs_4_), channel_id=1, source_target_pairs={{0,4},{2,6},{4,0},{6,2},{8,12},{10,14},{12,8},{14,10},{16,20},{18,... | collective-permute-start | bytes 1572872 | tf_op jit(solution)/shard_map/ppermute | solution.py:491
  34.1 18.3 %collective-permute-start.18 = (bf16[256,1024]{1,0:T(8,128)(2,1)S(1)}, bf16[256,1024]{1,0:T(8,128)(2,1)S(1)}, u32[]{:S(2)}, u32[]{:S(2)}) collective-permute-start(bf16[256,1024]{1,0:T(8,128)(2,1)S(1)} %collective-permute-done.2.refs_0_.refs_4_), channel_id=1, source_target_pairs={{0,8},{2,10},{4,12},{6,14},{8,16},{10,18},{12,20},{14,22},{16,24},... | collective-permute-start | bytes 1572872 | tf_op jit(solution)/shard_map/ppermute | solution.py:494
  45.7 8.8 %collective-permute-start.12 = (bf16[256,1024]{1,0:T(8,128)(2,1)}, bf16[256,1024]{1,0:T(8,128)(2,1)S(1)}, u32[]{:S(2)}, u32[]{:S(2)}) collective-permute-start(bf16[256,1024]{1,0:T(8,128)(2,1)} %collective-permute-done.10.refs_1_.refs_5_), channel_id=1, source_target_pairs={{0,2},{2,0},{4,6},{6,4},{8,10},{10,8},{12,14},{14,12},{16,18},{18,... | collective-permute-start | bytes 1572872 | tf_op jit(solution)/shard_map/ppermute | solution.py:488
  48.1 7.8 %collective-permute-start.11 = (bf16[256,1024]{1,0:T(8,128)(2,1)S(1)}, bf16[256,1024]{1,0:T(8,128)(2,1)S(1)}, u32[]{:S(2)}, u32[]{:S(2)}) collective-permute-start(bf16[256,1024]{1,0:T(8,128)(2,1)S(1)} %collective-permute-done.1.refs_0_.refs_4_), channel_id=1, source_target_pairs={{0,2},{2,0},{4,6},{6,4},{8,10},{10,8},{12,14},{14,12},{16,18},{18,... | collective-permute-start | bytes 1572872 | tf_op jit(solution)/shard_map/ppermute | solution.py:488
  48.2 9.2 %collective-permute-start.8 = (bf16[256,1024]{1,0:T(8,128)(2,1)S(1)}, bf16[256,1024]{1,0:T(8,128)(2,1)S(1)}, u32[]{:S(2)}, u32[]{:S(2)}) collective-permute-start(bf16[256,1024]{1,0:T(8,128)(2,1)S(1)} %collective-permute-done.2.refs_0_.refs_4_), channel_id=1, source_target_pairs={{0,2},{2,0},{4,6},{6,4},{8,10},{10,8},{12,14},{14,12},{16,18},{18,... | collective-permute-start | bytes 1572872 | tf_op jit(solution)/shard_map/ppermute | solution.py:488
  50.1 29.4 %collective-permute-start.9 = (bf16[256,1024]{1,0:T(8,128)(2,1)S(1)}, bf16[256,1024]{1,0:T(8,128)(2,1)}, u32[]{:S(2)}, u32[]{:S(2)}) collective-permute-start(bf16[256,1024]{1,0:T(8,128)(2,1)S(1)} %collective-permute-done.6.refs_1_.refs_5_), channel_id=1, source_target_pairs={{0,2},{2,0},{4,6},{6,4},{8,10},{10,8},{12,14},{14,12},{16,18},{18,... | collective-permute-start | bytes 1572872 | tf_op jit(solution)/shard_map/ppermute | solution.py:488
  53.2 38.3 %collective-permute-start.13 = (bf16[1040,128]{1,0:T(8,128)(2,1)S(1)}, bf16[1040,128]{1,0:T(8,128)(2,1)S(1)}, u32[]{:S(2)}, u32[]{:S(2)}) collective-permute-start(bf16[1040,128]{1,0:T(8,128)(2,1)S(1)} %get-tuple-element.78), channel_id=1, source_target_pairs={{0,8},{2,10},{4,12},{6,14},{8,16},{10,18},{12,20},{14,22},{16,24},... | collective-permute-start | bytes 798728 | tf_op jit(solution)/shard_map/ppermute | solution.py:494
  54.6 37.0 %collective-permute-start.14 = (bf16[1040,128]{1,0:T(8,128)(2,1)S(1)}, bf16[1040,128]{1,0:T(8,128)(2,1)S(1)}, u32[]{:S(2)}, u32[]{:S(2)}) collective-permute-start(bf16[1040,128]{1,0:T(8,128)(2,1)S(1)} %get-tuple-element.78), channel_id=1, source_target_pairs={{0,16},{2,18},{4,20},{6,22},{8,24},{10,26},{12,28},{14,30},{1,17},... | collective-permute-start | bytes 798728 | tf_op jit(solution)/shard_map/ppermute | solution.py:494
  55.9 35.7 %collective-permute-start.15 = (bf16[1040,128]{1,0:T(8,128)(2,1)S(1)}, bf16[1040,128]{1,0:T(8,128)(2,1)S(1)}, u32[]{:S(2)}, u32[]{:S(2)}) collective-permute-start(bf16[1040,128]{1,0:T(8,128)(2,1)S(1)} %get-tuple-element.78), channel_id=1, source_target_pairs={{0,24},{2,26},{4,28},{6,30},{1,25},{3,27},{5,29},{7,31}} | collective-permute-start | bytes 798728 | tf_op jit(solution)/shard_map/ppermute | solution.py:494
  58.2 48.3 %collective-permute-start.19 = (bf16[256,1024]{1,0:T(8,128)(2,1)}, bf16[256,1024]{1,0:T(8,128)(2,1)}, u32[]{:S(2)}, u32[]{:S(2)}) collective-permute-start(bf16[256,1024]{1,0:T(8,128)(2,1)} %copy-done.9), channel_id=1, source_target_pairs={{0,4},{2,6},{4,0},{6,2},{8,12},{10,14},{12,8},{14,10},{16,20},{18,... | collective-permute-start | bytes 1572872 | tf_op jit(solution)/shard_map/ppermute | solution.py:491
  92.8 14.4 %collective-permute-start.16 = (bf16[1040,128]{1,0:T(8,128)(2,1)S(1)}, bf16[1040,128]{1,0:T(8,128)(2,1)S(1)}, u32[]{:S(2)}, u32[]{:S(2)}) collective-permute-start(bf16[1040,128]{1,0:T(8,128)(2,1)S(1)} %get-tuple-element.82), channel_id=1, source_target_pairs={{0,4},{2,6},{4,0},{6,2},{8,12},{10,14},{12,8},{14,10},{16,20},{18,... | collective-permute-start | bytes 798728 | tf_op jit(solution)/shard_map/ppermute | solution.py:491
  106.5 3.2 %collective-permute-start.21 = (bf16[256,1024]{1,0:T(8,128)(2,1)}, bf16[256,1024]{1,0:T(8,128)(2,1)S(1)}, u32[]{:S(2)}, u32[]{:S(2)}) collective-permute-start(bf16[256,1024]{1,0:T(8,128)(2,1)} %collective-permute-done.19.refs_1_.refs_5_), channel_id=1, source_target_pairs={{0,2},{2,0},{4,6},{6,4},{8,10},{10,8},{12,14},{14,12},{16,18},{18,... | collective-permute-start | bytes 1572872 | tf_op jit(solution)/shard_map/ppermute | solution.py:488
  107.2 2.6 %collective-permute-start.20 = (bf16[256,1024]{1,0:T(8,128)(2,1)S(1)}, bf16[256,1024]{1,0:T(8,128)(2,1)S(1)}, u32[]{:S(2)}, u32[]{:S(2)}) collective-permute-start(bf16[256,1024]{1,0:T(8,128)(2,1)S(1)} %copy-done.10), channel_id=1, source_target_pairs={{0,2},{2,0},{4,6},{6,4},{8,10},{10,8},{12,14},{14,12},{16,18},{18,... | collective-permute-start | bytes 1572872 | tf_op jit(solution)/shard_map/ppermute | solution.py:488
  109.3 14.0 %collective-permute-start.17 = (bf16[2,1024,128]{2,1,0:T(8,128)(2,1)S(1)}, bf16[2,1024,128]{2,1,0:T(8,128)(2,1)S(1)}, u32[]{:S(2)}, u32[]{:S(2)}) collective-permute-start(bf16[2,1024,128]{2,1,0:T(8,128)(2,1)S(1)} %get-tuple-element.84), channel_id=1, source_target_pairs={{0,2},{2,0},{4,6},{6,4},{8,10},{10,8},{12,14},{14,12},{16,18},{18,... | collective-permute-start | bytes 1572872 | tf_op jit(solution)/shard_map/ppermute | solution.py:488
  132.9 14.2 %collective-permute-start.22 = (f32[256,128]{1,0:T(8,128)}, f32[256,128]{1,0:T(8,128)S(1)}, u32[]{:S(2)}, u32[]{:S(2)}) collective-permute-start(f32[256,128]{1,0:T(8,128)} %get-tuple-element.93), channel_id=1, source_target_pairs={{0,1},{1,0},{2,3},{3,2},{4,5},{5,4},{6,7},{7,6},{8,9},{9,8},{10,11... | collective-permute-start | bytes 393224 | tf_op jit(solution)/shard_map/ppermute | solution.py:563
  (17 other events, 115.1 us)

commit v3 on v2

--- a/solution.py
+++ b/solution.py
@@ -11,9 +11,10 @@
 HD = 128
 EPS = 1e-06
 LOW = -1e30
+LIMIT = 2.0**100
 PLANE = 4
 TAIL = 16
-VMEM = 60 * 2**20
+VMEM = 32 * 2**20
 F32 = jnp.float32
 BF16 = jnp.bfloat16
 HIGH = lax.Precision.HIGHEST
@@ -299,40 +300,46 @@
     )(pos, query, key, value, cum, cumt, keep, recv, token)
 
 
-def finish_kernel(raw_ref, ss_ref, gain_ref, gate_ref, token, out_ref, *, features):
-    mean = jnp.sum(ss_ref[...], axis=1, keepdims=True) / features
-    factor = lax.rsqrt(mean + EPS)
-    gate = 0.5 * jnp.tanh(0.5 * gate_ref[...].astype(F32)) + 0.5
-    out_ref[...] = (raw_ref[...].astype(F32) * factor * gain_ref[...] * gate).astype(BF16)
-
-
-def finish(raw, square, gain, gate, features, token):
+def finish_kernel(raw_ref, *refs, features):
+    squares, (gain_ref, gate_ref, token, out_ref, factor) = refs[:-5], refs[-5:]
+
+    @pl.when(pl.program_id(0) == 0)
+    def _():
+        square = squares[0][...]
+        for more in squares[1:]:
+            square = square + more[...]
+        mean = jnp.sum(square, axis=1, keepdims=True) / features
+        factor[...] = jnp.broadcast_to(lax.rsqrt(mean + EPS), factor.shape)
+
+    for i in range(out_ref.shape[1] // HD):
+        cols = slice(i * HD, (i + 1) * HD)
+        gate = 0.5 * jnp.tanh(0.5 * gate_ref[:, cols].astype(F32)) + 0.5
+        raw = raw_ref[:, cols].astype(F32)
+        out_ref[:, cols] = (raw * factor[...] * gain_ref[:, cols] * gate).astype(BF16)
+
+
+def finish(raw, squares, gain, gate, features, token):
     rows, width = raw.shape
-    wide = min(width, 512)
+    wide = width // 4
     block = pl.BlockSpec((rows, wide), lambda i: (0, i))
     return pl.pallas_call(
         functools.partial(finish_kernel, features=features),
-        grid=(width // wide,),
-        in_specs=[
-            block,
-            pl.BlockSpec((rows, HD), lambda i: (0, 0)),
-            pl.BlockSpec((1, wide), lambda i: (0, i)),
-            block,
-            SCALAR,
-        ],
+        grid=(4,),
+        in_specs=[block]
+        + [pl.BlockSpec((rows, HD), lambda i: (0, 0))] * len(squares)
+        + [pl.BlockSpec((1, wide), lambda i: (0, i)), block, SCALAR],
         out_specs=block,
         out_shape=jax.ShapeDtypeStruct((rows, width), BF16),
+        scratch_shapes=[pltpu.VMEM((rows, HD), F32)],
         compiler_params=params(),
         cost_estimate=COST,
         name="finish",
-    )(raw, square, gain.reshape(1, width), gate, token)
-
-
-def soft_kernel(pos, q_ref, *refs, group, distances, last, passed):
-    chunks = []
-    for _ in distances:
-        chunks.append((refs[:PLANE], refs[PLANE : 2 * PLANE]))
-        refs = refs[2 * PLANE :]
+    )(raw, *squares, gain.reshape(1, width), gate, token)
+
+
+def soft_kernel(pos, q_ref, *refs, group, distances, planes, last, passed):
+    count = planes * PLANE if last else len(distances) * PLANE
+    keys, values, refs = refs[:count], refs[count : 2 * count], refs[2 * count :]
     first = distances[0] == 0
     if not first:
         acc_in, stat_in, refs = refs[0], refs[1], refs[2:]
@@ -345,69 +352,106 @@
     after[0] = token[0]
     rows = q_ref.shape[0]
     lane = iota((rows, HD), 1)
+    causal = iota((rows, rows), 0) >= iota((rows, rows), 1)
     pair = min(group, 2)
+    flags = [None, x_of(pos) == 1, core_of(pos) == 1, x_of(pos) == 1]
 
     if not first:
         acc[...] = acc_in[...]
         stat[...] = stat_in[0]
 
-    def attend(keys, values, fresh):
-        keyed = jnp.concatenate([k[...] for k in keys], axis=0)
-        valued = jnp.concatenate([v[...] for v in values], axis=0)
-        valued = jnp.concatenate([valued, jnp.ones_like(valued)], axis=1)
+    def attend(keyed, valued, fresh):
+        wide = jnp.concatenate([v[...] for v in valued], axis=0)
+        wide = jnp.concatenate([wide, jnp.ones_like(wide)], axis=1)
         if fresh:
-            causal = iota((rows, rows), 0) >= iota((rows, rows), 1)
-            part = iota((1, (PLANE - 1) * rows), 1) // rows
-            shown = jnp.where(part == 1, core_of(pos), x_of(pos))
-            bias = jnp.where(shown == 1, 0.0, LOW).astype(F32)
+            own = keyed[0][...].astype(F32)
+            shifts = [
+                jnp.sum(q_ref[:, g * HD : (g + 1) * HD].astype(F32) * own, axis=1, keepdims=True) * SCALE2
+                for g in range(group)
+            ]
+        else:
+            shifts = [stat[:, g : g + 1] for g in range(group)]
 
         def scored(i):
             query = jnp.concatenate([q_ref[:, g * HD : (g + 1) * HD] for g in range(i, i + pair)], axis=0)
-            return mm_bt(query, keyed)
-
-        def masked(s):
-            return jnp.concatenate([jnp.where(causal, s[:, :rows], LOW), s[:, rows:] + bias], axis=1)
+            return [mm_bt(query, k[...]) for k in keyed]
 
         scores = scored(0)
         for i in range(0, group, pair):
             ahead = scored(i + pair) if i + pair < group else None
-            if fresh:
-                scores = jnp.concatenate(
-                    [masked(scores[n * rows : (n + 1) * rows]) for n in range(pair)], axis=0
-                )
-            top = jnp.max(scores, axis=1, keepdims=True)
-            if not fresh:
-                before = jnp.concatenate([stat[:, g : g + 1] for g in range(i, i + pair)], axis=0)
-                top = jnp.maximum(top, before)
-            shift = top * SCALE2
-            probs = jnp.exp2(scores * SCALE2 - shift).astype(BF16)
-            out = mm(probs, valued)
+            shift = jnp.concatenate(shifts[i : i + pair], axis=0)
+            probs = []
+            for n, s in enumerate(scores):
+                if fresh and n > 0:
+                    x = s * SCALE2 - (shift + jnp.where(flags[n], 0.0, -LOW).astype(F32))
+                else:
+                    x = s * SCALE2 - shift
+                if fresh and n == 0:
+                    x = jnp.concatenate(
+                        [jnp.where(causal, x[m * rows : (m + 1) * rows], LOW) for m in range(pair)], axis=0
+                    )
+                probs.append(jnp.exp2(x).astype(BF16))
+            out = mm(jnp.concatenate(probs, axis=1), wide)
             for n in range(pair):
                 g = i + n
                 cols = slice(g * HD, (g + 1) * HD)
                 band = slice(n * rows, (n + 1) * rows)
                 summed, total = out[band, :HD], out[band, HD:]
-                if not fresh:
-                    keep = jnp.exp2(before[band] * SCALE2 - shift[band])
-                    summed = summed + keep * acc[:, cols]
-                    total = total + keep * stat[:, group + g : group + g + 1]
-                acc[:, cols] = summed
-                now = jnp.where(lane == g, top[band], stat[...])
-                stat[...] = jnp.where(lane == group + g, total, now)
+                if fresh:
+                    acc[:, cols] = summed
+                    old = jnp.where(lane == g, shifts[g], 0.0 if g == 0 else stat[...])
+                    stat[...] = jnp.where(lane == group + g, total, old)
+                else:
+                    acc[:, cols] += summed
+                    stat[...] += jnp.where(lane == group + g, total, 0.0)
             scores = ahead
 
-    for (keys, values), distance in zip(chunks, distances):
+    for n, distance in enumerate(distances):
+        here = slice((distance if last else n) * PLANE, ((distance if last else n) + 1) * PLANE)
         if distance == 0:
-            attend(keys, values, True)
+            attend(keys[here], values[here], True)
         else:
-            pl.when(z_of(pos) >= distance)(functools.partial(attend, keys, values, False))
-    if last:
-        for g in range(group):
-            cols = slice(g * HD, (g + 1) * HD)
-            out_ref[:, cols] = (acc[:, cols] / stat[:, group + g : group + g + 1]).astype(BF16)
-
-
-def soft_step(pos, query, pieces, distances, state, into, span, kv_count, last, token):
+            pl.when(z_of(pos) >= distance)(functools.partial(attend, keys[here], values[here], False))
+    if not last:
+        return
+    for g in range(group):
+        cols = slice(g * HD, (g + 1) * HD)
+        out_ref[:, cols] = (acc[:, cols] / stat[:, group + g : group + g + 1]).astype(BF16)
+
+    sums = jnp.where((lane >= group) & (lane < 2 * group), stat[...], 0.0)
+    fine = jnp.min(jnp.where(sums < LIMIT, 1.0, 0.0))
+
+    @pl.when(fine < 0.5)
+    def _():
+        def one(g, carry):
+            cols = pl.ds(pl.multiple_of(g * HD, HD), HD)
+            query = q_ref[:, cols]
+            top = total = summed = None
+            for n in range(count):
+                x = mm_bt(query, keys[n][...]) * SCALE2
+                if n == 0:
+                    x = jnp.where(causal, x, LOW)
+                else:
+                    shown = flags[n] if n < PLANE else z_of(pos) >= n // PLANE
+                    x = jnp.where(shown, x, LOW)
+                high = jnp.max(x, axis=1, keepdims=True)
+                if n > 0:
+                    high = jnp.maximum(high, top)
+                probs = jnp.exp2(x - high)
+                part = mm(probs.astype(BF16), values[n][...])
+                more = jnp.sum(probs, axis=1, keepdims=True)
+                if n > 0:
+                    keep = jnp.exp2(top - high)
+                    part = part + keep * summed
+                    more = more + keep * total
+                top, total, summed = high, more, part
+            out_ref[:, cols] = (summed / total).astype(BF16)
+            return carry
+
+        lax.fori_loop(0, group, one, 0)
+
+
+def soft_step(pos, query, pieces, distances, state, into, span, kv_count, planes, last, token):
     rows, width = query.shape
     group = width // HD // kv_count
     first = distances[0] == 0
@@ -416,11 +460,9 @@
     stat = pl.BlockSpec((1, rows, HD), lambda k: (begin + k, 0, 0))
     keys = pl.BlockSpec((rows, HD), lambda k: (0, begin + k))
     values = pl.BlockSpec((rows, HD), lambda k: (0, kv_count + begin + k))
-    in_specs = [SCALAR, block]
-    operands = [pos, query]
-    for d in distances:
-        in_specs += [keys] * PLANE + [values] * PLANE
-        operands += pieces[d] + pieces[d]
+    used = [a for d in (range(planes) if last else distances) for a in pieces[d]]
+    in_specs = [SCALAR, block] + [keys] * len(used) + [values] * len(used)
+    operands = [pos, query] + used + used
     aliases = {}
     if not first:
         if not last:
@@ -449,7 +491,9 @@
         ]
         scratch = []
     return pl.pallas_call(
-        functools.partial(soft_kernel, group=group, distances=distances, last=last, passed=passed),
+        functools.partial(
+            soft_kernel, group=group, distances=distances, planes=planes, last=last, passed=passed
+        ),
         grid=(count,),
         in_specs=in_specs,
         out_specs=out_specs,
@@ -498,9 +542,11 @@
 
     paired = jnp.concatenate([soft_key, soft_value], axis=1)
     crossed = over_x(paired)
-    arrived = [paired]
-    for _ in range(1, planes):
-        arrived.append(over_z(arrived[-1], 1))
+    arrived = [paired, over_z(paired, 1)]
+
+    def forward(token):
+        arrived.append(over_z(after(arrived[-1], token), 1))
+
     pieces = [[paired, crossed, over_core(paired), over_core(crossed)]]
 
     half = max(kv_count // 2, 1)
@@ -508,7 +554,7 @@
 
     def soft(distances, state, last, token, span=None, into=None):
         *state, token = soft_step(
-            pos, soft_query, pieces, distances, state, into, span or (0, kv_count), kv_count, last, token
+            pos, soft_query, pieces, distances, state, into, span or (0, kv_count), kv_count, planes, last, token
         )
         return state, token
 
@@ -526,45 +572,50 @@
         pieces[d] += [over_core(after(a, token)) for a in pieces[d]]
 
     cross(1, token)
+    forward(token)
     state, token = soft((0,), None, False, token, spans[0])
     chip_send, chip_keep, token = small(chip_kernel, pos, [keep, other], [quarter, quarter], qh, "chip", token)
     chip_other = over_x(chip_send)
     cross(2, token)
+    forward(token)
     if len(spans) > 1:
         state, token = soft((0,), None, False, token, spans[1], state)
     plane, token = small(plane_kernel, pos, [chip_keep, chip_other], [quarter], qh, "plane", token)
     earlier = [over_z(plane, d) for d in range(1, planes)]
     spread_core(1, token)
     spread_core(2, token)
-    for d in range(1, planes - 2):
-        cross(d + 2, token)
-        state, token = soft((d,), state, False, token)
-        if d > 1:
-            spread_core(d + 1, token)
-    state, token = soft((planes - 2,), state, False, token, spans[0])
+    cross(3, token)
+    for d in range(3, planes - 1):
+        forward(token)
+        cross(d + 1, token)
+    both = (2, qh * HD, HD)
+    rest = (planes - 1,)
+    for middle in [(1, 2)] + [(d,) for d in range(3, planes - 1)]:
+        for n, span in enumerate(spans):
+            state, token = soft(middle, state, False, token, span)
+            if n == 0:
+                spread_core(middle[-1] + 1, token)
     enter_send, enter_keep, token = small(
         enter_kernel, pos, [chip_keep, chip_other] + earlier, [quarter, quarter], qh, "enter", token
     )
     enter_other = over_x(enter_send)
-    if len(spans) > 1:
-        state, token = soft((planes - 2,), state, False, token, spans[1])
-    spread_core(planes - 1, token)
-    both = (2, qh * HD, HD)
+    soft_out, token = soft(rest, state, True, token, spans[0])
     state_send, state_keep, token = small(
         core_kernel, pos, [enter_keep, enter_other, keep, other], [both, both], qh, "core", token
     )
     state_other = over_core(state_send)
-    soft_out, token = soft((planes - 1,), state, True, token, spans[0])
+    for span in spans[1:]:
+        soft_out, token = soft(rest, state, True, token, span, soft_out)
     raw, square, token = light(
         pos, light_query, light_key, light_value, cum, cumt, state_keep, state_other, token
     )
+    squares = [square]
     step = 1
     while step < tp:
-        square = square + lax.ppermute(square, "tp", [(i, i ^ step) for i in range(tp)])
+        square = sum(squares)
+        squares = [square, lax.ppermute(square, "tp", [(i, i ^ step) for i in range(tp)])]
         step *= 2
-    if len(spans) > 1:
-        soft_out, token = soft((planes - 1,), state, True, token, spans[1], soft_out)
-    light_out = finish(raw, square, norm_gain, out_gate, heads * HD * tp, token)
+    light_out = finish(raw, squares, norm_gain, out_gate, heads * HD * tp, token)
     return (light_out, soft_out[0])
 
 

time: 156 us -> 124 us (0.79)
  Pallas kernels: 117 us -> 77.3 us
  waiting for transfers between devices: 7.03 us -> 17.4 us
    pallas_call x7 -> x6, Pallas kernels: 88.9 us -> 57 us  [soft_step(): pl.pallas_call(functools.partial(soft_kernel, group=group, distances=dist...]
    pallas_call x1, Pallas kernels: 7.55 us -> 3.64 us  [finish(): pl.pallas_call(functools.partial(finish_kernel, features=features), grid=...]
    ppermute x1, waiting for transfers between devices: 0.01 us -> 3.83 us  [local(): lax.ppermute(square, 'tp', [(i, i ^ step) for i in range(tp)])]
    ppermute x6, waiting for transfers between devices: 5.8 us -> 9.45 us  [over_x(): return lax.ppermute(a, 'ctx', [(i, i ^ 2) for i in range(ctx)])]
    ppermute x6, waiting for transfers between devices: 1.2 us -> 4.07 us  [over_z(): lax.ppermute(a, 'ctx', [(i, i + PLANE * d) for i in range(ctx - PLANE * d)])]
    pallas_call x1, Pallas kernels: 8.81 us -> 6.69 us  [light(): pl.pallas_call(functools.partial(light_kernel, qh=wide // HD), grid=(4,),...]
    pallas_call x1, Pallas kernels: 7.15 us -> 5.12 us  [local_state(): pl.pallas_call(functools.partial(state_kernel, qh=qh, heads=heads), grid_...]
    unnamed x37 -> x17, local copies, waits for them, and re-layouts: 6.1 us -> 4.93 us
  transfers between devices with their start and end apart: 23 -> 23, of which waited for: 4 -> 5; matrix products, arithmetic and copies ran while one was open for 0% -> 0% of each run, Pallas kernels for 65% -> 53%
where the time goes in v3:
time: 124 us; the launch traced here: 123 us
  Pallas kernels  77.3 us (62%)
  starting transfers between devices  21.5 us (17%)
  waiting for transfers between devices  17.4 us (14%)
  local copies, waits for them, and re-layouts  5.91 us (5%)
    pallas_call x6, Pallas kernels, soft_step(): pl.pallas_call(functools.partial(soft_kernel, group=group, distances=dist...  57 us
    ppermute x6, waiting for transfers between devices, over_x(): return lax.ppermute(a, 'ctx', [(i, i ^ 2) for i in range(ctx)])  9.45 us
    ppermute x6, starting transfers between devices, over_z(): lax.ppermute(a, 'ctx', [(i, i + PLANE * d) for i in range(ctx - PLANE * d)])  7.89 us
    ppermute x10, starting transfers between devices, over_core(): return lax.ppermute(a, 'ctx', [(i, i ^ 1) for i in range(ctx)])  7.24 us
    pallas_call x1, Pallas kernels, light(): pl.pallas_call(functools.partial(light_kernel, qh=wide // HD), grid=(4,),...  6.69 us
    pallas_call x1, Pallas kernels, local_state(): pl.pallas_call(functools.partial(state_kernel, qh=qh, heads=heads), grid_...  5.12 us
    ppermute x6, starting transfers between devices, over_x(): return lax.ppermute(a, 'ctx', [(i, i ^ 2) for i in range(ctx)])  5.01 us
    unnamed x17, local copies, waits for them, and re-layouts  4.93 us
  transfers between devices with their start and end apart: 23, of which 5 were waited for; matrix products, arithmetic and copies ran while one was open for 0% of the time, Pallas kernels for 53%

profile of v3, /device:TPU:27, one launch (start us, length us, event | category | flops | bytes accessed | tf_op | source)
XLA Modules:
  0.0 122.9 jit_solution(11487788912493500709)
XLA Ops:
  3.6 1.3 %collective-permute-start.3 = (bf16[256,1024]{1,0:T(8,128)(2,1)S(1)}, bf16[256,1024]{1,0:T(8,128)(2,1)S(1)}, u32[]{:S(2)}, u32[]{:S(2)}) collective-permute-start(bf16[256,1024]{1,0:T(8,128)(2,1)S(1)} %constant_dynamic-update-slice_fusion.refs_0_.refs_4_.refs_16_), channel_id=1, source_target_pairs={{0,8},{2,10},{4,12},{6,14},{8,16},{10,18},{12,20},{14,22},{16,24},... | collective-permute-start | bytes 1572872 | tf_op jit(solution)/shard_map/ppermute | solution.py:538
  4.9 1.6 %copy-done.1 = bf16[256,4096]{1,0:T(8,128)(2,1)S(1)} copy-done((bf16[256,4096]{1,0:T(8,128)(2,1)S(1)}, bf16[256,4096]{1,0:T(8,128)(2,1)}, u32[]{:S(2)}) %copy-start.1) | copy-done | bytes 2097176
  6.5 1.6 %copy-done.3 = bf16[256,4096]{1,0:T(8,128)(2,1)S(1)} copy-done((bf16[256,4096]{1,0:T(8,128)(2,1)S(1)}, bf16[256,4096]{1,0:T(8,128)(2,1)}, u32[]{:S(2)}) %copy-start.3) | copy-done | bytes 2097176
  8.9 5.1 %local_state.1 = (bf16[2,1040,128]{2,1,0:T(8,128)(2,1)S(1)}, bf16[2,1040,128]{2,1,0:T(8,128)(2,1)S(1)}, f32[4,256,128]{2,1,0:T(8,128)S(1)}, f32[4,8,256]{2,1,0:T(8,128)S(1)}, s32[1]{0:T(128)}) custom-call(s32[1]{0:T(128)} %bitcast.pos, bf16[256,4096]{1,0:T(8,128)(2,1)S(1)} %copy-done.1, bf16[256,4096]{1,0:T(8,128)(2,1)S(1)} %copy-done.3, f32[32,256]{1,0:T(8,128)S(1)} %bitcast.3), custom_call_target="tpu_custom_call" | custom-call | flops 1000 | bytes 1048576 | tf_op jit(solution)/shard_map/local_state/pallas_call | solution.py:124
  14.4 2.4 %collective-permute-done.1.refs_1_.refs_5_.refs_17_ = bf16[256,1024]{1,0:T(8,128)(2,1)S(1)} collective-permute-done((bf16[256,1024]{1,0:T(8,128)(2,1)S(1)}, bf16[256,1024]{1,0:T(8,128)(2,1)S(1)}, u32[]{:S(2)}, u32[]{:S(2)}) %collective-permute-start.1) | collective-permute-done | bytes 524320 | tf_op jit(solution)/shard_map/ppermute | solution.py:535
  18.7 1.3 %collective-permute-start.9 = (bf16[256,1024]{1,0:T(8,128)(2,1)S(1)}, bf16[256,1024]{1,0:T(8,128)(2,1)S(1)}, u32[]{:S(2)}, u32[]{:S(2)}) collective-permute-start(bf16[256,1024]{1,0:T(8,128)(2,1)S(1)} %collective-permute-done.3.refs_0_.refs_8_.refs_4_.refs_20_), channel_id=1, source_target_pairs={{0,8},{2,10},{4,12},{6,14},{8,16},{10,18},{12,20},{14,22},{16,24},... | collective-permute-start | bytes 1572872 | tf_op jit(solution)/shard_map/ppermute | solution.py:538
  19.9 1.3 %collective-permute-start.4 = (bf16[256,1024]{1,0:T(8,128)(2,1)S(1)}, bf16[256,1024]{1,0:T(8,128)(2,1)S(1)}, u32[]{:S(2)}, u32[]{:S(2)}) collective-permute-start(bf16[256,1024]{1,0:T(8,128)(2,1)S(1)} %collective-permute-done.3.refs_0_.refs_8_.refs_4_.refs_20_), channel_id=1, source_target_pairs={{0,4},{2,6},{4,0},{6,2},{8,12},{10,14},{12,8},{14,10},{16,20},{18,... | collective-permute-start | bytes 1572872 | tf_op jit(solution)/shard_map/ppermute | solution.py:535
  21.2 7.2 %softmax.6 = (f32[256,4096]{1,0:T(8,128)S(1)}, f32[4,256,128]{2,1,0:T(8,128)S(1)}, s32[1]{0:T(128)}) custom-call(s32[1]{0:T(128)} %bitcast.pos, bf16[256,4096]{1,0:T(8,128)(2,1)S(1)} %copy-done, bf16[256,1024]{1,0:T(8,128)(2,1)S(1)} %constant_dynamic-update-slice_fusion.refs_0_.refs_4_.refs_16_, ...), custom_call_target="tpu_custom_call" | custom-call | flops 1000 | bytes 1048576 | tf_op jit(solution)/shard_map/softmax/pallas_call | solution.py:493
  29.7 3.1 %collective-permute-done.9.refs_4_.refs_12_.refs_8_.refs_24_ = bf16[256,1024]{1,0:T(8,128)(2,1)S(1)} collective-permute-done((bf16[256,1024]{1,0:T(8,128)(2,1)S(1)}, bf16[256,1024]{1,0:T(8,128)(2,1)S(1)}, u32[]{:S(2)}, u32[]{:S(2)}) %collective-permute-start.9) | collective-permute-done | bytes 524320 | tf_op jit(solution)/shard_map/ppermute | solution.py:538
  34.0 1.3 %collective-permute-start.13 = (bf16[256,1024]{1,0:T(8,128)(2,1)S(1)}, bf16[256,1024]{1,0:T(8,128)(2,1)S(1)}, u32[]{:S(2)}, u32[]{:S(2)}) collective-permute-start(bf16[256,1024]{1,0:T(8,128)(2,1)S(1)} %collective-permute-done.9.refs_4_.refs_12_.refs_8_.refs_24_), channel_id=1, source_target_pairs={{0,8},{2,10},{4,12},{6,14},{8,16},{10,18},{12,20},{14,22},{16,24},... | collective-permute-start | bytes 1572872 | tf_op jit(solution)/shard_map/ppermute | solution.py:538
  35.6 7.2 %softmax.7 = (f32[256,4096]{1,0:T(8,128)S(1)}, f32[4,256,128]{2,1,0:T(8,128)S(1)}, s32[1]{0:T(128)}) custom-call(s32[1]{0:T(128)} %bitcast.pos, bf16[256,4096]{1,0:T(8,128)(2,1)S(1)} %copy-done, bf16[256,1024]{1,0:T(8,128)(2,1)S(1)} %constant_dynamic-update-slice_fusion.refs_0_.refs_4_.refs_16_, ...), custom_call_target="tpu_custom_call", output_to_operand_aliasing={{0}: (11, {}), {1}: (12, {})} | custom-call | flops 1000 | bytes 1048576 | tf_op jit(solution)/shard_map/softmax/pallas_call | solution.py:493
  42.8 7.0 %collective-permute-done.6.refs_1_ = bf16[1040,128]{1,0:T(8,128)(2,1)S(1)} collective-permute-done((bf16[1040,128]{1,0:T(8,128)(2,1)S(1)}, bf16[1040,128]{1,0:T(8,128)(2,1)S(1)}, u32[]{:S(2)}, u32[]{:S(2)}) %collective-permute-start.6) | collective-permute-done | bytes 266272 | tf_op jit(solution)/shard_map/ppermute | solution.py:535
  51.0 3.1 %collective-permute-start.11 = (bf16[256,1024]{1,0:T(8,128)(2,1)S(1)}, bf16[256,1024]{1,0:T(8,128)(2,1)S(1)}, u32[]{:S(2)}, u32[]{:S(2)}) collective-permute-start(bf16[256,1024]{1,0:T(8,128)(2,1)S(1)} %collective-permute-done.9.refs_4_.refs_12_.refs_8_.refs_24_), channel_id=1, source_target_pairs={{0,2},{2,0},{4,6},{6,4},{8,10},{10,8},{12,14},{14,12},{16,18},{18,... | collective-permute-start | bytes 1572872 | tf_op jit(solution)/shard_map/ppermute | solution.py:532
  55.9 1.3 %collective-permute-start.17 = (bf16[1040,128]{1,0:T(8,128)(2,1)S(1)}, bf16[1040,128]{1,0:T(8,128)(2,1)S(1)}, u32[]{:S(2)}, u32[]{:S(2)}) collective-permute-start(bf16[1040,128]{1,0:T(8,128)(2,1)S(1)} %get-tuple-element.78), channel_id=1, source_target_pairs={{0,8},{2,10},{4,12},{6,14},{8,16},{10,18},{12,20},{14,22},{16,24},... | collective-permute-start | bytes 798728 | tf_op jit(solution)/shard_map/ppermute | solution.py:538
  57.2 1.3 %collective-permute-start.18 = (bf16[1040,128]{1,0:T(8,128)(2,1)S(1)}, bf16[1040,128]{1,0:T(8,128)(2,1)S(1)}, u32[]{:S(2)}, u32[]{:S(2)}) collective-permute-start(bf16[1040,128]{1,0:T(8,128)(2,1)S(1)} %get-tuple-element.78), channel_id=1, source_target_pairs={{0,16},{2,18},{4,20},{6,22},{8,24},{10,26},{12,28},{14,30},{1,17},... | collective-permute-start | bytes 798728 | tf_op jit(solution)/shard_map/ppermute | solution.py:538
  58.5 1.5 %collective-permute-start.19 = (bf16[1040,128]{1,0:T(8,128)(2,1)S(1)}, bf16[1040,128]{1,0:T(8,128)(2,1)S(1)}, u32[]{:S(2)}, u32[]{:S(2)}) collective-permute-start(bf16[1040,128]{1,0:T(8,128)(2,1)S(1)} %get-tuple-element.78), channel_id=1, source_target_pairs={{0,24},{2,26},{4,28},{6,30},{1,25},{3,27},{5,29},{7,31}} | collective-permute-start | bytes 798728 | tf_op jit(solution)/shard_map/ppermute | solution.py:538
  60.0 12.2 %softmax.8 = (f32[256,4096]{1,0:T(8,128)S(1)}, f32[4,256,128]{2,1,0:T(8,128)S(1)}, s32[1]{0:T(128)}) custom-call(s32[1]{0:T(128)} %bitcast.pos, bf16[256,4096]{1,0:T(8,128)(2,1)S(1)} %copy-done, bf16[256,1024]{1,0:T(8,128)(2,1)S(1)} %collective-permute-done.3.refs_0_.refs_8_.refs_4_.refs_20_, ...), custom_call_target="tpu_custom_call", output_to_operand_aliasing={{0}: (18, {}), {1}: (19, {})} | custom-call | flops 1000 | bytes 1048576 | tf_op jit(solution)/shard_map/softmax/pallas_call | solution.py:493
  73.0 12.1 %softmax.9 = (f32[256,4096]{1,0:T(8,128)S(1)}, f32[4,256,128]{2,1,0:T(8,128)S(1)}, s32[1]{0:T(128)}) custom-call(s32[1]{0:T(128)} %bitcast.pos, bf16[256,4096]{1,0:T(8,128)(2,1)S(1)} %copy-done, bf16[256,1024]{1,0:T(8,128)(2,1)S(1)} %collective-permute-done.3.refs_0_.refs_8_.refs_4_.refs_20_, ...), custom_call_target="tpu_custom_call", output_to_operand_aliasing={{0}: (18, {}), {1}: (19, {})} | custom-call | flops 1000 | bytes 1048576 | tf_op jit(solution)/shard_map/softmax/pallas_call | solution.py:493
  87.1 9.1 %softmax.10 = (bf16[256,4096]{1,0:T(8,128)(2,1)}, s32[1]{0:T(128)}) custom-call(s32[1]{0:T(128)} %bitcast.pos, bf16[256,4096]{1,0:T(8,128)(2,1)S(1)} %copy-done, bf16[256,1024]{1,0:T(8,128)(2,1)S(1)} %constant_dynamic-update-slice_fusion.refs_0_.refs_4_.refs_16_, bf16[256,1024]{1,0:T(8,128)(2,1)S(1)} %collective-permute-done.1.refs_1_.refs_5_.refs_17_, ...), custom_call_target="tpu_custom_call" | custom-call | flops 1000 | bytes 1048576 | tf_op jit(solution)/shard_map/softmax/pallas_call | solution.py:493
  98.1 9.3 %softmax.11 = (bf16[256,4096]{1,0:T(8,128)(2,1)}, s32[1]{0:T(128)}) custom-call(s32[1]{0:T(128)} %bitcast.pos, bf16[256,4096]{1,0:T(8,128)(2,1)S(1)} %copy-done, bf16[256,1024]{1,0:T(8,128)(2,1)S(1)} %constant_dynamic-update-slice_fusion.refs_0_.refs_4_.refs_16_, ...), custom_call_target="tpu_custom_call", output_to_operand_aliasing={{0}: (37, {})} | custom-call | flops 1000 | bytes 1048576 | tf_op jit(solution)/shard_map/softmax/pallas_call | solution.py:493
  107.4 6.7 %light.1 = (bf16[256,4096]{1,0:T(8,128)(2,1)S(1)}, f32[256,128]{1,0:T(8,128)S(1)}, s32[1]{0:T(128)}) custom-call(s32[1]{0:T(128)} %bitcast.pos, bf16[256,4096]{1,0:T(8,128)(2,1)S(1)} %copy-done.5, bf16[256,4096]{1,0:T(8,128)(2,1)S(1)} %copy-done.2, bf16[256,4096]{1,0:T(8,128)(2,1)S(1)} %copy-done.3, f32[4,256,128]{2,1,0:T(8,128)S(1)} %get-tuple-element.48.cum_ref, ...), custom_call_target="tpu_custom_call" | custom-call | flops 1000 | bytes 1048576 | tf_op jit(solution)/shard_map/light/pallas_call | solution.py:281
  114.1 1.3 %collective-permute-start.22 = (f32[256,128]{1,0:T(8,128)S(1)}, f32[256,128]{1,0:T(8,128)S(1)}, u32[]{:S(2)}, u32[]{:S(2)}) collective-permute-start(f32[256,128]{1,0:T(8,128)S(1)} %get-tuple-element.89.refs_0_), channel_id=1, source_target_pairs={{0,1},{1,0},{2,3},{3,2},{4,5},{5,4},{6,7},{7,6},{8,9},{9,8},{10,11... | collective-permute-start | bytes 393224 | tf_op jit(solution)/shard_map/ppermute | solution.py:616
  115.4 3.8 %collective-permute-done.22.refs_1_ = f32[256,128]{1,0:T(8,128)S(1)} collective-permute-done((f32[256,128]{1,0:T(8,128)S(1)}, f32[256,128]{1,0:T(8,128)S(1)}, u32[]{:S(2)}, u32[]{:S(2)}) %collective-permute-start.22) | collective-permute-done | bytes 131104 | tf_op jit(solution)/shard_map/ppermute | solution.py:616
  119.3 3.6 %finish.1 = bf16[256,4096]{1,0:T(8,128)(2,1)} custom-call(bf16[256,4096]{1,0:T(8,128)(2,1)S(1)} %get-tuple-element.88.raw_ref, f32[256,128]{1,0:T(8,128)S(1)} %get-tuple-element.89.refs_0_, f32[256,128]{1,0:T(8,128)S(1)} %collective-permute-done.22.refs_1_, f32[1,4096]{1,0:T(1,128)S(1)} %bitcast.4, bf16[256,4096]{1,0:T(8,128)(2,1)S(1)} %copy-done.4, ...), custom_call_target="tpu_custom_call" | custom-call | flops 1000 | bytes 1048576 | tf_op jit(solution)/shard_map/finish/pallas_call | solution.py:325
  (53 shorter events, 16.4 us)
Async XLA Ops:
  2.6 2.3 %collective-permute-start = (bf16[256,1024]{1,0:T(8,128)(2,1)S(1)}, bf16[256,1024]{1,0:T(8,128)(2,1)S(1)}, u32[]{:S(2)}, u32[]{:S(2)}) collective-permute-start(bf16[256,1024]{1,0:T(8,128)(2,1)S(1)} %constant_dynamic-update-slice_fusion.refs_0_.refs_4_.refs_16_), channel_id=1, source_target_pairs={{0,2},{2,0},{4,6},{6,4},{8,10},{10,8},{12,14},{14,12},{16,18},{18,... | collective-permute-start | bytes 1572872 | tf_op jit(solution)/shard_map/ppermute | solution.py:532
  3.3 13.5 %collective-permute-start.1 = (bf16[256,1024]{1,0:T(8,128)(2,1)S(1)}, bf16[256,1024]{1,0:T(8,128)(2,1)S(1)}, u32[]{:S(2)}, u32[]{:S(2)}) collective-permute-start(bf16[256,1024]{1,0:T(8,128)(2,1)S(1)} %constant_dynamic-update-slice_fusion.refs_0_.refs_4_.refs_16_), channel_id=1, source_target_pairs={{0,4},{2,6},{4,0},{6,2},{8,12},{10,14},{12,8},{14,10},{16,20},{18,... | collective-permute-start | bytes 1572872 | tf_op jit(solution)/shard_map/ppermute | solution.py:535
  3.6 15.0 %collective-permute-start.3 = (bf16[256,1024]{1,0:T(8,128)(2,1)S(1)}, bf16[256,1024]{1,0:T(8,128)(2,1)S(1)}, u32[]{:S(2)}, u32[]{:S(2)}) collective-permute-start(bf16[256,1024]{1,0:T(8,128)(2,1)S(1)} %constant_dynamic-update-slice_fusion.refs_0_.refs_4_.refs_16_), channel_id=1, source_target_pairs={{0,8},{2,10},{4,12},{6,14},{8,16},{10,18},{12,20},{14,22},{16,24},... | collective-permute-start | bytes 1572872 | tf_op jit(solution)/shard_map/ppermute | solution.py:538
  8.9 12.4 %copy-start = (bf16[256,4096]{1,0:T(8,128)(2,1)S(1)}, bf16[256,4096]{1,0:T(8,128)(2,1)}, u32[]{:S(2)}) copy-start(bf16[256,4096]{1,0:T(8,128)(2,1)} %q_ref.12) | copy-start | bytes 6291460
  14.0 14.5 %collective-permute-start.5 = (bf16[2,1040,128]{2,1,0:T(8,128)(2,1)S(1)}, bf16[2,1040,128]{2,1,0:T(8,128)(2,1)S(1)}, u32[]{:S(2)}, u32[]{:S(2)}) collective-permute-start(bf16[2,1040,128]{2,1,0:T(8,128)(2,1)S(1)} %get-tuple-element.54), channel_id=1, source_target_pairs={{0,2},{2,0},{4,6},{6,4},{8,10},{10,8},{12,14},{14,12},{16,18},{18,... | collective-permute-start | bytes 1597448 | tf_op jit(solution)/shard_map/ppermute | solution.py:532
  16.8 4.4 %collective-permute-start.2 = (bf16[256,1024]{1,0:T(8,128)(2,1)S(1)}, bf16[256,1024]{1,0:T(8,128)(2,1)S(1)}, u32[]{:S(2)}, u32[]{:S(2)}) collective-permute-start(bf16[256,1024]{1,0:T(8,128)(2,1)S(1)} %collective-permute-done.1.refs_1_.refs_5_.refs_17_), channel_id=1, source_target_pairs={{0,2},{2,0},{4,6},{6,4},{8,10},{10,8},{12,14},{14,12},{16,18},{18,... | collective-permute-start | bytes 1572872 | tf_op jit(solution)/shard_map/ppermute | solution.py:532
  18.7 14.1 %collective-permute-start.9 = (bf16[256,1024]{1,0:T(8,128)(2,1)S(1)}, bf16[256,1024]{1,0:T(8,128)(2,1)S(1)}, u32[]{:S(2)}, u32[]{:S(2)}) collective-permute-start(bf16[256,1024]{1,0:T(8,128)(2,1)S(1)} %collective-permute-done.3.refs_0_.refs_8_.refs_4_.refs_20_), channel_id=1, source_target_pairs={{0,8},{2,10},{4,12},{6,14},{8,16},{10,18},{12,20},{14,22},{16,24},... | collective-permute-start | bytes 1572872 | tf_op jit(solution)/shard_map/ppermute | solution.py:538
  19.9 34.1 %collective-permute-start.4 = (bf16[256,1024]{1,0:T(8,128)(2,1)S(1)}, bf16[256,1024]{1,0:T(8,128)(2,1)S(1)}, u32[]{:S(2)}, u32[]{:S(2)}) collective-permute-start(bf16[256,1024]{1,0:T(8,128)(2,1)S(1)} %collective-permute-done.3.refs_0_.refs_8_.refs_4_.refs_20_), channel_id=1, source_target_pairs={{0,4},{2,6},{4,0},{6,2},{8,12},{10,14},{12,8},{14,10},{16,20},{18,... | collective-permute-start | bytes 1572872 | tf_op jit(solution)/shard_map/ppermute | solution.py:535
  32.8 21.8 %collective-permute-start.10 = (bf16[256,1024]{1,0:T(8,128)(2,1)S(1)}, bf16[256,1024]{1,0:T(8,128)(2,1)S(1)}, u32[]{:S(2)}, u32[]{:S(2)}) collective-permute-start(bf16[256,1024]{1,0:T(8,128)(2,1)S(1)} %collective-permute-done.9.refs_4_.refs_12_.refs_8_.refs_24_), channel_id=1, source_target_pairs={{0,4},{2,6},{4,0},{6,2},{8,12},{10,14},{12,8},{14,10},{16,20},{18,... | collective-permute-start | bytes 1572872 | tf_op jit(solution)/shard_map/ppermute | solution.py:535
  34.0 20.6 %collective-permute-start.13 = (bf16[256,1024]{1,0:T(8,128)(2,1)S(1)}, bf16[256,1024]{1,0:T(8,128)(2,1)S(1)}, u32[]{:S(2)}, u32[]{:S(2)}) collective-permute-start(bf16[256,1024]{1,0:T(8,128)(2,1)S(1)} %collective-permute-done.9.refs_4_.refs_12_.refs_8_.refs_24_), channel_id=1, source_target_pairs={{0,8},{2,10},{4,12},{6,14},{8,16},{10,18},{12,20},{14,22},{16,24},... | collective-permute-start | bytes 1572872 | tf_op jit(solution)/shard_map/ppermute | solution.py:538
  35.3 14.5 %collective-permute-start.6 = (bf16[1040,128]{1,0:T(8,128)(2,1)S(1)}, bf16[1040,128]{1,0:T(8,128)(2,1)S(1)}, u32[]{:S(2)}, u32[]{:S(2)}) collective-permute-start(bf16[1040,128]{1,0:T(8,128)(2,1)S(1)} %get-tuple-element.60), channel_id=1, source_target_pairs={{0,4},{2,6},{4,0},{6,2},{8,12},{10,14},{12,8},{14,10},{16,20},{18,... | collective-permute-start | bytes 798728 | tf_op jit(solution)/shard_map/ppermute | solution.py:535
  51.0 4.9 %collective-permute-start.11 = (bf16[256,1024]{1,0:T(8,128)(2,1)S(1)}, bf16[256,1024]{1,0:T(8,128)(2,1)S(1)}, u32[]{:S(2)}, u32[]{:S(2)}) collective-permute-start(bf16[256,1024]{1,0:T(8,128)(2,1)S(1)} %collective-permute-done.9.refs_4_.refs_12_.refs_8_.refs_24_), channel_id=1, source_target_pairs={{0,2},{2,0},{4,6},{6,4},{8,10},{10,8},{12,14},{14,12},{16,18},{18,... | collective-permute-start | bytes 1572872 | tf_op jit(solution)/shard_map/ppermute | solution.py:532
  54.0 3.1 %collective-permute-start.8 = (bf16[256,1024]{1,0:T(8,128)(2,1)S(1)}, bf16[256,1024]{1,0:T(8,128)(2,1)S(1)}, u32[]{:S(2)}, u32[]{:S(2)}) collective-permute-start(bf16[256,1024]{1,0:T(8,128)(2,1)S(1)} %collective-permute-done.4.refs_1_.refs_9_.refs_5_.refs_21_), channel_id=1, source_target_pairs={{0,2},{2,0},{4,6},{6,4},{8,10},{10,8},{12,14},{14,12},{16,18},{18,... | collective-permute-start | bytes 1572872 | tf_op jit(solution)/shard_map/ppermute | solution.py:532
  54.1 4.3 %collective-permute-start.7 = (bf16[256,1024]{1,0:T(8,128)(2,1)S(1)}, bf16[256,1024]{1,0:T(8,128)(2,1)S(1)}, u32[]{:S(2)}, u32[]{:S(2)}) collective-permute-start(bf16[256,1024]{1,0:T(8,128)(2,1)S(1)} %collective-permute-done.3.refs_0_.refs_8_.refs_4_.refs_20_), channel_id=1, source_target_pairs={{0,2},{2,0},{4,6},{6,4},{8,10},{10,8},{12,14},{14,12},{16,18},{18,... | collective-permute-start | bytes 1572872 | tf_op jit(solution)/shard_map/ppermute | solution.py:532
  54.6 5.4 %collective-permute-start.12 = (bf16[256,1024]{1,0:T(8,128)(2,1)S(1)}, bf16[256,1024]{1,0:T(8,128)(2,1)S(1)}, u32[]{:S(2)}, u32[]{:S(2)}) collective-permute-start(bf16[256,1024]{1,0:T(8,128)(2,1)S(1)} %collective-permute-done.10.refs_5_.refs_13_.refs_9_.refs_25_), channel_id=1, source_target_pairs={{0,2},{2,0},{4,6},{6,4},{8,10},{10,8},{12,14},{14,12},{16,18},{18,... | collective-permute-start | bytes 1572872 | tf_op jit(solution)/shard_map/ppermute | solution.py:532
  54.6 17.5 %collective-permute-start.14 = (bf16[256,1024]{1,0:T(8,128)(2,1)S(1)}, bf16[256,1024]{1,0:T(8,128)(2,1)S(1)}, u32[]{:S(2)}, u32[]{:S(2)}) collective-permute-start(bf16[256,1024]{1,0:T(8,128)(2,1)S(1)} %collective-permute-done.13.refs_12_.refs_28_), channel_id=1, source_target_pairs={{0,4},{2,6},{4,0},{6,2},{8,12},{10,14},{12,8},{14,10},{16,20},{18,... | collective-permute-start | bytes 1572872 | tf_op jit(solution)/shard_map/ppermute | solution.py:535
  55.9 29.3 %collective-permute-start.17 = (bf16[1040,128]{1,0:T(8,128)(2,1)S(1)}, bf16[1040,128]{1,0:T(8,128)(2,1)S(1)}, u32[]{:S(2)}, u32[]{:S(2)}) collective-permute-start(bf16[1040,128]{1,0:T(8,128)(2,1)S(1)} %get-tuple-element.78), channel_id=1, source_target_pairs={{0,8},{2,10},{4,12},{6,14},{8,16},{10,18},{12,20},{14,22},{16,24},... | collective-permute-start | bytes 798728 | tf_op jit(solution)/shard_map/ppermute | solution.py:538
  57.2 28.0 %collective-permute-start.18 = (bf16[1040,128]{1,0:T(8,128)(2,1)S(1)}, bf16[1040,128]{1,0:T(8,128)(2,1)S(1)}, u32[]{:S(2)}, u32[]{:S(2)}) collective-permute-start(bf16[1040,128]{1,0:T(8,128)(2,1)S(1)} %get-tuple-element.78), channel_id=1, source_target_pairs={{0,16},{2,18},{4,20},{6,22},{8,24},{10,26},{12,28},{14,30},{1,17},... | collective-permute-start | bytes 798728 | tf_op jit(solution)/shard_map/ppermute | solution.py:538
  58.5 26.7 %collective-permute-start.19 = (bf16[1040,128]{1,0:T(8,128)(2,1)S(1)}, bf16[1040,128]{1,0:T(8,128)(2,1)S(1)}, u32[]{:S(2)}, u32[]{:S(2)}) collective-permute-start(bf16[1040,128]{1,0:T(8,128)(2,1)S(1)} %get-tuple-element.78), channel_id=1, source_target_pairs={{0,24},{2,26},{4,28},{6,30},{1,25},{3,27},{5,29},{7,31}} | collective-permute-start | bytes 798728 | tf_op jit(solution)/shard_map/ppermute | solution.py:538
  72.2 14.9 %collective-permute-start.16 = (bf16[256,1024]{1,0:T(8,128)(2,1)S(1)}, bf16[256,1024]{1,0:T(8,128)(2,1)S(1)}, u32[]{:S(2)}, u32[]{:S(2)}) collective-permute-start(bf16[256,1024]{1,0:T(8,128)(2,1)S(1)} %collective-permute-done.14.refs_13_.refs_29_), channel_id=1, source_target_pairs={{0,2},{2,0},{4,6},{6,4},{8,10},{10,8},{12,14},{14,12},{16,18},{18,... | collective-permute-start | bytes 1572872 | tf_op jit(solution)/shard_map/ppermute | solution.py:532
  72.9 14.2 %collective-permute-start.15 = (bf16[256,1024]{1,0:T(8,128)(2,1)S(1)}, bf16[256,1024]{1,0:T(8,128)(2,1)S(1)}, u32[]{:S(2)}, u32[]{:S(2)}) collective-permute-start(bf16[256,1024]{1,0:T(8,128)(2,1)S(1)} %collective-permute-done.13.refs_12_.refs_28_), channel_id=1, source_target_pairs={{0,2},{2,0},{4,6},{6,4},{8,10},{10,8},{12,14},{14,12},{16,18},{18,... | collective-permute-start | bytes 1572872 | tf_op jit(solution)/shard_map/ppermute | solution.py:532
  86.4 9.8 %collective-permute-start.20 = (bf16[1040,128]{1,0:T(8,128)(2,1)S(1)}, bf16[1040,128]{1,0:T(8,128)(2,1)S(1)}, u32[]{:S(2)}, u32[]{:S(2)}) collective-permute-start(bf16[1040,128]{1,0:T(8,128)(2,1)S(1)} %get-tuple-element.82), channel_id=1, source_target_pairs={{0,4},{2,6},{4,0},{6,2},{8,12},{10,14},{12,8},{14,10},{16,20},{18,... | collective-permute-start | bytes 798728 | tf_op jit(solution)/shard_map/ppermute | solution.py:535
  97.4 10.0 %collective-permute-start.21 = (bf16[2,1024,128]{2,1,0:T(8,128)(2,1)S(1)}, bf16[2,1024,128]{2,1,0:T(8,128)(2,1)S(1)}, u32[]{:S(2)}, u32[]{:S(2)}) collective-permute-start(bf16[2,1024,128]{2,1,0:T(8,128)(2,1)S(1)} %get-tuple-element.84), channel_id=1, source_target_pairs={{0,2},{2,0},{4,6},{6,4},{8,10},{10,8},{12,14},{14,12},{16,18},{18,... | collective-permute-start | bytes 1572872 | tf_op jit(solution)/shard_map/ppermute | solution.py:532
  114.1 5.2 %collective-permute-start.22 = (f32[256,128]{1,0:T(8,128)S(1)}, f32[256,128]{1,0:T(8,128)S(1)}, u32[]{:S(2)}, u32[]{:S(2)}) collective-permute-start(f32[256,128]{1,0:T(8,128)S(1)} %get-tuple-element.89.refs_0_), channel_id=1, source_target_pairs={{0,1},{1,0},{2,3},{3,2},{4,5},{5,4},{6,7},{7,6},{8,9},{9,8},{10,11... | collective-permute-start | bytes 393224 | tf_op jit(solution)/shard_map/ppermute | solution.py:616
  (7 other events, 46.3 us)

commit v4 on v3

--- a/solution.py
+++ b/solution.py
@@ -15,18 +15,20 @@
 PLANE = 4
 TAIL = 16
 VMEM = 32 * 2**20
+BIG = 60 * 2**20
 F32 = jnp.float32
 BF16 = jnp.bfloat16
 HIGH = lax.Precision.HIGHEST
 SCALAR = pl.BlockSpec(memory_space=pltpu.SMEM)
 ANY = pl.BlockSpec(memory_space=pl.ANY)
 NEXT = jax.ShapeDtypeStruct((1,), jnp.int32)
+FORMS = [(2, False, False), (2, False, False), (2, True, False), (2, False, True), (1, False, False), (2, False, False), (2, False, False)]
 COST = pl.CostEstimate(flops=1000, bytes_accessed=2**20, transcendentals=0)
 SCALE2 = HD ** (-0.5) * math.log2(math.e)
 
 
-def params(**more):
-    return pltpu.CompilerParams(vmem_limit_bytes=VMEM, **more)
+def params(limit=None):
+    return pltpu.CompilerParams(vmem_limit_bytes=limit or VMEM)
 
 
 def mm(a, b):
@@ -147,7 +149,7 @@
             jax.ShapeDtypeStruct((4, 8, rows), F32),
             NEXT,
         ],
-        compiler_params=params(),
+        compiler_params=params(BIG),
         cost_estimate=COST,
         name="local_state",
     )(pos, key, value, log_decay)
@@ -337,15 +339,25 @@
     )(raw, *squares, gain.reshape(1, width), gate, token)
 
 
-def soft_kernel(pos, q_ref, *refs, group, distances, planes, last, passed):
-    count = planes * PLANE if last else len(distances) * PLANE
+def shown(pos, rule):
+    if rule == "x":
+        return x_of(pos) == 1
+    if rule == "core":
+        return core_of(pos) == 1
+    return z_of(pos) >= rule
+
+
+def soft_kernel(pos, q_ref, *refs, group, rules, all_rules, last, passed, kv_count, begin, form):
+    pair, fold, early = form
+    pair = min(pair, group)
+    count = len(rules)
     keys, values, refs = refs[:count], refs[count : 2 * count], refs[2 * count :]
-    first = distances[0] == 0
+    first = rules[0] == "own"
     if not first:
         acc_in, stat_in, refs = refs[0], refs[1], refs[2:]
-    token, refs = refs[0], refs[passed:]
+    token, every, refs = refs[0], refs[1:passed], refs[passed:]
     if last:
-        out_ref, after, acc, stat = refs
+        out_ref, after, acc, stat, key_all, value_all = refs
     else:
         acc, stat, after = refs
         stat = stat.at[0]
@@ -353,39 +365,57 @@
     rows = q_ref.shape[0]
     lane = iota((rows, HD), 1)
     causal = iota((rows, rows), 0) >= iota((rows, rows), 1)
-    pair = min(group, 2)
-    flags = [None, x_of(pos) == 1, core_of(pos) == 1, x_of(pos) == 1]
 
     if not first:
         acc[...] = acc_in[...]
         stat[...] = stat_in[0]
 
-    def attend(keyed, valued, fresh):
+    def attend(keyed, valued, fresh, hidden):
         wide = jnp.concatenate([v[...] for v in valued], axis=0)
         wide = jnp.concatenate([wide, jnp.ones_like(wide)], axis=1)
+        keyed = [k[...] for k in keyed]
         if fresh:
-            own = keyed[0][...].astype(F32)
+            own = keyed[0].astype(F32)
             shifts = [
-                jnp.sum(q_ref[:, g * HD : (g + 1) * HD].astype(F32) * own, axis=1, keepdims=True) * SCALE2
+                jnp.sum(q_ref[:, g * HD : (g + 1) * HD].astype(F32) * own, axis=1, keepdims=True)
                 for g in range(group)
             ]
         else:
             shifts = [stat[:, g : g + 1] for g in range(group)]
+        if fold:
+            keyed = [
+                jnp.concatenate(
+                    [k, jnp.where(lane < 3, 1.0, jnp.where(lane == 3, h, 0.0)).astype(BF16)], axis=1
+                )
+                for k, h in zip(keyed, hidden)
+            ]
 
         def scored(i):
-            query = jnp.concatenate([q_ref[:, g * HD : (g + 1) * HD] for g in range(i, i + pair)], axis=0)
-            return [mm_bt(query, k[...]) for k in keyed]
-
-        scores = scored(0)
+            parts = []
+            for g in range(i, i + pair):
+                query = q_ref[:, g * HD : (g + 1) * HD]
+                if fold:
+                    high = shifts[g].astype(BF16).astype(F32)
+                    middle = (shifts[g] - high).astype(BF16).astype(F32)
+                    low = shifts[g] - high - middle
+                    more = jnp.where(lane == 0, -high, jnp.where(lane == 1, -middle, jnp.where(lane == 2, -low, 1.0)))
+                    query = jnp.concatenate([query, more.astype(BF16)], axis=1)
+                parts.append(query)
+            query = jnp.concatenate(parts, axis=0)
+            return [mm_bt(query, k) for k in keyed]
+
+        ahead = scored(0)
         for i in range(0, group, pair):
-            ahead = scored(i + pair) if i + pair < group else None
-            shift = jnp.concatenate(shifts[i : i + pair], axis=0)
+            scores = ahead if early or i == 0 else scored(i)
+            if early and i + pair < group:
+                ahead = scored(i + pair)
+            shift = jnp.concatenate(shifts[i : i + pair], axis=0) * SCALE2
             probs = []
             for n, s in enumerate(scores):
-                if fresh and n > 0:
-                    x = s * SCALE2 - (shift + jnp.where(flags[n], 0.0, -LOW).astype(F32))
+                if fold:
+                    x = s * SCALE2
                 else:
-                    x = s * SCALE2 - shift
+                    x = s * SCALE2 - (shift - hidden[n])
                 if fresh and n == 0:
                     x = jnp.concatenate(
                         [jnp.where(causal, x[m * rows : (m + 1) * rows], LOW) for m in range(pair)], axis=0
@@ -404,14 +434,15 @@
                 else:
                     acc[:, cols] += summed
                     stat[...] += jnp.where(lane == group + g, total, 0.0)
-            scores = ahead
-
-    for n, distance in enumerate(distances):
-        here = slice((distance if last else n) * PLANE, ((distance if last else n) + 1) * PLANE)
-        if distance == 0:
-            attend(keys[here], values[here], True)
-        else:
-            pl.when(z_of(pos) >= distance)(functools.partial(attend, keys[here], values[here], False))
+
+    if first:
+        attend(keys, values, True, [0.0] + [jnp.where(shown(pos, r), 0.0, LOW).astype(F32) for r in rules[1:]])
+    elif len(set(rules)) == 1:
+        pl.when(shown(pos, rules[0]))(lambda: attend(keys, values, False, [0.0] * count))
+    else:
+        some = functools.reduce(jnp.logical_or, [shown(pos, r) for r in rules])
+        hidden = [jnp.where(shown(pos, r), 0.0, LOW).astype(F32) for r in rules]
+        pl.when(some)(lambda: attend(keys, values, False, hidden))
     if not last:
         return
     for g in range(group):
@@ -423,22 +454,30 @@
 
     @pl.when(fine < 0.5)
     def _():
+        head = begin + pl.program_id(0)
+        for n in range(len(all_rules)):
+            here = pl.ds(n * rows, rows)
+            pltpu.sync_copy(every[n].at[:, pl.ds(pl.multiple_of(head * HD, HD), HD)], key_all.at[here])
+            pltpu.sync_copy(
+                every[n].at[:, pl.ds(pl.multiple_of((kv_count + head) * HD, HD), HD)], value_all.at[here]
+            )
+
         def one(g, carry):
             cols = pl.ds(pl.multiple_of(g * HD, HD), HD)
             query = q_ref[:, cols]
             top = total = summed = None
-            for n in range(count):
-                x = mm_bt(query, keys[n][...]) * SCALE2
+            for n, rule in enumerate(all_rules):
+                here = slice(n * rows, (n + 1) * rows)
+                x = mm_bt(query, key_all[here, :]) * SCALE2
                 if n == 0:
                     x = jnp.where(causal, x, LOW)
                 else:
-                    shown = flags[n] if n < PLANE else z_of(pos) >= n // PLANE
-                    x = jnp.where(shown, x, LOW)
+                    x = jnp.where(shown(pos, rule), x, LOW)
                 high = jnp.max(x, axis=1, keepdims=True)
                 if n > 0:
                     high = jnp.maximum(high, top)
                 probs = jnp.exp2(x - high)
-                part = mm(probs.astype(BF16), values[n][...])
+                part = mm(probs.astype(BF16), value_all[here, :])
                 more = jnp.sum(probs, axis=1, keepdims=True)
                 if n > 0:
                     keep = jnp.exp2(top - high)
@@ -451,16 +490,17 @@
         lax.fori_loop(0, group, one, 0)
 
 
-def soft_step(pos, query, pieces, distances, state, into, span, kv_count, planes, last, token):
+def soft_step(pos, query, blocks, every, state, into, span, kv_count, last, token, form):
     rows, width = query.shape
     group = width // HD // kv_count
-    first = distances[0] == 0
+    used, rules = zip(*blocks)
+    used = list(used)
+    first = rules[0] == "own"
     begin, count = span
     block = pl.BlockSpec((rows, group * HD), lambda k: (0, begin + k))
     stat = pl.BlockSpec((1, rows, HD), lambda k: (begin + k, 0, 0))
     keys = pl.BlockSpec((rows, HD), lambda k: (0, begin + k))
     values = pl.BlockSpec((rows, HD), lambda k: (0, kv_count + begin + k))
-    used = [a for d in (range(planes) if last else distances) for a in pieces[d]]
     in_specs = [SCALAR, block] + [keys] * len(used) + [values] * len(used)
     operands = [pos, query] + used + used
     aliases = {}
@@ -469,19 +509,20 @@
             aliases = {len(operands): 0, len(operands) + 1: 1}
         in_specs += [block, stat]
         operands += list(state)
-    passed = 1
     in_specs.append(SCALAR)
     operands.append(token)
+    rest = [a for a, _ in every] if last else []
     if into is not None:
-        passed += len(into)
         for i, a in enumerate(into):
-            aliases[len(operands)] = i
-            in_specs.append(ANY)
-            operands.append(a)
+            aliases[len(operands) + len(rest) + i] = i
+        rest = rest + list(into)
+    in_specs += [ANY] * len(rest)
+    operands += rest
     if last:
         out_specs = [block, SCALAR]
         out_shape = [jax.ShapeDtypeStruct((rows, width), BF16), NEXT]
         scratch = [pltpu.VMEM((rows, group * HD), F32), pltpu.VMEM((rows, HD), F32)]
+        scratch += [pltpu.VMEM((len(every) * rows, HD), BF16)] * 2
     else:
         out_specs = [block, stat, SCALAR]
         out_shape = [
@@ -492,7 +533,15 @@
         scratch = []
     return pl.pallas_call(
         functools.partial(
-            soft_kernel, group=group, distances=distances, planes=planes, last=last, passed=passed
+            soft_kernel,
+            group=group,
+            rules=rules,
+            all_rules=[rule for _, rule in every],
+            last=last,
+            passed=1 + len(rest),
+            kv_count=kv_count,
+            begin=begin,
+            form=form,
         ),
         grid=(count,),
         in_specs=in_specs,
@@ -540,75 +589,69 @@
     def after(a, token):
         return lax.optimization_barrier((a, token))[0]
 
-    paired = jnp.concatenate([soft_key, soft_value], axis=1)
-    crossed = over_x(paired)
-    arrived = [paired, over_z(paired, 1)]
-
-    def forward(token):
-        arrived.append(over_z(after(arrived[-1], token), 1))
-
-    pieces = [[paired, crossed, over_core(paired), over_core(crossed)]]
-
     half = max(kv_count // 2, 1)
     spans = [(0, half), (half, kv_count - half)] if kv_count > 1 else [(0, 1)]
-
-    def soft(distances, state, last, token, span=None, into=None):
+    every = []
+
+    def soft(blocks, state, token, form, span=None, last=False, into=None):
+        if not any(a is blocks[0][0] for a, _ in every):
+            every.extend(blocks)
         *state, token = soft_step(
-            pos, soft_query, pieces, distances, state, into, span or (0, kv_count), kv_count, planes, last, token
+            pos, soft_query, blocks, every, state, into, span or (0, kv_count), kv_count, last, token, form
         )
         return state, token
 
+    def pair(a, rule, token):
+        return [(a, rule), (over_core(after(a, token)), rule)]
+
+    paired = jnp.concatenate([soft_key, soft_value], axis=1)
+    own = [(paired, "own"), (over_core(paired), "core")]
+    beside = over_x(paired)
+    same = over_z(paired, 1)
+
     send, keep, cum, cumt, token = local_state(
-        pos, light_key, light_value, after(log_decay.T, pieces[0][2])
+        pos, light_key, light_value, after(log_decay.T, own[1][0])
     )
     other = over_core(send)
     quarter = (length, HD)
-
-    def cross(d, token):
-        a = after(arrived[d], token)
-        pieces.append([a, over_x(a)])
-
-    def spread_core(d, token):
-        pieces[d] += [over_core(after(a, token)) for a in pieces[d]]
-
-    cross(1, token)
-    forward(token)
-    state, token = soft((0,), None, False, token, spans[0])
+    both = (2, qh * HD, HD)
+
+    state, token = soft(own, None, token, FORMS[0])
+    blocks = pair(beside, "x", token) + pair(same, 1, token)
+    ahead = over_z(after(same, token), 1)
+    beside = over_x(after(same, token))
+    state, token = soft(blocks, state, token, FORMS[1], spans[0])
     chip_send, chip_keep, token = small(chip_kernel, pos, [keep, other], [quarter, quarter], qh, "chip", token)
     chip_other = over_x(chip_send)
-    cross(2, token)
-    forward(token)
     if len(spans) > 1:
-        state, token = soft((0,), None, False, token, spans[1], state)
+        state, token = soft(blocks, state, token, FORMS[1], spans[1])
     plane, token = small(plane_kernel, pos, [chip_keep, chip_other], [quarter], qh, "plane", token)
     earlier = [over_z(plane, d) for d in range(1, planes)]
-    spread_core(1, token)
-    spread_core(2, token)
-    cross(3, token)
-    for d in range(3, planes - 1):
-        forward(token)
-        cross(d + 1, token)
-    both = (2, qh * HD, HD)
-    rest = (planes - 1,)
-    for middle in [(1, 2)] + [(d,) for d in range(3, planes - 1)]:
-        for n, span in enumerate(spans):
-            state, token = soft(middle, state, False, token, span)
-            if n == 0:
-                spread_core(middle[-1] + 1, token)
+    for d in range(1, planes - 1):
+        same = ahead
+        blocks = pair(beside, d, token) + pair(same, d + 1, token)
+        if d < planes - 2:
+            beside = over_x(after(same, token))
+            ahead = over_z(after(same, token), 1)
+            for span in spans:
+                state, token = soft(blocks, state, token, FORMS[2], span)
     enter_send, enter_keep, token = small(
         enter_kernel, pos, [chip_keep, chip_other] + earlier, [quarter, quarter], qh, "enter", token
     )
     enter_other = over_x(enter_send)
-    soft_out, token = soft(rest, state, True, token, spans[0])
+    state, token = soft(blocks, state, token, FORMS[3], spans[0])
+    beside = over_x(after(same, token))
     state_send, state_keep, token = small(
         core_kernel, pos, [enter_keep, enter_other, keep, other], [both, both], qh, "core", token
     )
     state_other = over_core(state_send)
-    for span in spans[1:]:
-        soft_out, token = soft(rest, state, True, token, span, soft_out)
+    if len(spans) > 1:
+        state, token = soft(blocks, state, token, FORMS[4], spans[1])
+    blocks = pair(beside, planes - 1, token)
     raw, square, token = light(
         pos, light_query, light_key, light_value, cum, cumt, state_keep, state_other, token
     )
+    soft_out, token = soft(blocks, state, token, FORMS[5], None, True)
     squares = [square]
     step = 1
     while step < tp:

time: 124 us -> 146 us (1.18)
  waiting for transfers between devices: 17.4 us -> 36.9 us
  Pallas kernels: 77.3 us -> 83.2 us
  local copies, waits for them, and re-layouts: 5.91 us -> 3.82 us
  starting transfers between devices: 21.5 us -> 19.9 us
    ppermute x6, waiting for transfers between devices: 4.07 us -> 19.4 us  [over_z(): lax.ppermute(a, 'ctx', [(i, i + PLANE * d) for i in range(ctx - PLANE * d)])]
    ppermute x6, waiting for transfers between devices: 9.45 us -> 17.4 us  [over_x(): return lax.ppermute(a, 'ctx', [(i, i ^ 2) for i in range(ctx)])]
    ppermute x1, waiting for transfers between devices: 3.83 us -> 0.01 us  [local(): lax.ppermute(square, 'tp', [(i, i ^ step) for i in range(tp)])]
    pallas_call x6 -> x8, Pallas kernels: 57 us -> 60.8 us  [soft_step(): pl.pallas_call(functools.partial(soft_kernel, group=group, rules=rules, a...]
    unnamed x17 -> x25, local copies, waits for them, and re-layouts: 4.93 us -> 2.85 us
    pallas_call x1, Pallas kernels: 5.12 us -> 7.13 us  [local_state(): pl.pallas_call(functools.partial(state_kernel, qh=qh, heads=heads), grid_...]
    ppermute x10, starting transfers between devices: 7.24 us -> 5.26 us  [over_core(): return lax.ppermute(a, 'ctx', [(i, i ^ 1) for i in range(ctx)])]
  transfers between devices with their start and end apart: 23 -> 23, of which waited for: 5 -> 4; matrix products, arithmetic and copies ran while one was open for 0% -> 0% of each run, Pallas kernels for 53% -> 50%
where the time goes in v4:
time: 146 us; the launch traced here: 145 us
  Pallas kernels  83.2 us (57%)
  waiting for transfers between devices  36.9 us (25%)
  starting transfers between devices  19.9 us (14%)
  local copies, waits for them, and re-layouts  3.82 us (3%)
    pallas_call x8, Pallas kernels, soft_step(): pl.pallas_call(functools.partial(soft_kernel, group=group, rules=rules, a...  60.8 us
    ppermute x6, waiting for transfers between devices, over_z(): lax.ppermute(a, 'ctx', [(i, i + PLANE * d) for i in range(ctx - PLANE * d)])  19.4 us
    ppermute x6, waiting for transfers between devices, over_x(): return lax.ppermute(a, 'ctx', [(i, i ^ 2) for i in range(ctx)])  17.4 us
    ppermute x6, starting transfers between devices, over_z(): lax.ppermute(a, 'ctx', [(i, i + PLANE * d) for i in range(ctx - PLANE * d)])  8.11 us
    pallas_call x1, Pallas kernels, local_state(): pl.pallas_call(functools.partial(state_kernel, qh=qh, heads=heads), grid_...  7.13 us
    pallas_call x1, Pallas kernels, light(): pl.pallas_call(functools.partial(light_kernel, qh=wide // HD), grid=(4,),...  6.71 us
    ppermute x10, starting transfers between devices, over_core(): return lax.ppermute(a, 'ctx', [(i, i ^ 1) for i in range(ctx)])  5.26 us
    ppermute x6, starting transfers between devices, over_x(): return lax.ppermute(a, 'ctx', [(i, i ^ 2) for i in range(ctx)])  5.19 us
  transfers between devices with their start and end apart: 23, of which 4 were waited for; matrix products, arithmetic and copies ran while one was open for 0% of the time, Pallas kernels for 50%

profile of v4, /device:TPU:27, one launch (start us, length us, event | category | flops | bytes accessed | tf_op | source)
XLA Modules:
  0.0 144.7 jit_solution(7639387453896132095)
XLA Ops:
  3.6 1.3 collective-permute-start.1
  5.7 7.1 %local_state.1 = (bf16[2,1040,128]{2,1,0:T(8,128)(2,1)}, bf16[2,1040,128]{2,1,0:T(8,128)(2,1)}, f32[4,256,128]{2,1,0:T(8,128)}, f32[4,8,256]{2,1,0:T(8,128)}, s32[1]{0:T(128)}) custom-call(s32[1]{0:T(128)} %bitcast.pos, bf16[256,4096]{1,0:T(8,128)(2,1)} %k_ref.3, bf16[256,4096]{1,0:T(8,128)(2,1)} %v_ref.3, f32[32,256]{1,0:T(8,128)} %bitcast.4), custom_call_target="tpu_custom_call" | custom-call | flops 1000 | bytes 1048576 | tf_op jit(solution)/shard_map/local_state/pallas_call | solution.py:126
  14.3 8.1 %softmax.8 = (f32[256,4096]{1,0:T(8,128)S(1)}, f32[4,256,128]{2,1,0:T(8,128)S(1)}, s32[1]{0:T(128)}) custom-call(s32[1]{0:T(128)} %bitcast.pos, bf16[256,4096]{1,0:T(8,128)(2,1)S(1)} %copy-done, bf16[256,1024]{1,0:T(8,128)(2,1)S(1)} %constant_dynamic-update-slice_fusion.refs_0_.refs_2_.refs_7_, bf16[256,1024]{1,0:T(8,128)(2,1)S(1)} %copy-done.4, ...), custom_call_target="tpu_custom_call" | custom-call | flops 1000 | bytes 1048576 | tf_op jit(solution)/shard_map/softmax/pallas_call | solution.py:534
  24.2 1.3 collective-permute-start.2
  25.5 7.0 %softmax.9 = (f32[256,4096]{1,0:T(8,128)S(1)}, f32[4,256,128]{2,1,0:T(8,128)S(1)}, s32[1]{0:T(128)}) custom-call(s32[1]{0:T(128)} %bitcast.pos, bf16[256,4096]{1,0:T(8,128)(2,1)S(1)} %copy-done, bf16[256,1024]{1,0:T(8,128)(2,1)S(1)} %collective-permute-done.3.refs_0_.refs_4_.refs_9_, ...), custom_call_target="tpu_custom_call", output_to_operand_aliasing={{0}: (10, {}), {1}: (11, {})} | custom-call | flops 1000 | bytes 1048576 | tf_op jit(solution)/shard_map/softmax/pallas_call | solution.py:534
  32.5 1.3 chip.1
  34.8 7.0 %softmax.10 = (f32[256,4096]{1,0:T(8,128)S(1)}, f32[4,256,128]{2,1,0:T(8,128)S(1)}, s32[1]{0:T(128)}) custom-call(s32[1]{0:T(128)} %bitcast.pos, bf16[256,4096]{1,0:T(8,128)(2,1)S(1)} %copy-done, bf16[256,1024]{1,0:T(8,128)(2,1)S(1)} %collective-permute-done.3.refs_0_.refs_4_.refs_9_, ...), custom_call_target="tpu_custom_call", output_to_operand_aliasing={{0}: (10, {}), {1}: (11, {})} | custom-call | flops 1000 | bytes 1048576 | tf_op jit(solution)/shard_map/softmax/pallas_call | solution.py:534
  44.4 1.5 %collective-permute-start.13 = (bf16[256,1024]{1,0:T(8,128)(2,1)S(1)}, bf16[256,1024]{1,0:T(8,128)(2,1)S(1)}, u32[]{:S(2)}, u32[]{:S(2)}) collective-permute-start(bf16[256,1024]{1,0:T(8,128)(2,1)S(1)} %collective-permute-done.2.refs_2_.refs_6_.refs_15_), channel_id=1, source_target_pairs={{0,8},{2,10},{4,12},{6,14},{8,16},{10,18},{12,20},{14,22},{16,24},... | collective-permute-start | bytes 1572872 | tf_op jit(solution)/shard_map/ppermute | solution.py:587
  45.9 1.3 collective-permute-start.8
  47.2 7.1 %softmax.11 = (f32[256,4096]{1,0:T(8,128)S(1)}, f32[4,256,128]{2,1,0:T(8,128)S(1)}, s32[1]{0:T(128)}) custom-call(s32[1]{0:T(128)} %bitcast.pos, bf16[256,4096]{1,0:T(8,128)(2,1)S(1)} %copy-done, bf16[256,1024]{1,0:T(8,128)(2,1)S(1)} %collective-permute-done.9.refs_0_.refs_4_.refs_13_, ...), custom_call_target="tpu_custom_call", output_to_operand_aliasing={{0}: (10, {}), {1}: (11, {})} | custom-call | flops 1000 | bytes 1048576 | tf_op jit(solution)/shard_map/softmax/pallas_call | solution.py:534
  54.3 7.1 %softmax.12 = (f32[256,4096]{1,0:T(8,128)S(1)}, f32[4,256,128]{2,1,0:T(8,128)S(1)}, s32[1]{0:T(128)}) custom-call(s32[1]{0:T(128)} %bitcast.pos, bf16[256,4096]{1,0:T(8,128)(2,1)S(1)} %copy-done, bf16[256,1024]{1,0:T(8,128)(2,1)S(1)} %collective-permute-done.9.refs_0_.refs_4_.refs_13_, ...), custom_call_target="tpu_custom_call", output_to_operand_aliasing={{0}: (10, {}), {1}: (11, {})} | custom-call | flops 1000 | bytes 1048576 | tf_op jit(solution)/shard_map/softmax/pallas_call | solution.py:534
  62.3 1.3 collective-permute-start.17
  63.6 1.3 collective-permute-start.16
  64.9 1.5 %collective-permute-start.15 = (bf16[1040,128]{1,0:T(8,128)(2,1)S(1)}, bf16[1040,128]{1,0:T(8,128)(2,1)S(1)}, u32[]{:S(2)}, u32[]{:S(2)}) collective-permute-start(bf16[1040,128]{1,0:T(8,128)(2,1)S(1)} %get-tuple-element.84), channel_id=1, source_target_pairs={{0,8},{2,10},{4,12},{6,14},{8,16},{10,18},{12,20},{14,22},{16,24},... | collective-permute-start | bytes 798728 | tf_op jit(solution)/shard_map/ppermute | solution.py:587
  66.4 7.2 %collective-permute-done.17.refs_4_ = bf16[1040,128]{1,0:T(8,128)(2,1)S(1)} collective-permute-done((bf16[1040,128]{1,0:T(8,128)(2,1)S(1)}, bf16[1040,128]{1,0:T(8,128)(2,1)S(1)}, u32[]{:S(2)}, u32[]{:S(2)}) %collective-permute-start.17) | collective-permute-done | bytes 266272 | tf_op jit(solution)/shard_map/ppermute | solution.py:587
  73.6 12.2 %collective-permute-done.16.refs_3_ = bf16[1040,128]{1,0:T(8,128)(2,1)S(1)} collective-permute-done((bf16[1040,128]{1,0:T(8,128)(2,1)S(1)}, bf16[1040,128]{1,0:T(8,128)(2,1)S(1)}, u32[]{:S(2)}, u32[]{:S(2)}) %collective-permute-start.16) | collective-permute-done | bytes 266272 | tf_op jit(solution)/shard_map/ppermute | solution.py:587
  87.1 7.1 %softmax.13 = (f32[256,4096]{1,0:T(8,128)S(1)}, f32[4,256,128]{2,1,0:T(8,128)S(1)}, s32[1]{0:T(128)}) custom-call(s32[1]{0:T(128)} %bitcast.pos, bf16[256,4096]{1,0:T(8,128)(2,1)S(1)} %copy-done, bf16[256,1024]{1,0:T(8,128)(2,1)S(1)} %collective-permute-done.8.refs_0_.refs_4_.refs_17_, ...), custom_call_target="tpu_custom_call", output_to_operand_aliasing={{0}: (10, {}), {1}: (11, {})} | custom-call | flops 1000 | bytes 1048576 | tf_op jit(solution)/shard_map/softmax/pallas_call | solution.py:534
  95.7 17.2 %collective-permute-done.18.refs_1_ = bf16[1040,128]{1,0:T(8,128)(2,1)S(1)} collective-permute-done((bf16[1040,128]{1,0:T(8,128)(2,1)S(1)}, bf16[1040,128]{1,0:T(8,128)(2,1)S(1)}, u32[]{:S(2)}, u32[]{:S(2)}) %collective-permute-start.18) | collective-permute-done | bytes 266272 | tf_op jit(solution)/shard_map/ppermute | solution.py:584
  114.1 1.4 collective-permute-start.19
  115.6 7.2 %softmax.14 = (f32[256,4096]{1,0:T(8,128)S(1)}, f32[4,256,128]{2,1,0:T(8,128)S(1)}, s32[1]{0:T(128)}) custom-call(s32[1]{0:T(128)} %bitcast.pos, bf16[256,4096]{1,0:T(8,128)(2,1)S(1)} %copy-done, bf16[256,1024]{1,0:T(8,128)(2,1)S(1)} %collective-permute-done.8.refs_0_.refs_4_.refs_17_, ...), custom_call_target="tpu_custom_call", output_to_operand_aliasing={{0}: (10, {}), {1}: (11, {})} | custom-call | flops 1000 | bytes 1048576 | tf_op jit(solution)/shard_map/softmax/pallas_call | solution.py:534
  123.0 6.7 %light.1 = (bf16[256,4096]{1,0:T(8,128)(2,1)S(1)}, f32[256,128]{1,0:T(8,128)S(1)}, s32[1]{0:T(128)}) custom-call(s32[1]{0:T(128)} %bitcast.pos, bf16[256,4096]{1,0:T(8,128)(2,1)S(1)} %copy-done.8, bf16[256,4096]{1,0:T(8,128)(2,1)S(1)} %copy-done.1, bf16[256,4096]{1,0:T(8,128)(2,1)S(1)} %copy-done.2, f32[4,256,128]{2,1,0:T(8,128)S(1)} %copy-done.9, ...), custom_call_target="tpu_custom_call" | custom-call | flops 1000 | bytes 1048576 | tf_op jit(solution)/shard_map/light/pallas_call | solution.py:283
  129.7 1.3 collective-permute-start.20
  131.0 10.1 %softmax.15 = (bf16[256,4096]{1,0:T(8,128)(2,1)}, s32[1]{0:T(128)}) custom-call(s32[1]{0:T(128)} %bitcast.pos, bf16[256,4096]{1,0:T(8,128)(2,1)S(1)} %copy-done, bf16[256,1024]{1,0:T(8,128)(2,1)S(1)} %collective-permute-done.21.refs_0_.refs_2_.refs_21_, bf16[256,1024]{1,0:T(8,128)(2,1)S(1)} %collective-permute-done.22.refs_1_.refs_3_.refs_22_, ...), custom_call_target="tpu_custom_call" | custom-call | flops 1000 | bytes 1048576 | tf_op jit(solution)/shard_map/softmax/pallas_call | solution.py:534
  141.2 3.6 %finish.1 = bf16[256,4096]{1,0:T(8,128)(2,1)} custom-call(bf16[256,4096]{1,0:T(8,128)(2,1)S(1)} %get-tuple-element.95.raw_ref, f32[256,128]{1,0:T(8,128)S(1)} %get-tuple-element.96.refs_0_, f32[256,128]{1,0:T(8,128)S(1)} %collective-permute-done.20.refs_1_, f32[1,4096]{1,0:T(1,128)S(1)} %bitcast.3, bf16[256,4096]{1,0:T(8,128)(2,1)S(1)} %copy-done.7, ...), custom_call_target="tpu_custom_call" | custom-call | flops 1000 | bytes 1048576 | tf_op jit(solution)/shard_map/finish/pallas_call | solution.py:327
  (63 shorter events, 15.5 us)
Async XLA Ops:
  2.6 2.3 %collective-permute-start = (bf16[256,1024]{1,0:T(8,128)(2,1)S(1)}, bf16[256,1024]{1,0:T(8,128)(2,1)S(1)}, u32[]{:S(2)}, u32[]{:S(2)}) collective-permute-start(bf16[256,1024]{1,0:T(8,128)(2,1)S(1)} %constant_dynamic-update-slice_fusion.refs_0_.refs_2_.refs_7_), channel_id=1, source_target_pairs={{0,2},{2,0},{4,6},{6,4},{8,10},{10,8},{12,14},{14,12},{16,18},{18,... | collective-permute-start | bytes 1572872 | tf_op jit(solution)/shard_map/ppermute | solution.py:581
  3.3 19.1 %collective-permute-start.3 = (bf16[256,1024]{1,0:T(8,128)(2,1)S(1)}, bf16[256,1024]{1,0:T(8,128)(2,1)S(1)}, u32[]{:S(2)}, u32[]{:S(2)}) collective-permute-start(bf16[256,1024]{1,0:T(8,128)(2,1)S(1)} %constant_dynamic-update-slice_fusion.refs_0_.refs_2_.refs_7_), channel_id=1, source_target_pairs={{0,4},{2,6},{4,0},{6,2},{8,12},{10,14},{12,8},{14,10},{16,20},{18,... | collective-permute-start | bytes 1572872 | tf_op jit(solution)/shard_map/ppermute | solution.py:584
  3.6 18.8 %collective-permute-start.1 = (bf16[256,1024]{1,0:T(8,128)(2,1)S(1)}, bf16[256,1024]{1,0:T(8,128)(2,1)S(1)}, u32[]{:S(2)}, u32[]{:S(2)}) collective-permute-start(bf16[256,1024]{1,0:T(8,128)(2,1)S(1)} %constant_dynamic-update-slice_fusion.refs_0_.refs_2_.refs_7_), channel_id=1, source_target_pairs={{0,8},{2,10},{4,12},{6,14},{8,16},{10,18},{12,20},{14,22},{16,24},... | collective-permute-start | bytes 1572872 | tf_op jit(solution)/shard_map/ppermute | solution.py:587
  12.8 19.7 %collective-permute-start.6 = (bf16[2,1040,128]{2,1,0:T(8,128)(2,1)}, bf16[2,1040,128]{2,1,0:T(8,128)(2,1)S(1)}, u32[]{:S(2)}, u32[]{:S(2)}) collective-permute-start(bf16[2,1040,128]{2,1,0:T(8,128)(2,1)} %get-tuple-element.66), channel_id=1, source_target_pairs={{0,2},{2,0},{4,6},{6,4},{8,10},{10,8},{12,14},{14,12},{16,18},{18,... | collective-permute-start | bytes 1597448 | tf_op jit(solution)/shard_map/ppermute | solution.py:581
  22.4 3.1 %collective-permute-start.5 = (bf16[256,1024]{1,0:T(8,128)(2,1)S(1)}, bf16[256,1024]{1,0:T(8,128)(2,1)S(1)}, u32[]{:S(2)}, u32[]{:S(2)}) collective-permute-start(bf16[256,1024]{1,0:T(8,128)(2,1)S(1)} %collective-permute-done.1.refs_2_.refs_6_.refs_11_), channel_id=1, source_target_pairs={{0,2},{2,0},{4,6},{6,4},{8,10},{10,8},{12,14},{14,12},{16,18},{18,... | collective-permute-start | bytes 1572872 | tf_op jit(solution)/shard_map/ppermute | solution.py:581
  22.6 2.9 %collective-permute-start.4 = (bf16[256,1024]{1,0:T(8,128)(2,1)S(1)}, bf16[256,1024]{1,0:T(8,128)(2,1)S(1)}, u32[]{:S(2)}, u32[]{:S(2)}) collective-permute-start(bf16[256,1024]{1,0:T(8,128)(2,1)S(1)} %collective-permute-done.3.refs_0_.refs_4_.refs_9_), channel_id=1, source_target_pairs={{0,2},{2,0},{4,6},{6,4},{8,10},{10,8},{12,14},{14,12},{16,18},{18,... | collective-permute-start | bytes 1572872 | tf_op jit(solution)/shard_map/ppermute | solution.py:581
  23.0 20.3 %collective-permute-start.9 = (bf16[256,1024]{1,0:T(8,128)(2,1)S(1)}, bf16[256,1024]{1,0:T(8,128)(2,1)S(1)}, u32[]{:S(2)}, u32[]{:S(2)}) collective-permute-start(bf16[256,1024]{1,0:T(8,128)(2,1)S(1)} %collective-permute-done.1.refs_2_.refs_6_.refs_11_), channel_id=1, source_target_pairs={{0,4},{2,6},{4,0},{6,2},{8,12},{10,14},{12,8},{14,10},{16,20},{18,... | collective-permute-start | bytes 1572872 | tf_op jit(solution)/shard_map/ppermute | solution.py:584
  24.2 19.1 %collective-permute-start.2 = (bf16[256,1024]{1,0:T(8,128)(2,1)S(1)}, bf16[256,1024]{1,0:T(8,128)(2,1)S(1)}, u32[]{:S(2)}, u32[]{:S(2)}) collective-permute-start(bf16[256,1024]{1,0:T(8,128)(2,1)S(1)} %collective-permute-done.1.refs_2_.refs_6_.refs_11_), channel_id=1, source_target_pairs={{0,8},{2,10},{4,12},{6,14},{8,16},{10,18},{12,20},{14,22},{16,24},... | collective-permute-start | bytes 1572872 | tf_op jit(solution)/shard_map/ppermute | solution.py:587
  33.9 8.2 %collective-permute-start.7 = (bf16[1040,128]{1,0:T(8,128)(2,1)S(1)}, bf16[1040,128]{1,0:T(8,128)(2,1)S(1)}, u32[]{:S(2)}, u32[]{:S(2)}) collective-permute-start(bf16[1040,128]{1,0:T(8,128)(2,1)S(1)} %get-tuple-element.70), channel_id=1, source_target_pairs={{0,4},{2,6},{4,0},{6,2},{8,12},{10,14},{12,8},{14,10},{16,20},{18,... | collective-permute-start | bytes 798728 | tf_op jit(solution)/shard_map/ppermute | solution.py:584
  43.3 3.9 %collective-permute-start.11 = (bf16[256,1024]{1,0:T(8,128)(2,1)S(1)}, bf16[256,1024]{1,0:T(8,128)(2,1)S(1)}, u32[]{:S(2)}, u32[]{:S(2)}) collective-permute-start(bf16[256,1024]{1,0:T(8,128)(2,1)S(1)} %collective-permute-done.2.refs_2_.refs_6_.refs_15_), channel_id=1, source_target_pairs={{0,2},{2,0},{4,6},{6,4},{8,10},{10,8},{12,14},{14,12},{16,18},{18,... | collective-permute-start | bytes 1572872 | tf_op jit(solution)/shard_map/ppermute | solution.py:581
  44.3 2.8 %collective-permute-start.10 = (bf16[256,1024]{1,0:T(8,128)(2,1)S(1)}, bf16[256,1024]{1,0:T(8,128)(2,1)S(1)}, u32[]{:S(2)}, u32[]{:S(2)}) collective-permute-start(bf16[256,1024]{1,0:T(8,128)(2,1)S(1)} %collective-permute-done.9.refs_0_.refs_4_.refs_13_), channel_id=1, source_target_pairs={{0,2},{2,0},{4,6},{6,4},{8,10},{10,8},{12,14},{14,12},{16,18},{18,... | collective-permute-start | bytes 1572872 | tf_op jit(solution)/shard_map/ppermute | solution.py:581
  44.4 17.0 %collective-permute-start.13 = (bf16[256,1024]{1,0:T(8,128)(2,1)S(1)}, bf16[256,1024]{1,0:T(8,128)(2,1)S(1)}, u32[]{:S(2)}, u32[]{:S(2)}) collective-permute-start(bf16[256,1024]{1,0:T(8,128)(2,1)S(1)} %collective-permute-done.2.refs_2_.refs_6_.refs_15_), channel_id=1, source_target_pairs={{0,8},{2,10},{4,12},{6,14},{8,16},{10,18},{12,20},{14,22},{16,24},... | collective-permute-start | bytes 1572872 | tf_op jit(solution)/shard_map/ppermute | solution.py:587
  45.9 15.6 %collective-permute-start.8 = (bf16[256,1024]{1,0:T(8,128)(2,1)S(1)}, bf16[256,1024]{1,0:T(8,128)(2,1)S(1)}, u32[]{:S(2)}, u32[]{:S(2)}) collective-permute-start(bf16[256,1024]{1,0:T(8,128)(2,1)S(1)} %collective-permute-done.2.refs_2_.refs_6_.refs_15_), channel_id=1, source_target_pairs={{0,4},{2,6},{4,0},{6,2},{8,12},{10,14},{12,8},{14,10},{16,20},{18,... | collective-permute-start | bytes 1572872 | tf_op jit(solution)/shard_map/ppermute | solution.py:584
  61.5 25.6 %collective-permute-start.12 = (bf16[256,1024]{1,0:T(8,128)(2,1)S(1)}, bf16[256,1024]{1,0:T(8,128)(2,1)S(1)}, u32[]{:S(2)}, u32[]{:S(2)}) collective-permute-start(bf16[256,1024]{1,0:T(8,128)(2,1)S(1)} %collective-permute-done.8.refs_0_.refs_4_.refs_17_), channel_id=1, source_target_pairs={{0,2},{2,0},{4,6},{6,4},{8,10},{10,8},{12,14},{14,12},{16,18},{18,... | collective-permute-start | bytes 1572872 | tf_op jit(solution)/shard_map/ppermute | solution.py:581
  62.3 24.8 %collective-permute-start.14 = (bf16[256,1024]{1,0:T(8,128)(2,1)S(1)}, bf16[256,1024]{1,0:T(8,128)(2,1)S(1)}, u32[]{:S(2)}, u32[]{:S(2)}) collective-permute-start(bf16[256,1024]{1,0:T(8,128)(2,1)S(1)} %collective-permute-done.13.refs_2_.refs_6_.refs_19_), channel_id=1, source_target_pairs={{0,2},{2,0},{4,6},{6,4},{8,10},{10,8},{12,14},{14,12},{16,18},{18,... | collective-permute-start | bytes 1572872 | tf_op jit(solution)/shard_map/ppermute | solution.py:581
  62.3 11.3 %collective-permute-start.17 = (bf16[1040,128]{1,0:T(8,128)(2,1)S(1)}, bf16[1040,128]{1,0:T(8,128)(2,1)S(1)}, u32[]{:S(2)}, u32[]{:S(2)}) collective-permute-start(bf16[1040,128]{1,0:T(8,128)(2,1)S(1)} %get-tuple-element.84), channel_id=1, source_target_pairs={{0,24},{2,26},{4,28},{6,30},{1,25},{3,27},{5,29},{7,31}} | collective-permute-start | bytes 798728 | tf_op jit(solution)/shard_map/ppermute | solution.py:587
  63.6 22.2 %collective-permute-start.16 = (bf16[1040,128]{1,0:T(8,128)(2,1)S(1)}, bf16[1040,128]{1,0:T(8,128)(2,1)S(1)}, u32[]{:S(2)}, u32[]{:S(2)}) collective-permute-start(bf16[1040,128]{1,0:T(8,128)(2,1)S(1)} %get-tuple-element.84), channel_id=1, source_target_pairs={{0,16},{2,18},{4,20},{6,22},{8,24},{10,26},{12,28},{14,30},{1,17},... | collective-permute-start | bytes 798728 | tf_op jit(solution)/shard_map/ppermute | solution.py:587
  64.9 20.9 %collective-permute-start.15 = (bf16[1040,128]{1,0:T(8,128)(2,1)S(1)}, bf16[1040,128]{1,0:T(8,128)(2,1)S(1)}, u32[]{:S(2)}, u32[]{:S(2)}) collective-permute-start(bf16[1040,128]{1,0:T(8,128)(2,1)S(1)} %get-tuple-element.84), channel_id=1, source_target_pairs={{0,8},{2,10},{4,12},{6,14},{8,16},{10,18},{12,20},{14,22},{16,24},... | collective-permute-start | bytes 798728 | tf_op jit(solution)/shard_map/ppermute | solution.py:587
  94.1 28.7 %collective-permute-start.21 = (bf16[256,1024]{1,0:T(8,128)(2,1)S(1)}, bf16[256,1024]{1,0:T(8,128)(2,1)S(1)}, u32[]{:S(2)}, u32[]{:S(2)}) collective-permute-start(bf16[256,1024]{1,0:T(8,128)(2,1)S(1)} %collective-permute-done.13.refs_2_.refs_6_.refs_19_), channel_id=1, source_target_pairs={{0,4},{2,6},{4,0},{6,2},{8,12},{10,14},{12,8},{14,10},{16,20},{18,... | collective-permute-start | bytes 1572872 | tf_op jit(solution)/shard_map/ppermute | solution.py:584
  94.6 18.2 %collective-permute-start.18 = (bf16[1040,128]{1,0:T(8,128)(2,1)S(1)}, bf16[1040,128]{1,0:T(8,128)(2,1)S(1)}, u32[]{:S(2)}, u32[]{:S(2)}) collective-permute-start(bf16[1040,128]{1,0:T(8,128)(2,1)S(1)} %get-tuple-element.88), channel_id=1, source_target_pairs={{0,4},{2,6},{4,0},{6,2},{8,12},{10,14},{12,8},{14,10},{16,20},{18,... | collective-permute-start | bytes 798728 | tf_op jit(solution)/shard_map/ppermute | solution.py:584
  114.1 8.8 %collective-permute-start.19 = (bf16[2,1024,128]{2,1,0:T(8,128)(2,1)S(1)}, bf16[2,1024,128]{2,1,0:T(8,128)(2,1)S(1)}, u32[]{:S(2)}, u32[]{:S(2)}) collective-permute-start(bf16[2,1024,128]{2,1,0:T(8,128)(2,1)S(1)} %get-tuple-element.90), channel_id=1, source_target_pairs={{0,2},{2,0},{4,6},{6,4},{8,10},{10,8},{12,14},{14,12},{16,18},{18,... | collective-permute-start | bytes 1572872 | tf_op jit(solution)/shard_map/ppermute | solution.py:581
  122.8 8.2 %collective-permute-start.22 = (bf16[256,1024]{1,0:T(8,128)(2,1)S(1)}, bf16[256,1024]{1,0:T(8,128)(2,1)S(1)}, u32[]{:S(2)}, u32[]{:S(2)}) collective-permute-start(bf16[256,1024]{1,0:T(8,128)(2,1)S(1)} %collective-permute-done.21.refs_0_.refs_2_.refs_21_), channel_id=1, source_target_pairs={{0,2},{2,0},{4,6},{6,4},{8,10},{10,8},{12,14},{14,12},{16,18},{18,... | collective-permute-start | bytes 1572872 | tf_op jit(solution)/shard_map/ppermute | solution.py:581
  129.7 11.5 %collective-permute-start.20 = (f32[256,128]{1,0:T(8,128)S(1)}, f32[256,128]{1,0:T(8,128)S(1)}, u32[]{:S(2)}, u32[]{:S(2)}) collective-permute-start(f32[256,128]{1,0:T(8,128)S(1)} %get-tuple-element.96.refs_0_), channel_id=1, source_target_pairs={{0,1},{1,0},{2,3},{3,2},{4,5},{5,4},{6,7},{7,6},{8,9},{9,8},{10,11... | collective-permute-start | bytes 393224 | tf_op jit(solution)/shard_map/ppermute | solution.py:659
  131.0 10.2 %copy-start.11 = (f32[4096]{0:T(1024)S(1)}, f32[4096]{0:T(1024)}, u32[]{:S(2)}) copy-start(f32[4096]{0:T(1024)} %param.14) | copy-start | bytes 49156
  (11 other events, 71.5 us)

commit v5 on v3

--- a/solution.py
+++ b/solution.py
@@ -337,15 +337,16 @@
     )(raw, *squares, gain.reshape(1, width), gate, token)
 
 
-def soft_kernel(pos, q_ref, *refs, group, distances, planes, last, passed):
-    count = planes * PLANE if last else len(distances) * PLANE
+def soft_kernel(pos, q_ref, *refs, group, distances, planes, last, passed, kv_count, begin):
+    pair = min(2, group)
+    count = len(distances) * PLANE
     keys, values, refs = refs[:count], refs[count : 2 * count], refs[2 * count :]
     first = distances[0] == 0
     if not first:
         acc_in, stat_in, refs = refs[0], refs[1], refs[2:]
-    token, refs = refs[0], refs[passed:]
+    token, every, refs = refs[0], refs[1:passed], refs[passed:]
     if last:
-        out_ref, after, acc, stat = refs
+        out_ref, after, acc, stat, key_all, value_all = refs
     else:
         acc, stat, after = refs
         stat = stat.at[0]
@@ -353,7 +354,6 @@
     rows = q_ref.shape[0]
     lane = iota((rows, HD), 1)
     causal = iota((rows, rows), 0) >= iota((rows, rows), 1)
-    pair = min(group, 2)
     flags = [None, x_of(pos) == 1, core_of(pos) == 1, x_of(pos) == 1]
 
     if not first:
@@ -363,29 +363,33 @@
     def attend(keyed, valued, fresh):
         wide = jnp.concatenate([v[...] for v in valued], axis=0)
         wide = jnp.concatenate([wide, jnp.ones_like(wide)], axis=1)
+        keyed = [k[...] for k in keyed]
         if fresh:
-            own = keyed[0][...].astype(F32)
+            own = keyed[0].astype(F32)
             shifts = [
-                jnp.sum(q_ref[:, g * HD : (g + 1) * HD].astype(F32) * own, axis=1, keepdims=True) * SCALE2
+                jnp.sum(q_ref[:, g * HD : (g + 1) * HD].astype(F32) * own, axis=1, keepdims=True)
                 for g in range(group)
             ]
         else:
             shifts = [stat[:, g : g + 1] for g in range(group)]
-
+        hidden = [0.0] + [
+            jnp.where(flags[n], 0.0, LOW).astype(F32) if fresh else 0.0 for n in range(1, len(keyed))
+        ]
         def scored(i):
-            query = jnp.concatenate([q_ref[:, g * HD : (g + 1) * HD] for g in range(i, i + pair)], axis=0)
-            return [mm_bt(query, k[...]) for k in keyed]
+            parts = []
+            for g in range(i, i + pair):
+                query = q_ref[:, g * HD : (g + 1) * HD]
+                parts.append(query)
+            query = jnp.concatenate(parts, axis=0)
+            return [mm_bt(query, k) for k in keyed]
 
         scores = scored(0)
         for i in range(0, group, pair):
             ahead = scored(i + pair) if i + pair < group else None
-            shift = jnp.concatenate(shifts[i : i + pair], axis=0)
+            shift = jnp.concatenate(shifts[i : i + pair], axis=0) * SCALE2
             probs = []
             for n, s in enumerate(scores):
-                if fresh and n > 0:
-                    x = s * SCALE2 - (shift + jnp.where(flags[n], 0.0, -LOW).astype(F32))
-                else:
-                    x = s * SCALE2 - shift
+                x = s * SCALE2 - (shift - hidden[n])
                 if fresh and n == 0:
                     x = jnp.concatenate(
                         [jnp.where(causal, x[m * rows : (m + 1) * rows], LOW) for m in range(pair)], axis=0
@@ -407,44 +411,54 @@
             scores = ahead
 
     for n, distance in enumerate(distances):
-        here = slice((distance if last else n) * PLANE, ((distance if last else n) + 1) * PLANE)
+        here = slice(n * PLANE, (n + 1) * PLANE)
         if distance == 0:
             attend(keys[here], values[here], True)
         else:
             pl.when(z_of(pos) >= distance)(functools.partial(attend, keys[here], values[here], False))
     if not last:
         return
+    totals = (lane >= group) & (lane < 2 * group)
+    inverse = 1.0 / jnp.where(totals, stat[...], 1.0)
     for g in range(group):
         cols = slice(g * HD, (g + 1) * HD)
-        out_ref[:, cols] = (acc[:, cols] / stat[:, group + g : group + g + 1]).astype(BF16)
-
-    sums = jnp.where((lane >= group) & (lane < 2 * group), stat[...], 0.0)
+        out_ref[:, cols] = (acc[:, cols] * inverse[:, group + g : group + g + 1]).astype(BF16)
+
+    sums = jnp.where(totals, stat[...], 0.0)
     fine = jnp.min(jnp.where(sums < LIMIT, 1.0, 0.0))
 
     @pl.when(fine < 0.5)
     def _():
+        head = begin + pl.program_id(0)
+        for n in range(planes * PLANE):
+            here = pl.ds(n * rows, rows)
+            pltpu.sync_copy(every[n].at[:, pl.ds(pl.multiple_of(head * HD, HD), HD)], key_all.at[here])
+            pltpu.sync_copy(
+                every[n].at[:, pl.ds(pl.multiple_of((kv_count + head) * HD, HD), HD)], value_all.at[here]
+            )
+
         def one(g, carry):
             cols = pl.ds(pl.multiple_of(g * HD, HD), HD)
             query = q_ref[:, cols]
-            top = total = summed = None
-            for n in range(count):
-                x = mm_bt(query, keys[n][...]) * SCALE2
-                if n == 0:
-                    x = jnp.where(causal, x, LOW)
-                else:
-                    shown = flags[n] if n < PLANE else z_of(pos) >= n // PLANE
-                    x = jnp.where(shown, x, LOW)
-                high = jnp.max(x, axis=1, keepdims=True)
-                if n > 0:
-                    high = jnp.maximum(high, top)
+            x = jnp.where(causal, mm_bt(query, key_all[0:rows, :]) * SCALE2, LOW)
+            top = jnp.max(x, axis=1, keepdims=True)
+            probs = jnp.exp2(x - top)
+            total = jnp.sum(probs, axis=1, keepdims=True)
+            summed = mm(probs.astype(BF16), value_all[0:rows, :])
+
+            def more(n, sums):
+                top, total, summed = sums
+                here = pl.ds(pl.multiple_of(n * rows, rows), rows)
+                near = jnp.where(n == 2, core_of(pos), x_of(pos)) == 1
+                seen = jnp.where(n < PLANE, near, z_of(pos) >= n // PLANE)
+                x = jnp.where(seen, mm_bt(query, key_all[here, :]) * SCALE2, LOW)
+                high = jnp.maximum(jnp.max(x, axis=1, keepdims=True), top)
                 probs = jnp.exp2(x - high)
-                part = mm(probs.astype(BF16), values[n][...])
-                more = jnp.sum(probs, axis=1, keepdims=True)
-                if n > 0:
-                    keep = jnp.exp2(top - high)
-                    part = part + keep * summed
-                    more = more + keep * total
-                top, total, summed = high, more, part
+                keep = jnp.exp2(top - high)
+                part = mm(probs.astype(BF16), value_all[here, :])
+                return high, keep * total + jnp.sum(probs, axis=1, keepdims=True), keep * summed + part
+
+            top, total, summed = lax.fori_loop(1, planes * PLANE, more, (top, total, summed))
             out_ref[:, cols] = (summed / total).astype(BF16)
             return carry
 
@@ -460,7 +474,7 @@
     stat = pl.BlockSpec((1, rows, HD), lambda k: (begin + k, 0, 0))
     keys = pl.BlockSpec((rows, HD), lambda k: (0, begin + k))
     values = pl.BlockSpec((rows, HD), lambda k: (0, kv_count + begin + k))
-    used = [a for d in (range(planes) if last else distances) for a in pieces[d]]
+    used = [a for d in distances for a in pieces[d]]
     in_specs = [SCALAR, block] + [keys] * len(used) + [values] * len(used)
     operands = [pos, query] + used + used
     aliases = {}
@@ -469,19 +483,20 @@
             aliases = {len(operands): 0, len(operands) + 1: 1}
         in_specs += [block, stat]
         operands += list(state)
-    passed = 1
     in_specs.append(SCALAR)
     operands.append(token)
+    rest = [a for d in range(planes) for a in pieces[d]] if last else []
     if into is not None:
-        passed += len(into)
         for i, a in enumerate(into):
-            aliases[len(operands)] = i
-            in_specs.append(ANY)
-            operands.append(a)
+            aliases[len(operands) + len(rest) + i] = i
+        rest = rest + list(into)
+    in_specs += [ANY] * len(rest)
+    operands += rest
     if last:
         out_specs = [block, SCALAR]
         out_shape = [jax.ShapeDtypeStruct((rows, width), BF16), NEXT]
         scratch = [pltpu.VMEM((rows, group * HD), F32), pltpu.VMEM((rows, HD), F32)]
+        scratch += [pltpu.VMEM((planes * PLANE * rows, HD), BF16)] * 2
     else:
         out_specs = [block, stat, SCALAR]
         out_shape = [
@@ -492,7 +507,14 @@
         scratch = []
     return pl.pallas_call(
         functools.partial(
-            soft_kernel, group=group, distances=distances, planes=planes, last=last, passed=passed
+            soft_kernel,
+            group=group,
+            distances=distances,
+            planes=planes,
+            last=last,
+            passed=1 + len(rest),
+            kv_count=kv_count,
+            begin=begin,
         ),
         grid=(count,),
         in_specs=in_specs,
@@ -604,11 +626,11 @@
         core_kernel, pos, [enter_keep, enter_other, keep, other], [both, both], qh, "core", token
     )
     state_other = over_core(state_send)
-    for span in spans[1:]:
-        soft_out, token = soft(rest, state, True, token, span, soft_out)
     raw, square, token = light(
         pos, light_query, light_key, light_value, cum, cumt, state_keep, state_other, token
     )
+    for span in spans[1:]:
+        soft_out, token = soft(rest, state, True, token, span, soft_out)
     squares = [square]
     step = 1
     while step < tp:

time: 124 us -> 119 us (0.960)
  waiting for transfers between devices: 17.4 us -> 15.1 us
  Pallas kernels: 77.3 us -> 75 us
    ppermute x1, waiting for transfers between devices: 3.83 us -> 0.01 us  [local(): lax.ppermute(square, 'tp', [(i, i ^ step) for i in range(tp)])]
    pallas_call x6, Pallas kernels: 57 us -> 54.9 us  [soft_step(): pl.pallas_call(functools.partial(soft_kernel, group=group, distances=dist...]
    ppermute x10, waiting for transfers between devices: 0.03 us -> 1.56 us  [over_core(): return lax.ppermute(a, 'ctx', [(i, i ^ 1) for i in range(ctx)])]
  transfers between devices with their start and end apart: 23 -> 23, of which waited for: 5 -> 5; matrix products, arithmetic and copies ran while one was open for 0% -> 0% of each run, Pallas kernels for 53% -> 54%
where the time goes in v5:
time: 119 us; the launch traced here: 118 us
  Pallas kernels  75 us (63%)
  starting transfers between devices  21.4 us (18%)
  waiting for transfers between devices  15.1 us (13%)
  local copies, waits for them, and re-layouts  5.91 us (5%)
    pallas_call x6, Pallas kernels, soft_step(): pl.pallas_call(functools.partial(soft_kernel, group=group, distances=dist...  54.9 us
    ppermute x6, waiting for transfers between devices, over_x(): return lax.ppermute(a, 'ctx', [(i, i ^ 2) for i in range(ctx)])  9.45 us
    ppermute x6, starting transfers between devices, over_z(): lax.ppermute(a, 'ctx', [(i, i + PLANE * d) for i in range(ctx - PLANE * d)])  7.89 us
    ppermute x10, starting transfers between devices, over_core(): return lax.ppermute(a, 'ctx', [(i, i ^ 1) for i in range(ctx)])  7.25 us
    pallas_call x1, Pallas kernels, light(): pl.pallas_call(functools.partial(light_kernel, qh=wide // HD), grid=(4,),...  6.62 us
    pallas_call x1, Pallas kernels, local_state(): pl.pallas_call(functools.partial(state_kernel, qh=qh, heads=heads), grid_...  5.12 us
    ppermute x6, starting transfers between devices, over_x(): return lax.ppermute(a, 'ctx', [(i, i ^ 2) for i in range(ctx)])  4.99 us
    unnamed x17, local copies, waits for them, and re-layouts  4.93 us
  transfers between devices with their start and end apart: 23, of which 5 were waited for; matrix products, arithmetic and copies ran while one was open for 0% of the time, Pallas kernels for 54%

profile of v5, /device:TPU:27, one launch (start us, length us, event | category | flops | bytes accessed | tf_op | source)
XLA Modules:
  0.0 118.3 jit_solution(13448653218897631759)
XLA Ops:
  3.6 1.3 %collective-permute-start.1 = (bf16[256,1024]{1,0:T(8,128)(2,1)S(1)}, bf16[256,1024]{1,0:T(8,128)(2,1)S(1)}, u32[]{:S(2)}, u32[]{:S(2)}) collective-permute-start(bf16[256,1024]{1,0:T(8,128)(2,1)S(1)} %constant_dynamic-update-slice_fusion.refs_0_.refs_4_.refs_11_), channel_id=1, source_target_pairs={{0,8},{2,10},{4,12},{6,14},{8,16},{10,18},{12,20},{14,22},{16,24},... | collective-permute-start | bytes 1572872 | tf_op jit(solution)/shard_map/ppermute | solution.py:560
  4.9 1.6 %copy-done.1 = bf16[256,4096]{1,0:T(8,128)(2,1)S(1)} copy-done((bf16[256,4096]{1,0:T(8,128)(2,1)S(1)}, bf16[256,4096]{1,0:T(8,128)(2,1)}, u32[]{:S(2)}) %copy-start.1) | copy-done | bytes 2097176
  6.5 1.6 %copy-done.3 = bf16[256,4096]{1,0:T(8,128)(2,1)S(1)} copy-done((bf16[256,4096]{1,0:T(8,128)(2,1)S(1)}, bf16[256,4096]{1,0:T(8,128)(2,1)}, u32[]{:S(2)}) %copy-start.3) | copy-done | bytes 2097176
  8.9 5.1 %local_state.1 = (bf16[2,1040,128]{2,1,0:T(8,128)(2,1)S(1)}, bf16[2,1040,128]{2,1,0:T(8,128)(2,1)S(1)}, f32[4,256,128]{2,1,0:T(8,128)S(1)}, f32[4,8,256]{2,1,0:T(8,128)S(1)}, s32[1]{0:T(128)}) custom-call(s32[1]{0:T(128)} %bitcast.pos, bf16[256,4096]{1,0:T(8,128)(2,1)S(1)} %copy-done.1, bf16[256,4096]{1,0:T(8,128)(2,1)S(1)} %copy-done.3, f32[32,256]{1,0:T(8,128)S(1)} %bitcast.3), custom_call_target="tpu_custom_call" | custom-call | flops 1000 | bytes 1048576 | tf_op jit(solution)/shard_map/local_state/pallas_call | solution.py:124
  14.4 2.4 %collective-permute-done.3.refs_1_.refs_5_.refs_12_ = bf16[256,1024]{1,0:T(8,128)(2,1)S(1)} collective-permute-done((bf16[256,1024]{1,0:T(8,128)(2,1)S(1)}, bf16[256,1024]{1,0:T(8,128)(2,1)S(1)}, u32[]{:S(2)}, u32[]{:S(2)}) %collective-permute-start.3) | collective-permute-done | bytes 524320 | tf_op jit(solution)/shard_map/ppermute | solution.py:557
  18.7 1.3 %collective-permute-start.2 = (bf16[256,1024]{1,0:T(8,128)(2,1)S(1)}, bf16[256,1024]{1,0:T(8,128)(2,1)S(1)}, u32[]{:S(2)}, u32[]{:S(2)}) collective-permute-start(bf16[256,1024]{1,0:T(8,128)(2,1)S(1)} %collective-permute-done.1.refs_0_.refs_8_.refs_15_), channel_id=1, source_target_pairs={{0,8},{2,10},{4,12},{6,14},{8,16},{10,18},{12,20},{14,22},{16,24},... | collective-permute-start | bytes 1572872 | tf_op jit(solution)/shard_map/ppermute | solution.py:560
  19.9 1.3 %collective-permute-start.9 = (bf16[256,1024]{1,0:T(8,128)(2,1)S(1)}, bf16[256,1024]{1,0:T(8,128)(2,1)S(1)}, u32[]{:S(2)}, u32[]{:S(2)}) collective-permute-start(bf16[256,1024]{1,0:T(8,128)(2,1)S(1)} %collective-permute-done.1.refs_0_.refs_8_.refs_15_), channel_id=1, source_target_pairs={{0,4},{2,6},{4,0},{6,2},{8,12},{10,14},{12,8},{14,10},{16,20},{18,... | collective-permute-start | bytes 1572872 | tf_op jit(solution)/shard_map/ppermute | solution.py:557
  21.2 7.2 %softmax.6 = (f32[256,4096]{1,0:T(8,128)S(1)}, f32[4,256,128]{2,1,0:T(8,128)S(1)}, s32[1]{0:T(128)}) custom-call(s32[1]{0:T(128)} %bitcast.pos, bf16[256,4096]{1,0:T(8,128)(2,1)S(1)} %copy-done, bf16[256,1024]{1,0:T(8,128)(2,1)S(1)} %constant_dynamic-update-slice_fusion.refs_0_.refs_4_.refs_11_, ...), custom_call_target="tpu_custom_call" | custom-call | flops 1000 | bytes 1048576 | tf_op jit(solution)/shard_map/softmax/pallas_call | solution.py:508
  29.7 3.1 %collective-permute-done.2.refs_4_.refs_12_.refs_19_ = bf16[256,1024]{1,0:T(8,128)(2,1)S(1)} collective-permute-done((bf16[256,1024]{1,0:T(8,128)(2,1)S(1)}, bf16[256,1024]{1,0:T(8,128)(2,1)S(1)}, u32[]{:S(2)}, u32[]{:S(2)}) %collective-permute-start.2) | collective-permute-done | bytes 524320 | tf_op jit(solution)/shard_map/ppermute | solution.py:560
  34.0 1.3 %collective-permute-start.6 = (bf16[256,1024]{1,0:T(8,128)(2,1)S(1)}, bf16[256,1024]{1,0:T(8,128)(2,1)S(1)}, u32[]{:S(2)}, u32[]{:S(2)}) collective-permute-start(bf16[256,1024]{1,0:T(8,128)(2,1)S(1)} %collective-permute-done.2.refs_4_.refs_12_.refs_19_), channel_id=1, source_target_pairs={{0,8},{2,10},{4,12},{6,14},{8,16},{10,18},{12,20},{14,22},{16,24},... | collective-permute-start | bytes 1572872 | tf_op jit(solution)/shard_map/ppermute | solution.py:560
  35.6 7.2 %softmax.7 = (f32[256,4096]{1,0:T(8,128)S(1)}, f32[4,256,128]{2,1,0:T(8,128)S(1)}, s32[1]{0:T(128)}) custom-call(s32[1]{0:T(128)} %bitcast.pos, bf16[256,4096]{1,0:T(8,128)(2,1)S(1)} %copy-done, bf16[256,1024]{1,0:T(8,128)(2,1)S(1)} %constant_dynamic-update-slice_fusion.refs_0_.refs_4_.refs_11_, ...), custom_call_target="tpu_custom_call", output_to_operand_aliasing={{0}: (11, {}), {1}: (12, {})} | custom-call | flops 1000 | bytes 1048576 | tf_op jit(solution)/shard_map/softmax/pallas_call | solution.py:508
  42.8 7.0 %collective-permute-done.7.refs_1_ = bf16[1040,128]{1,0:T(8,128)(2,1)S(1)} collective-permute-done((bf16[1040,128]{1,0:T(8,128)(2,1)S(1)}, bf16[1040,128]{1,0:T(8,128)(2,1)S(1)}, u32[]{:S(2)}, u32[]{:S(2)}) %collective-permute-start.7) | collective-permute-done | bytes 266272 | tf_op jit(solution)/shard_map/ppermute | solution.py:557
  51.0 3.1 %collective-permute-start.10 = (bf16[256,1024]{1,0:T(8,128)(2,1)S(1)}, bf16[256,1024]{1,0:T(8,128)(2,1)S(1)}, u32[]{:S(2)}, u32[]{:S(2)}) collective-permute-start(bf16[256,1024]{1,0:T(8,128)(2,1)S(1)} %collective-permute-done.1.refs_0_.refs_8_.refs_15_), channel_id=1, source_target_pairs={{0,2},{2,0},{4,6},{6,4},{8,10},{10,8},{12,14},{14,12},{16,18},{18,... | collective-permute-start | bytes 1572872 | tf_op jit(solution)/shard_map/ppermute | solution.py:554
  55.9 1.3 %collective-permute-start.19 = (bf16[1040,128]{1,0:T(8,128)(2,1)S(1)}, bf16[1040,128]{1,0:T(8,128)(2,1)S(1)}, u32[]{:S(2)}, u32[]{:S(2)}) collective-permute-start(bf16[1040,128]{1,0:T(8,128)(2,1)S(1)} %get-tuple-element.78), channel_id=1, source_target_pairs={{0,24},{2,26},{4,28},{6,30},{1,25},{3,27},{5,29},{7,31}} | collective-permute-start | bytes 798728 | tf_op jit(solution)/shard_map/ppermute | solution.py:560
  57.2 1.3 %collective-permute-start.18 = (bf16[1040,128]{1,0:T(8,128)(2,1)S(1)}, bf16[1040,128]{1,0:T(8,128)(2,1)S(1)}, u32[]{:S(2)}, u32[]{:S(2)}) collective-permute-start(bf16[1040,128]{1,0:T(8,128)(2,1)S(1)} %get-tuple-element.78), channel_id=1, source_target_pairs={{0,16},{2,18},{4,20},{6,22},{8,24},{10,26},{12,28},{14,30},{1,17},... | collective-permute-start | bytes 798728 | tf_op jit(solution)/shard_map/ppermute | solution.py:560
  58.5 1.5 %collective-permute-start.17 = (bf16[1040,128]{1,0:T(8,128)(2,1)S(1)}, bf16[1040,128]{1,0:T(8,128)(2,1)S(1)}, u32[]{:S(2)}, u32[]{:S(2)}) collective-permute-start(bf16[1040,128]{1,0:T(8,128)(2,1)S(1)} %get-tuple-element.78), channel_id=1, source_target_pairs={{0,8},{2,10},{4,12},{6,14},{8,16},{10,18},{12,20},{14,22},{16,24},... | collective-permute-start | bytes 798728 | tf_op jit(solution)/shard_map/ppermute | solution.py:560
  60.0 12.2 %softmax.8 = (f32[256,4096]{1,0:T(8,128)S(1)}, f32[4,256,128]{2,1,0:T(8,128)S(1)}, s32[1]{0:T(128)}) custom-call(s32[1]{0:T(128)} %bitcast.pos, bf16[256,4096]{1,0:T(8,128)(2,1)S(1)} %copy-done, bf16[256,1024]{1,0:T(8,128)(2,1)S(1)} %collective-permute-done.1.refs_0_.refs_8_.refs_15_, ...), custom_call_target="tpu_custom_call", output_to_operand_aliasing={{0}: (18, {}), {1}: (19, {})} | custom-call | flops 1000 | bytes 1048576 | tf_op jit(solution)/shard_map/softmax/pallas_call | solution.py:508
  73.0 12.1 %softmax.9 = (f32[256,4096]{1,0:T(8,128)S(1)}, f32[4,256,128]{2,1,0:T(8,128)S(1)}, s32[1]{0:T(128)}) custom-call(s32[1]{0:T(128)} %bitcast.pos, bf16[256,4096]{1,0:T(8,128)(2,1)S(1)} %copy-done, bf16[256,1024]{1,0:T(8,128)(2,1)S(1)} %collective-permute-done.1.refs_0_.refs_8_.refs_15_, ...), custom_call_target="tpu_custom_call", output_to_operand_aliasing={{0}: (18, {}), {1}: (19, {})} | custom-call | flops 1000 | bytes 1048576 | tf_op jit(solution)/shard_map/softmax/pallas_call | solution.py:508
  87.1 8.2 %softmax.10 = (bf16[256,4096]{1,0:T(8,128)(2,1)}, s32[1]{0:T(128)}) custom-call(s32[1]{0:T(128)} %bitcast.pos, bf16[256,4096]{1,0:T(8,128)(2,1)S(1)} %copy-done, bf16[256,1024]{1,0:T(8,128)(2,1)S(1)} %collective-permute-done.6.refs_0_.refs_4_.refs_23_, bf16[256,1024]{1,0:T(8,128)(2,1)S(1)} %collective-permute-done.8.refs_1_.refs_5_.refs_24_, ...), custom_call_target="tpu_custom_call" | custom-call | flops 1000 | bytes 1048576 | tf_op jit(solution)/shard_map/softmax/pallas_call | solution.py:508
  97.2 1.5 %collective-permute-done.21.recv_ref = bf16[2,1024,128]{2,1,0:T(8,128)(2,1)S(1)} collective-permute-done((bf16[2,1024,128]{2,1,0:T(8,128)(2,1)S(1)}, bf16[2,1024,128]{2,1,0:T(8,128)(2,1)S(1)}, u32[]{:S(2)}, u32[]{:S(2)}) %collective-permute-start.21) | collective-permute-done | bytes 524320 | tf_op jit(solution)/shard_map/ppermute | solution.py:554
  98.8 6.6 %light.1 = (bf16[256,4096]{1,0:T(8,128)(2,1)S(1)}, f32[256,128]{1,0:T(8,128)S(1)}, s32[1]{0:T(128)}) custom-call(s32[1]{0:T(128)} %bitcast.pos, bf16[256,4096]{1,0:T(8,128)(2,1)S(1)} %copy-done.5, bf16[256,4096]{1,0:T(8,128)(2,1)S(1)} %copy-done.2, bf16[256,4096]{1,0:T(8,128)(2,1)S(1)} %copy-done.3, f32[4,256,128]{2,1,0:T(8,128)S(1)} %get-tuple-element.48.cum_ref, ...), custom_call_target="tpu_custom_call" | custom-call | flops 1000 | bytes 1048576 | tf_op jit(solution)/shard_map/light/pallas_call | solution.py:281
  105.4 1.3 %collective-permute-start.22 = (f32[256,128]{1,0:T(8,128)S(1)}, f32[256,128]{1,0:T(8,128)S(1)}, u32[]{:S(2)}, u32[]{:S(2)}) collective-permute-start(f32[256,128]{1,0:T(8,128)S(1)} %get-tuple-element.87.refs_0_), channel_id=1, source_target_pairs={{0,1},{1,0},{2,3},{3,2},{4,5},{5,4},{6,7},{7,6},{8,9},{9,8},{10,11... | collective-permute-start | bytes 393224 | tf_op jit(solution)/shard_map/ppermute | solution.py:638
  106.7 7.9 %softmax.11 = (bf16[256,4096]{1,0:T(8,128)(2,1)}, s32[1]{0:T(128)}) custom-call(s32[1]{0:T(128)} %bitcast.pos, bf16[256,4096]{1,0:T(8,128)(2,1)S(1)} %copy-done, bf16[256,1024]{1,0:T(8,128)(2,1)S(1)} %collective-permute-done.6.refs_0_.refs_4_.refs_23_, ...), custom_call_target="tpu_custom_call", output_to_operand_aliasing={{0}: (29, {})} | custom-call | flops 1000 | bytes 1048576 | tf_op jit(solution)/shard_map/softmax/pallas_call | solution.py:508
  114.7 3.6 %finish.1 = bf16[256,4096]{1,0:T(8,128)(2,1)} custom-call(bf16[256,4096]{1,0:T(8,128)(2,1)S(1)} %get-tuple-element.86.raw_ref, f32[256,128]{1,0:T(8,128)S(1)} %get-tuple-element.87.refs_0_, f32[256,128]{1,0:T(8,128)S(1)} %collective-permute-done.22.refs_1_, f32[1,4096]{1,0:T(1,128)S(1)} %bitcast.4, bf16[256,4096]{1,0:T(8,128)(2,1)S(1)} %copy-done.4, ...), custom_call_target="tpu_custom_call" | custom-call | flops 1000 | bytes 1048576 | tf_op jit(solution)/shard_map/finish/pallas_call | solution.py:325
  (53 shorter events, 16.4 us)
Async XLA Ops:
  2.6 2.3 %collective-permute-start = (bf16[256,1024]{1,0:T(8,128)(2,1)S(1)}, bf16[256,1024]{1,0:T(8,128)(2,1)S(1)}, u32[]{:S(2)}, u32[]{:S(2)}) collective-permute-start(bf16[256,1024]{1,0:T(8,128)(2,1)S(1)} %constant_dynamic-update-slice_fusion.refs_0_.refs_4_.refs_11_), channel_id=1, source_target_pairs={{0,2},{2,0},{4,6},{6,4},{8,10},{10,8},{12,14},{14,12},{16,18},{18,... | collective-permute-start | bytes 1572872 | tf_op jit(solution)/shard_map/ppermute | solution.py:554
  3.3 13.5 %collective-permute-start.3 = (bf16[256,1024]{1,0:T(8,128)(2,1)S(1)}, bf16[256,1024]{1,0:T(8,128)(2,1)S(1)}, u32[]{:S(2)}, u32[]{:S(2)}) collective-permute-start(bf16[256,1024]{1,0:T(8,128)(2,1)S(1)} %constant_dynamic-update-slice_fusion.refs_0_.refs_4_.refs_11_), channel_id=1, source_target_pairs={{0,4},{2,6},{4,0},{6,2},{8,12},{10,14},{12,8},{14,10},{16,20},{18,... | collective-permute-start | bytes 1572872 | tf_op jit(solution)/shard_map/ppermute | solution.py:557
  3.6 15.0 %collective-permute-start.1 = (bf16[256,1024]{1,0:T(8,128)(2,1)S(1)}, bf16[256,1024]{1,0:T(8,128)(2,1)S(1)}, u32[]{:S(2)}, u32[]{:S(2)}) collective-permute-start(bf16[256,1024]{1,0:T(8,128)(2,1)S(1)} %constant_dynamic-update-slice_fusion.refs_0_.refs_4_.refs_11_), channel_id=1, source_target_pairs={{0,8},{2,10},{4,12},{6,14},{8,16},{10,18},{12,20},{14,22},{16,24},... | collective-permute-start | bytes 1572872 | tf_op jit(solution)/shard_map/ppermute | solution.py:560
  8.9 12.4 %copy-start = (bf16[256,4096]{1,0:T(8,128)(2,1)S(1)}, bf16[256,4096]{1,0:T(8,128)(2,1)}, u32[]{:S(2)}) copy-start(bf16[256,4096]{1,0:T(8,128)(2,1)} %q_ref.13) | copy-start | bytes 6291460
  14.0 14.4 %collective-permute-start.5 = (bf16[2,1040,128]{2,1,0:T(8,128)(2,1)S(1)}, bf16[2,1040,128]{2,1,0:T(8,128)(2,1)S(1)}, u32[]{:S(2)}, u32[]{:S(2)}) collective-permute-start(bf16[2,1040,128]{2,1,0:T(8,128)(2,1)S(1)} %get-tuple-element.54), channel_id=1, source_target_pairs={{0,2},{2,0},{4,6},{6,4},{8,10},{10,8},{12,14},{14,12},{16,18},{18,... | collective-permute-start | bytes 1597448 | tf_op jit(solution)/shard_map/ppermute | solution.py:554
  16.8 4.4 %collective-permute-start.4 = (bf16[256,1024]{1,0:T(8,128)(2,1)S(1)}, bf16[256,1024]{1,0:T(8,128)(2,1)S(1)}, u32[]{:S(2)}, u32[]{:S(2)}) collective-permute-start(bf16[256,1024]{1,0:T(8,128)(2,1)S(1)} %collective-permute-done.3.refs_1_.refs_5_.refs_12_), channel_id=1, source_target_pairs={{0,2},{2,0},{4,6},{6,4},{8,10},{10,8},{12,14},{14,12},{16,18},{18,... | collective-permute-start | bytes 1572872 | tf_op jit(solution)/shard_map/ppermute | solution.py:554
  18.7 14.1 %collective-permute-start.2 = (bf16[256,1024]{1,0:T(8,128)(2,1)S(1)}, bf16[256,1024]{1,0:T(8,128)(2,1)S(1)}, u32[]{:S(2)}, u32[]{:S(2)}) collective-permute-start(bf16[256,1024]{1,0:T(8,128)(2,1)S(1)} %collective-permute-done.1.refs_0_.refs_8_.refs_15_), channel_id=1, source_target_pairs={{0,8},{2,10},{4,12},{6,14},{8,16},{10,18},{12,20},{14,22},{16,24},... | collective-permute-start | bytes 1572872 | tf_op jit(solution)/shard_map/ppermute | solution.py:560
  19.9 34.1 %collective-permute-start.9 = (bf16[256,1024]{1,0:T(8,128)(2,1)S(1)}, bf16[256,1024]{1,0:T(8,128)(2,1)S(1)}, u32[]{:S(2)}, u32[]{:S(2)}) collective-permute-start(bf16[256,1024]{1,0:T(8,128)(2,1)S(1)} %collective-permute-done.1.refs_0_.refs_8_.refs_15_), channel_id=1, source_target_pairs={{0,4},{2,6},{4,0},{6,2},{8,12},{10,14},{12,8},{14,10},{16,20},{18,... | collective-permute-start | bytes 1572872 | tf_op jit(solution)/shard_map/ppermute | solution.py:557
  32.8 21.8 %collective-permute-start.12 = (bf16[256,1024]{1,0:T(8,128)(2,1)S(1)}, bf16[256,1024]{1,0:T(8,128)(2,1)S(1)}, u32[]{:S(2)}, u32[]{:S(2)}) collective-permute-start(bf16[256,1024]{1,0:T(8,128)(2,1)S(1)} %collective-permute-done.2.refs_4_.refs_12_.refs_19_), channel_id=1, source_target_pairs={{0,4},{2,6},{4,0},{6,2},{8,12},{10,14},{12,8},{14,10},{16,20},{18,... | collective-permute-start | bytes 1572872 | tf_op jit(solution)/shard_map/ppermute | solution.py:557
  34.0 20.6 %collective-permute-start.6 = (bf16[256,1024]{1,0:T(8,128)(2,1)S(1)}, bf16[256,1024]{1,0:T(8,128)(2,1)S(1)}, u32[]{:S(2)}, u32[]{:S(2)}) collective-permute-start(bf16[256,1024]{1,0:T(8,128)(2,1)S(1)} %collective-permute-done.2.refs_4_.refs_12_.refs_19_), channel_id=1, source_target_pairs={{0,8},{2,10},{4,12},{6,14},{8,16},{10,18},{12,20},{14,22},{16,24},... | collective-permute-start | bytes 1572872 | tf_op jit(solution)/shard_map/ppermute | solution.py:560
  35.3 14.5 %collective-permute-start.7 = (bf16[1040,128]{1,0:T(8,128)(2,1)S(1)}, bf16[1040,128]{1,0:T(8,128)(2,1)S(1)}, u32[]{:S(2)}, u32[]{:S(2)}) collective-permute-start(bf16[1040,128]{1,0:T(8,128)(2,1)S(1)} %get-tuple-element.61), channel_id=1, source_target_pairs={{0,4},{2,6},{4,0},{6,2},{8,12},{10,14},{12,8},{14,10},{16,20},{18,... | collective-permute-start | bytes 798728 | tf_op jit(solution)/shard_map/ppermute | solution.py:557
  51.0 4.9 %collective-permute-start.10 = (bf16[256,1024]{1,0:T(8,128)(2,1)S(1)}, bf16[256,1024]{1,0:T(8,128)(2,1)S(1)}, u32[]{:S(2)}, u32[]{:S(2)}) collective-permute-start(bf16[256,1024]{1,0:T(8,128)(2,1)S(1)} %collective-permute-done.1.refs_0_.refs_8_.refs_15_), channel_id=1, source_target_pairs={{0,2},{2,0},{4,6},{6,4},{8,10},{10,8},{12,14},{14,12},{16,18},{18,... | collective-permute-start | bytes 1572872 | tf_op jit(solution)/shard_map/ppermute | solution.py:554
  54.0 3.1 %collective-permute-start.11 = (bf16[256,1024]{1,0:T(8,128)(2,1)S(1)}, bf16[256,1024]{1,0:T(8,128)(2,1)S(1)}, u32[]{:S(2)}, u32[]{:S(2)}) collective-permute-start(bf16[256,1024]{1,0:T(8,128)(2,1)S(1)} %collective-permute-done.9.refs_1_.refs_9_.refs_16_), channel_id=1, source_target_pairs={{0,2},{2,0},{4,6},{6,4},{8,10},{10,8},{12,14},{14,12},{16,18},{18,... | collective-permute-start | bytes 1572872 | tf_op jit(solution)/shard_map/ppermute | solution.py:554
  54.1 4.3 %collective-permute-start.13 = (bf16[256,1024]{1,0:T(8,128)(2,1)S(1)}, bf16[256,1024]{1,0:T(8,128)(2,1)S(1)}, u32[]{:S(2)}, u32[]{:S(2)}) collective-permute-start(bf16[256,1024]{1,0:T(8,128)(2,1)S(1)} %collective-permute-done.2.refs_4_.refs_12_.refs_19_), channel_id=1, source_target_pairs={{0,2},{2,0},{4,6},{6,4},{8,10},{10,8},{12,14},{14,12},{16,18},{18,... | collective-permute-start | bytes 1572872 | tf_op jit(solution)/shard_map/ppermute | solution.py:554
  54.6 5.4 %collective-permute-start.14 = (bf16[256,1024]{1,0:T(8,128)(2,1)S(1)}, bf16[256,1024]{1,0:T(8,128)(2,1)S(1)}, u32[]{:S(2)}, u32[]{:S(2)}) collective-permute-start(bf16[256,1024]{1,0:T(8,128)(2,1)S(1)} %collective-permute-done.12.refs_5_.refs_13_.refs_20_), channel_id=1, source_target_pairs={{0,2},{2,0},{4,6},{6,4},{8,10},{10,8},{12,14},{14,12},{16,18},{18,... | collective-permute-start | bytes 1572872 | tf_op jit(solution)/shard_map/ppermute | solution.py:554
  54.6 18.3 %collective-permute-start.8 = (bf16[256,1024]{1,0:T(8,128)(2,1)S(1)}, bf16[256,1024]{1,0:T(8,128)(2,1)S(1)}, u32[]{:S(2)}, u32[]{:S(2)}) collective-permute-start(bf16[256,1024]{1,0:T(8,128)(2,1)S(1)} %collective-permute-done.6.refs_0_.refs_4_.refs_23_), channel_id=1, source_target_pairs={{0,4},{2,6},{4,0},{6,2},{8,12},{10,14},{12,8},{14,10},{16,20},{18,... | collective-permute-start | bytes 1572872 | tf_op jit(solution)/shard_map/ppermute | solution.py:557
  55.9 29.3 %collective-permute-start.19 = (bf16[1040,128]{1,0:T(8,128)(2,1)S(1)}, bf16[1040,128]{1,0:T(8,128)(2,1)S(1)}, u32[]{:S(2)}, u32[]{:S(2)}) collective-permute-start(bf16[1040,128]{1,0:T(8,128)(2,1)S(1)} %get-tuple-element.78), channel_id=1, source_target_pairs={{0,24},{2,26},{4,28},{6,30},{1,25},{3,27},{5,29},{7,31}} | collective-permute-start | bytes 798728 | tf_op jit(solution)/shard_map/ppermute | solution.py:560
  57.2 28.0 %collective-permute-start.18 = (bf16[1040,128]{1,0:T(8,128)(2,1)S(1)}, bf16[1040,128]{1,0:T(8,128)(2,1)S(1)}, u32[]{:S(2)}, u32[]{:S(2)}) collective-permute-start(bf16[1040,128]{1,0:T(8,128)(2,1)S(1)} %get-tuple-element.78), channel_id=1, source_target_pairs={{0,16},{2,18},{4,20},{6,22},{8,24},{10,26},{12,28},{14,30},{1,17},... | collective-permute-start | bytes 798728 | tf_op jit(solution)/shard_map/ppermute | solution.py:560
  58.5 26.7 %collective-permute-start.17 = (bf16[1040,128]{1,0:T(8,128)(2,1)S(1)}, bf16[1040,128]{1,0:T(8,128)(2,1)S(1)}, u32[]{:S(2)}, u32[]{:S(2)}) collective-permute-start(bf16[1040,128]{1,0:T(8,128)(2,1)S(1)} %get-tuple-element.78), channel_id=1, source_target_pairs={{0,8},{2,10},{4,12},{6,14},{8,16},{10,18},{12,20},{14,22},{16,24},... | collective-permute-start | bytes 798728 | tf_op jit(solution)/shard_map/ppermute | solution.py:560
  72.1 14.9 %collective-permute-start.15 = (bf16[256,1024]{1,0:T(8,128)(2,1)S(1)}, bf16[256,1024]{1,0:T(8,128)(2,1)S(1)}, u32[]{:S(2)}, u32[]{:S(2)}) collective-permute-start(bf16[256,1024]{1,0:T(8,128)(2,1)S(1)} %collective-permute-done.6.refs_0_.refs_4_.refs_23_), channel_id=1, source_target_pairs={{0,2},{2,0},{4,6},{6,4},{8,10},{10,8},{12,14},{14,12},{16,18},{18,... | collective-permute-start | bytes 1572872 | tf_op jit(solution)/shard_map/ppermute | solution.py:554
  72.9 14.2 %collective-permute-start.16 = (bf16[256,1024]{1,0:T(8,128)(2,1)S(1)}, bf16[256,1024]{1,0:T(8,128)(2,1)S(1)}, u32[]{:S(2)}, u32[]{:S(2)}) collective-permute-start(bf16[256,1024]{1,0:T(8,128)(2,1)S(1)} %collective-permute-done.8.refs_1_.refs_5_.refs_24_), channel_id=1, source_target_pairs={{0,2},{2,0},{4,6},{6,4},{8,10},{10,8},{12,14},{14,12},{16,18},{18,... | collective-permute-start | bytes 1572872 | tf_op jit(solution)/shard_map/ppermute | solution.py:554
  86.4 8.9 %collective-permute-start.20 = (bf16[1040,128]{1,0:T(8,128)(2,1)S(1)}, bf16[1040,128]{1,0:T(8,128)(2,1)S(1)}, u32[]{:S(2)}, u32[]{:S(2)}) collective-permute-start(bf16[1040,128]{1,0:T(8,128)(2,1)S(1)} %get-tuple-element.82), channel_id=1, source_target_pairs={{0,4},{2,6},{4,0},{6,2},{8,12},{10,14},{12,8},{14,10},{16,20},{18,... | collective-permute-start | bytes 798728 | tf_op jit(solution)/shard_map/ppermute | solution.py:557
  96.5 2.3 %collective-permute-start.21 = (bf16[2,1024,128]{2,1,0:T(8,128)(2,1)S(1)}, bf16[2,1024,128]{2,1,0:T(8,128)(2,1)S(1)}, u32[]{:S(2)}, u32[]{:S(2)}) collective-permute-start(bf16[2,1024,128]{2,1,0:T(8,128)(2,1)S(1)} %get-tuple-element.84), channel_id=1, source_target_pairs={{0,2},{2,0},{4,6},{6,4},{8,10},{10,8},{12,14},{14,12},{16,18},{18,... | collective-permute-start | bytes 1572872 | tf_op jit(solution)/shard_map/ppermute | solution.py:554
  105.4 9.3 %collective-permute-start.22 = (f32[256,128]{1,0:T(8,128)S(1)}, f32[256,128]{1,0:T(8,128)S(1)}, u32[]{:S(2)}, u32[]{:S(2)}) collective-permute-start(f32[256,128]{1,0:T(8,128)S(1)} %get-tuple-element.87.refs_0_), channel_id=1, source_target_pairs={{0,1},{1,0},{2,3},{3,2},{4,5},{5,4},{6,7},{7,6},{8,9},{9,8},{10,11... | collective-permute-start | bytes 393224 | tf_op jit(solution)/shard_map/ppermute | solution.py:638
  (7 other events, 43.2 us)

commit v6 on v5

--- a/solution.py
+++ b/solution.py
@@ -602,9 +602,9 @@
     forward(token)
     if len(spans) > 1:
         state, token = soft((0,), None, False, token, spans[1], state)
+    spread_core(1, token)
     plane, token = small(plane_kernel, pos, [chip_keep, chip_other], [quarter], qh, "plane", token)
     earlier = [over_z(plane, d) for d in range(1, planes)]
-    spread_core(1, token)
     spread_core(2, token)
     cross(3, token)
     for d in range(3, planes - 1):

time: 119 us -> 119 us (level)
  waiting for transfers between devices: 15.1 us -> 12.3 us
  starting transfers between devices: 21.4 us -> 23.4 us
    ppermute x6, waiting for transfers between devices: 9.45 us -> 6.64 us  [over_x(): return lax.ppermute(a, 'ctx', [(i, i ^ 2) for i in range(ctx)])]
    ppermute x10, starting transfers between devices: 7.25 us -> 9.59 us  [over_core(): return lax.ppermute(a, 'ctx', [(i, i ^ 1) for i in range(ctx)])]
where the time goes in v6:
time: 119 us; the launch traced here: 117 us
  Pallas kernels  75 us (63%)
  starting transfers between devices  23.4 us (20%)
  waiting for transfers between devices  12.3 us (10%)
  local copies, waits for them, and re-layouts  5.91 us (5%)
    pallas_call x6, Pallas kernels, soft_step(): pl.pallas_call(functools.partial(soft_kernel, group=group, distances=dist...  54.9 us
    ppermute x10, starting transfers between devices, over_core(): return lax.ppermute(a, 'ctx', [(i, i ^ 1) for i in range(ctx)])  9.59 us
    ppermute x6, starting transfers between devices, over_z(): lax.ppermute(a, 'ctx', [(i, i + PLANE * d) for i in range(ctx - PLANE * d)])  7.89 us
    ppermute x6, waiting for transfers between devices, over_x(): return lax.ppermute(a, 'ctx', [(i, i ^ 2) for i in range(ctx)])  6.64 us
    pallas_call x1, Pallas kernels, light(): pl.pallas_call(functools.partial(light_kernel, qh=wide // HD), grid=(4,),...  6.62 us
    pallas_call x1, Pallas kernels, local_state(): pl.pallas_call(functools.partial(state_kernel, qh=qh, heads=heads), grid_...  5.12 us
    unnamed x17, local copies, waits for them, and re-layouts  4.93 us
    pallas_call x4, Pallas kernels, small(): pl.pallas_call(functools.partial(with_token, functools.partial(kernel, qh...  4.76 us
  transfers between devices with their start and end apart: 23, of which 5 were waited for; matrix products, arithmetic and copies ran while one was open for 0% of the time, Pallas kernels for 54%

profile of v6, /device:TPU:27, one launch (start us, length us, event | category | flops | bytes accessed | tf_op | source)
XLA Modules:
  0.0 117.5 jit_solution(9945414381863093091)
XLA Ops:
  3.6 1.3 %collective-permute-start.1 = (bf16[256,1024]{1,0:T(8,128)(2,1)S(1)}, bf16[256,1024]{1,0:T(8,128)(2,1)S(1)}, u32[]{:S(2)}, u32[]{:S(2)}) collective-permute-start(bf16[256,1024]{1,0:T(8,128)(2,1)S(1)} %constant_dynamic-update-slice_fusion.refs_0_.refs_4_.refs_11_), channel_id=1, source_target_pairs={{0,8},{2,10},{4,12},{6,14},{8,16},{10,18},{12,20},{14,22},{16,24},... | collective-permute-start | bytes 1572872 | tf_op jit(solution)/shard_map/ppermute | solution.py:560
  4.9 1.6 %copy-done.1 = bf16[256,4096]{1,0:T(8,128)(2,1)S(1)} copy-done((bf16[256,4096]{1,0:T(8,128)(2,1)S(1)}, bf16[256,4096]{1,0:T(8,128)(2,1)}, u32[]{:S(2)}) %copy-start.1) | copy-done | bytes 2097176
  6.5 1.6 %copy-done.3 = bf16[256,4096]{1,0:T(8,128)(2,1)S(1)} copy-done((bf16[256,4096]{1,0:T(8,128)(2,1)S(1)}, bf16[256,4096]{1,0:T(8,128)(2,1)}, u32[]{:S(2)}) %copy-start.3) | copy-done | bytes 2097176
  8.9 5.1 %local_state.1 = (bf16[2,1040,128]{2,1,0:T(8,128)(2,1)S(1)}, bf16[2,1040,128]{2,1,0:T(8,128)(2,1)S(1)}, f32[4,256,128]{2,1,0:T(8,128)S(1)}, f32[4,8,256]{2,1,0:T(8,128)S(1)}, s32[1]{0:T(128)}) custom-call(s32[1]{0:T(128)} %bitcast.pos, bf16[256,4096]{1,0:T(8,128)(2,1)S(1)} %copy-done.1, bf16[256,4096]{1,0:T(8,128)(2,1)S(1)} %copy-done.3, f32[32,256]{1,0:T(8,128)S(1)} %bitcast.3), custom_call_target="tpu_custom_call" | custom-call | flops 1000 | bytes 1048576 | tf_op jit(solution)/shard_map/local_state/pallas_call | solution.py:124
  14.4 2.4 %collective-permute-done.3.refs_1_.refs_5_.refs_12_ = bf16[256,1024]{1,0:T(8,128)(2,1)S(1)} collective-permute-done((bf16[256,1024]{1,0:T(8,128)(2,1)S(1)}, bf16[256,1024]{1,0:T(8,128)(2,1)S(1)}, u32[]{:S(2)}, u32[]{:S(2)}) %collective-permute-start.3) | collective-permute-done | bytes 524320 | tf_op jit(solution)/shard_map/ppermute | solution.py:557
  18.7 1.3 %collective-permute-start.2 = (bf16[256,1024]{1,0:T(8,128)(2,1)S(1)}, bf16[256,1024]{1,0:T(8,128)(2,1)S(1)}, u32[]{:S(2)}, u32[]{:S(2)}) collective-permute-start(bf16[256,1024]{1,0:T(8,128)(2,1)S(1)} %collective-permute-done.1.refs_0_.refs_8_.refs_15_), channel_id=1, source_target_pairs={{0,8},{2,10},{4,12},{6,14},{8,16},{10,18},{12,20},{14,22},{16,24},... | collective-permute-start | bytes 1572872 | tf_op jit(solution)/shard_map/ppermute | solution.py:560
  21.2 7.2 %softmax.6 = (f32[256,4096]{1,0:T(8,128)S(1)}, f32[4,256,128]{2,1,0:T(8,128)S(1)}, s32[1]{0:T(128)}) custom-call(s32[1]{0:T(128)} %bitcast.pos, bf16[256,4096]{1,0:T(8,128)(2,1)S(1)} %copy-done, bf16[256,1024]{1,0:T(8,128)(2,1)S(1)} %constant_dynamic-update-slice_fusion.refs_0_.refs_4_.refs_11_, ...), custom_call_target="tpu_custom_call" | custom-call | flops 1000 | bytes 1048576 | tf_op jit(solution)/shard_map/softmax/pallas_call | solution.py:508
  29.7 3.1 %collective-permute-done.2.refs_4_.refs_12_.refs_19_ = bf16[256,1024]{1,0:T(8,128)(2,1)S(1)} collective-permute-done((bf16[256,1024]{1,0:T(8,128)(2,1)S(1)}, bf16[256,1024]{1,0:T(8,128)(2,1)S(1)}, u32[]{:S(2)}, u32[]{:S(2)}) %collective-permute-start.2) | collective-permute-done | bytes 524320 | tf_op jit(solution)/shard_map/ppermute | solution.py:560
  34.0 1.3 %collective-permute-start.6 = (bf16[256,1024]{1,0:T(8,128)(2,1)S(1)}, bf16[256,1024]{1,0:T(8,128)(2,1)S(1)}, u32[]{:S(2)}, u32[]{:S(2)}) collective-permute-start(bf16[256,1024]{1,0:T(8,128)(2,1)S(1)} %collective-permute-done.2.refs_4_.refs_12_.refs_19_), channel_id=1, source_target_pairs={{0,8},{2,10},{4,12},{6,14},{8,16},{10,18},{12,20},{14,22},{16,24},... | collective-permute-start | bytes 1572872 | tf_op jit(solution)/shard_map/ppermute | solution.py:560
  35.6 7.2 %softmax.7 = (f32[256,4096]{1,0:T(8,128)S(1)}, f32[4,256,128]{2,1,0:T(8,128)S(1)}, s32[1]{0:T(128)}) custom-call(s32[1]{0:T(128)} %bitcast.pos, bf16[256,4096]{1,0:T(8,128)(2,1)S(1)} %copy-done, bf16[256,1024]{1,0:T(8,128)(2,1)S(1)} %constant_dynamic-update-slice_fusion.refs_0_.refs_4_.refs_11_, ...), custom_call_target="tpu_custom_call", output_to_operand_aliasing={{0}: (11, {}), {1}: (12, {})} | custom-call | flops 1000 | bytes 1048576 | tf_op jit(solution)/shard_map/softmax/pallas_call | solution.py:508
  42.8 2.7 %collective-permute-start.10 = (bf16[256,1024]{1,0:T(8,128)(2,1)S(1)}, bf16[256,1024]{1,0:T(8,128)(2,1)S(1)}, u32[]{:S(2)}, u32[]{:S(2)}) collective-permute-start(bf16[256,1024]{1,0:T(8,128)(2,1)S(1)} %collective-permute-done.1.refs_0_.refs_8_.refs_15_), channel_id=1, source_target_pairs={{0,2},{2,0},{4,6},{6,4},{8,10},{10,8},{12,14},{14,12},{16,18},{18,... | collective-permute-start | bytes 1572872 | tf_op jit(solution)/shard_map/ppermute | solution.py:554
  45.6 4.2 %collective-permute-done.7.refs_1_ = bf16[1040,128]{1,0:T(8,128)(2,1)S(1)} collective-permute-done((bf16[1040,128]{1,0:T(8,128)(2,1)S(1)}, bf16[1040,128]{1,0:T(8,128)(2,1)S(1)}, u32[]{:S(2)}, u32[]{:S(2)}) %collective-permute-start.7) | collective-permute-done | bytes 266272 | tf_op jit(solution)/shard_map/ppermute | solution.py:557
  51.0 3.1 %collective-permute-start.13 = (bf16[256,1024]{1,0:T(8,128)(2,1)S(1)}, bf16[256,1024]{1,0:T(8,128)(2,1)S(1)}, u32[]{:S(2)}, u32[]{:S(2)}) collective-permute-start(bf16[256,1024]{1,0:T(8,128)(2,1)S(1)} %collective-permute-done.2.refs_4_.refs_12_.refs_19_), channel_id=1, source_target_pairs={{0,2},{2,0},{4,6},{6,4},{8,10},{10,8},{12,14},{14,12},{16,18},{18,... | collective-permute-start | bytes 1572872 | tf_op jit(solution)/shard_map/ppermute | solution.py:554
  55.3 1.3 %collective-permute-start.19 = (bf16[1040,128]{1,0:T(8,128)(2,1)S(1)}, bf16[1040,128]{1,0:T(8,128)(2,1)S(1)}, u32[]{:S(2)}, u32[]{:S(2)}) collective-permute-start(bf16[1040,128]{1,0:T(8,128)(2,1)S(1)} %get-tuple-element.78), channel_id=1, source_target_pairs={{0,24},{2,26},{4,28},{6,30},{1,25},{3,27},{5,29},{7,31}} | collective-permute-start | bytes 798728 | tf_op jit(solution)/shard_map/ppermute | solution.py:560
  56.6 1.3 %collective-permute-start.18 = (bf16[1040,128]{1,0:T(8,128)(2,1)S(1)}, bf16[1040,128]{1,0:T(8,128)(2,1)S(1)}, u32[]{:S(2)}, u32[]{:S(2)}) collective-permute-start(bf16[1040,128]{1,0:T(8,128)(2,1)S(1)} %get-tuple-element.78), channel_id=1, source_target_pairs={{0,16},{2,18},{4,20},{6,22},{8,24},{10,26},{12,28},{14,30},{1,17},... | collective-permute-start | bytes 798728 | tf_op jit(solution)/shard_map/ppermute | solution.py:560
  58.0 1.5 %collective-permute-start.17 = (bf16[1040,128]{1,0:T(8,128)(2,1)S(1)}, bf16[1040,128]{1,0:T(8,128)(2,1)S(1)}, u32[]{:S(2)}, u32[]{:S(2)}) collective-permute-start(bf16[1040,128]{1,0:T(8,128)(2,1)S(1)} %get-tuple-element.78), channel_id=1, source_target_pairs={{0,8},{2,10},{4,12},{6,14},{8,16},{10,18},{12,20},{14,22},{16,24},... | collective-permute-start | bytes 798728 | tf_op jit(solution)/shard_map/ppermute | solution.py:560
  59.4 12.2 %softmax.8 = (f32[256,4096]{1,0:T(8,128)S(1)}, f32[4,256,128]{2,1,0:T(8,128)S(1)}, s32[1]{0:T(128)}) custom-call(s32[1]{0:T(128)} %bitcast.pos, bf16[256,4096]{1,0:T(8,128)(2,1)S(1)} %copy-done, bf16[256,1024]{1,0:T(8,128)(2,1)S(1)} %collective-permute-done.1.refs_0_.refs_8_.refs_15_, ...), custom_call_target="tpu_custom_call", output_to_operand_aliasing={{0}: (18, {}), {1}: (19, {})} | custom-call | flops 1000 | bytes 1048576 | tf_op jit(solution)/shard_map/softmax/pallas_call | solution.py:508
  72.5 12.1 %softmax.9 = (f32[256,4096]{1,0:T(8,128)S(1)}, f32[4,256,128]{2,1,0:T(8,128)S(1)}, s32[1]{0:T(128)}) custom-call(s32[1]{0:T(128)} %bitcast.pos, bf16[256,4096]{1,0:T(8,128)(2,1)S(1)} %copy-done, bf16[256,1024]{1,0:T(8,128)(2,1)S(1)} %collective-permute-done.1.refs_0_.refs_8_.refs_15_, ...), custom_call_target="tpu_custom_call", output_to_operand_aliasing={{0}: (18, {}), {1}: (19, {})} | custom-call | flops 1000 | bytes 1048576 | tf_op jit(solution)/shard_map/softmax/pallas_call | solution.py:508
  86.2 8.2 %softmax.10 = (bf16[256,4096]{1,0:T(8,128)(2,1)}, s32[1]{0:T(128)}) custom-call(s32[1]{0:T(128)} %bitcast.pos, bf16[256,4096]{1,0:T(8,128)(2,1)S(1)} %copy-done, bf16[256,1024]{1,0:T(8,128)(2,1)S(1)} %collective-permute-done.6.refs_0_.refs_4_.refs_23_, bf16[256,1024]{1,0:T(8,128)(2,1)S(1)} %collective-permute-done.8.refs_1_.refs_5_.refs_24_, ...), custom_call_target="tpu_custom_call" | custom-call | flops 1000 | bytes 1048576 | tf_op jit(solution)/shard_map/softmax/pallas_call | solution.py:508
  96.4 1.5 %collective-permute-done.21.recv_ref = bf16[2,1024,128]{2,1,0:T(8,128)(2,1)S(1)} collective-permute-done((bf16[2,1024,128]{2,1,0:T(8,128)(2,1)S(1)}, bf16[2,1024,128]{2,1,0:T(8,128)(2,1)S(1)}, u32[]{:S(2)}, u32[]{:S(2)}) %collective-permute-start.21) | collective-permute-done | bytes 524320 | tf_op jit(solution)/shard_map/ppermute | solution.py:554
  97.9 6.6 %light.1 = (bf16[256,4096]{1,0:T(8,128)(2,1)S(1)}, f32[256,128]{1,0:T(8,128)S(1)}, s32[1]{0:T(128)}) custom-call(s32[1]{0:T(128)} %bitcast.pos, bf16[256,4096]{1,0:T(8,128)(2,1)S(1)} %copy-done.5, bf16[256,4096]{1,0:T(8,128)(2,1)S(1)} %copy-done.2, bf16[256,4096]{1,0:T(8,128)(2,1)S(1)} %copy-done.3, f32[4,256,128]{2,1,0:T(8,128)S(1)} %get-tuple-element.48.cum_ref, ...), custom_call_target="tpu_custom_call" | custom-call | flops 1000 | bytes 1048576 | tf_op jit(solution)/shard_map/light/pallas_call | solution.py:281
  104.6 1.3 %collective-permute-start.22 = (f32[256,128]{1,0:T(8,128)S(1)}, f32[256,128]{1,0:T(8,128)S(1)}, u32[]{:S(2)}, u32[]{:S(2)}) collective-permute-start(f32[256,128]{1,0:T(8,128)S(1)} %get-tuple-element.87.refs_0_), channel_id=1, source_target_pairs={{0,1},{1,0},{2,3},{3,2},{4,5},{5,4},{6,7},{7,6},{8,9},{9,8},{10,11... | collective-permute-start | bytes 393224 | tf_op jit(solution)/shard_map/ppermute | solution.py:638
  105.9 7.9 %softmax.11 = (bf16[256,4096]{1,0:T(8,128)(2,1)}, s32[1]{0:T(128)}) custom-call(s32[1]{0:T(128)} %bitcast.pos, bf16[256,4096]{1,0:T(8,128)(2,1)S(1)} %copy-done, bf16[256,1024]{1,0:T(8,128)(2,1)S(1)} %collective-permute-done.6.refs_0_.refs_4_.refs_23_, ...), custom_call_target="tpu_custom_call", output_to_operand_aliasing={{0}: (29, {})} | custom-call | flops 1000 | bytes 1048576 | tf_op jit(solution)/shard_map/softmax/pallas_call | solution.py:508
  113.8 3.6 %finish.1 = bf16[256,4096]{1,0:T(8,128)(2,1)} custom-call(bf16[256,4096]{1,0:T(8,128)(2,1)S(1)} %get-tuple-element.86.raw_ref, f32[256,128]{1,0:T(8,128)S(1)} %get-tuple-element.87.refs_0_, f32[256,128]{1,0:T(8,128)S(1)} %collective-permute-done.22.refs_1_, f32[1,4096]{1,0:T(1,128)S(1)} %bitcast.4, bf16[256,4096]{1,0:T(8,128)(2,1)S(1)} %copy-done.4, ...), custom_call_target="tpu_custom_call" | custom-call | flops 1000 | bytes 1048576 | tf_op jit(solution)/shard_map/finish/pallas_call | solution.py:325
  (53 shorter events, 16.9 us)
Async XLA Ops:
  2.6 2.3 %collective-permute-start = (bf16[256,1024]{1,0:T(8,128)(2,1)S(1)}, bf16[256,1024]{1,0:T(8,128)(2,1)S(1)}, u32[]{:S(2)}, u32[]{:S(2)}) collective-permute-start(bf16[256,1024]{1,0:T(8,128)(2,1)S(1)} %constant_dynamic-update-slice_fusion.refs_0_.refs_4_.refs_11_), channel_id=1, source_target_pairs={{0,2},{2,0},{4,6},{6,4},{8,10},{10,8},{12,14},{14,12},{16,18},{18,... | collective-permute-start | bytes 1572872 | tf_op jit(solution)/shard_map/ppermute | solution.py:554
  3.3 13.5 %collective-permute-start.3 = (bf16[256,1024]{1,0:T(8,128)(2,1)S(1)}, bf16[256,1024]{1,0:T(8,128)(2,1)S(1)}, u32[]{:S(2)}, u32[]{:S(2)}) collective-permute-start(bf16[256,1024]{1,0:T(8,128)(2,1)S(1)} %constant_dynamic-update-slice_fusion.refs_0_.refs_4_.refs_11_), channel_id=1, source_target_pairs={{0,4},{2,6},{4,0},{6,2},{8,12},{10,14},{12,8},{14,10},{16,20},{18,... | collective-permute-start | bytes 1572872 | tf_op jit(solution)/shard_map/ppermute | solution.py:557
  3.6 15.0 %collective-permute-start.1 = (bf16[256,1024]{1,0:T(8,128)(2,1)S(1)}, bf16[256,1024]{1,0:T(8,128)(2,1)S(1)}, u32[]{:S(2)}, u32[]{:S(2)}) collective-permute-start(bf16[256,1024]{1,0:T(8,128)(2,1)S(1)} %constant_dynamic-update-slice_fusion.refs_0_.refs_4_.refs_11_), channel_id=1, source_target_pairs={{0,8},{2,10},{4,12},{6,14},{8,16},{10,18},{12,20},{14,22},{16,24},... | collective-permute-start | bytes 1572872 | tf_op jit(solution)/shard_map/ppermute | solution.py:560
  8.9 12.4 %copy-start = (bf16[256,4096]{1,0:T(8,128)(2,1)S(1)}, bf16[256,4096]{1,0:T(8,128)(2,1)}, u32[]{:S(2)}) copy-start(bf16[256,4096]{1,0:T(8,128)(2,1)} %q_ref.13) | copy-start | bytes 6291460
  14.0 14.4 %collective-permute-start.5 = (bf16[2,1040,128]{2,1,0:T(8,128)(2,1)S(1)}, bf16[2,1040,128]{2,1,0:T(8,128)(2,1)S(1)}, u32[]{:S(2)}, u32[]{:S(2)}) collective-permute-start(bf16[2,1040,128]{2,1,0:T(8,128)(2,1)S(1)} %get-tuple-element.54), channel_id=1, source_target_pairs={{0,2},{2,0},{4,6},{6,4},{8,10},{10,8},{12,14},{14,12},{16,18},{18,... | collective-permute-start | bytes 1597448 | tf_op jit(solution)/shard_map/ppermute | solution.py:554
  16.8 4.4 %collective-permute-start.4 = (bf16[256,1024]{1,0:T(8,128)(2,1)S(1)}, bf16[256,1024]{1,0:T(8,128)(2,1)S(1)}, u32[]{:S(2)}, u32[]{:S(2)}) collective-permute-start(bf16[256,1024]{1,0:T(8,128)(2,1)S(1)} %collective-permute-done.3.refs_1_.refs_5_.refs_12_), channel_id=1, source_target_pairs={{0,2},{2,0},{4,6},{6,4},{8,10},{10,8},{12,14},{14,12},{16,18},{18,... | collective-permute-start | bytes 1572872 | tf_op jit(solution)/shard_map/ppermute | solution.py:554
  18.7 14.1 %collective-permute-start.2 = (bf16[256,1024]{1,0:T(8,128)(2,1)S(1)}, bf16[256,1024]{1,0:T(8,128)(2,1)S(1)}, u32[]{:S(2)}, u32[]{:S(2)}) collective-permute-start(bf16[256,1024]{1,0:T(8,128)(2,1)S(1)} %collective-permute-done.1.refs_0_.refs_8_.refs_15_), channel_id=1, source_target_pairs={{0,8},{2,10},{4,12},{6,14},{8,16},{10,18},{12,20},{14,22},{16,24},... | collective-permute-start | bytes 1572872 | tf_op jit(solution)/shard_map/ppermute | solution.py:560
  19.9 22.9 %collective-permute-start.9 = (bf16[256,1024]{1,0:T(8,128)(2,1)S(1)}, bf16[256,1024]{1,0:T(8,128)(2,1)S(1)}, u32[]{:S(2)}, u32[]{:S(2)}) collective-permute-start(bf16[256,1024]{1,0:T(8,128)(2,1)S(1)} %collective-permute-done.1.refs_0_.refs_8_.refs_15_), channel_id=1, source_target_pairs={{0,4},{2,6},{4,0},{6,2},{8,12},{10,14},{12,8},{14,10},{16,20},{18,... | collective-permute-start | bytes 1572872 | tf_op jit(solution)/shard_map/ppermute | solution.py:557
  32.8 21.3 %collective-permute-start.12 = (bf16[256,1024]{1,0:T(8,128)(2,1)S(1)}, bf16[256,1024]{1,0:T(8,128)(2,1)S(1)}, u32[]{:S(2)}, u32[]{:S(2)}) collective-permute-start(bf16[256,1024]{1,0:T(8,128)(2,1)S(1)} %collective-permute-done.2.refs_4_.refs_12_.refs_19_), channel_id=1, source_target_pairs={{0,4},{2,6},{4,0},{6,2},{8,12},{10,14},{12,8},{14,10},{16,20},{18,... | collective-permute-start | bytes 1572872 | tf_op jit(solution)/shard_map/ppermute | solution.py:557
  34.0 20.1 %collective-permute-start.6 = (bf16[256,1024]{1,0:T(8,128)(2,1)S(1)}, bf16[256,1024]{1,0:T(8,128)(2,1)S(1)}, u32[]{:S(2)}, u32[]{:S(2)}) collective-permute-start(bf16[256,1024]{1,0:T(8,128)(2,1)S(1)} %collective-permute-done.2.refs_4_.refs_12_.refs_19_), channel_id=1, source_target_pairs={{0,8},{2,10},{4,12},{6,14},{8,16},{10,18},{12,20},{14,22},{16,24},... | collective-permute-start | bytes 1572872 | tf_op jit(solution)/shard_map/ppermute | solution.py:560
  35.3 14.5 %collective-permute-start.7 = (bf16[1040,128]{1,0:T(8,128)(2,1)S(1)}, bf16[1040,128]{1,0:T(8,128)(2,1)S(1)}, u32[]{:S(2)}, u32[]{:S(2)}) collective-permute-start(bf16[1040,128]{1,0:T(8,128)(2,1)S(1)} %get-tuple-element.61), channel_id=1, source_target_pairs={{0,4},{2,6},{4,0},{6,2},{8,12},{10,14},{12,8},{14,10},{16,20},{18,... | collective-permute-start | bytes 798728 | tf_op jit(solution)/shard_map/ppermute | solution.py:557
  42.8 12.5 %collective-permute-start.10 = (bf16[256,1024]{1,0:T(8,128)(2,1)S(1)}, bf16[256,1024]{1,0:T(8,128)(2,1)S(1)}, u32[]{:S(2)}, u32[]{:S(2)}) collective-permute-start(bf16[256,1024]{1,0:T(8,128)(2,1)S(1)} %collective-permute-done.1.refs_0_.refs_8_.refs_15_), channel_id=1, source_target_pairs={{0,2},{2,0},{4,6},{6,4},{8,10},{10,8},{12,14},{14,12},{16,18},{18,... | collective-permute-start | bytes 1572872 | tf_op jit(solution)/shard_map/ppermute | solution.py:554
  45.5 11.1 %collective-permute-start.11 = (bf16[256,1024]{1,0:T(8,128)(2,1)S(1)}, bf16[256,1024]{1,0:T(8,128)(2,1)S(1)}, u32[]{:S(2)}, u32[]{:S(2)}) collective-permute-start(bf16[256,1024]{1,0:T(8,128)(2,1)S(1)} %collective-permute-done.9.refs_1_.refs_9_.refs_16_), channel_id=1, source_target_pairs={{0,2},{2,0},{4,6},{6,4},{8,10},{10,8},{12,14},{14,12},{16,18},{18,... | collective-permute-start | bytes 1572872 | tf_op jit(solution)/shard_map/ppermute | solution.py:554
  51.0 7.0 %collective-permute-start.13 = (bf16[256,1024]{1,0:T(8,128)(2,1)S(1)}, bf16[256,1024]{1,0:T(8,128)(2,1)S(1)}, u32[]{:S(2)}, u32[]{:S(2)}) collective-permute-start(bf16[256,1024]{1,0:T(8,128)(2,1)S(1)} %collective-permute-done.2.refs_4_.refs_12_.refs_19_), channel_id=1, source_target_pairs={{0,2},{2,0},{4,6},{6,4},{8,10},{10,8},{12,14},{14,12},{16,18},{18,... | collective-permute-start | bytes 1572872 | tf_op jit(solution)/shard_map/ppermute | solution.py:554
  54.0 5.4 %collective-permute-start.14 = (bf16[256,1024]{1,0:T(8,128)(2,1)S(1)}, bf16[256,1024]{1,0:T(8,128)(2,1)S(1)}, u32[]{:S(2)}, u32[]{:S(2)}) collective-permute-start(bf16[256,1024]{1,0:T(8,128)(2,1)S(1)} %collective-permute-done.12.refs_5_.refs_13_.refs_20_), channel_id=1, source_target_pairs={{0,2},{2,0},{4,6},{6,4},{8,10},{10,8},{12,14},{14,12},{16,18},{18,... | collective-permute-start | bytes 1572872 | tf_op jit(solution)/shard_map/ppermute | solution.py:554
  54.1 18.3 %collective-permute-start.8 = (bf16[256,1024]{1,0:T(8,128)(2,1)S(1)}, bf16[256,1024]{1,0:T(8,128)(2,1)S(1)}, u32[]{:S(2)}, u32[]{:S(2)}) collective-permute-start(bf16[256,1024]{1,0:T(8,128)(2,1)S(1)} %collective-permute-done.6.refs_0_.refs_4_.refs_23_), channel_id=1, source_target_pairs={{0,4},{2,6},{4,0},{6,2},{8,12},{10,14},{12,8},{14,10},{16,20},{18,... | collective-permute-start | bytes 1572872 | tf_op jit(solution)/shard_map/ppermute | solution.py:557
  55.3 29.3 %collective-permute-start.19 = (bf16[1040,128]{1,0:T(8,128)(2,1)S(1)}, bf16[1040,128]{1,0:T(8,128)(2,1)S(1)}, u32[]{:S(2)}, u32[]{:S(2)}) collective-permute-start(bf16[1040,128]{1,0:T(8,128)(2,1)S(1)} %get-tuple-element.78), channel_id=1, source_target_pairs={{0,24},{2,26},{4,28},{6,30},{1,25},{3,27},{5,29},{7,31}} | collective-permute-start | bytes 798728 | tf_op jit(solution)/shard_map/ppermute | solution.py:560
  56.6 28.0 %collective-permute-start.18 = (bf16[1040,128]{1,0:T(8,128)(2,1)S(1)}, bf16[1040,128]{1,0:T(8,128)(2,1)S(1)}, u32[]{:S(2)}, u32[]{:S(2)}) collective-permute-start(bf16[1040,128]{1,0:T(8,128)(2,1)S(1)} %get-tuple-element.78), channel_id=1, source_target_pairs={{0,16},{2,18},{4,20},{6,22},{8,24},{10,26},{12,28},{14,30},{1,17},... | collective-permute-start | bytes 798728 | tf_op jit(solution)/shard_map/ppermute | solution.py:560
  58.0 26.7 %collective-permute-start.17 = (bf16[1040,128]{1,0:T(8,128)(2,1)S(1)}, bf16[1040,128]{1,0:T(8,128)(2,1)S(1)}, u32[]{:S(2)}, u32[]{:S(2)}) collective-permute-start(bf16[1040,128]{1,0:T(8,128)(2,1)S(1)} %get-tuple-element.78), channel_id=1, source_target_pairs={{0,8},{2,10},{4,12},{6,14},{8,16},{10,18},{12,20},{14,22},{16,24},... | collective-permute-start | bytes 798728 | tf_op jit(solution)/shard_map/ppermute | solution.py:560
  71.6 14.6 %collective-permute-start.15 = (bf16[256,1024]{1,0:T(8,128)(2,1)S(1)}, bf16[256,1024]{1,0:T(8,128)(2,1)S(1)}, u32[]{:S(2)}, u32[]{:S(2)}) collective-permute-start(bf16[256,1024]{1,0:T(8,128)(2,1)S(1)} %collective-permute-done.6.refs_0_.refs_4_.refs_23_), channel_id=1, source_target_pairs={{0,2},{2,0},{4,6},{6,4},{8,10},{10,8},{12,14},{14,12},{16,18},{18,... | collective-permute-start | bytes 1572872 | tf_op jit(solution)/shard_map/ppermute | solution.py:554
  72.4 13.8 %collective-permute-start.16 = (bf16[256,1024]{1,0:T(8,128)(2,1)S(1)}, bf16[256,1024]{1,0:T(8,128)(2,1)S(1)}, u32[]{:S(2)}, u32[]{:S(2)}) collective-permute-start(bf16[256,1024]{1,0:T(8,128)(2,1)S(1)} %collective-permute-done.8.refs_1_.refs_5_.refs_24_), channel_id=1, source_target_pairs={{0,2},{2,0},{4,6},{6,4},{8,10},{10,8},{12,14},{14,12},{16,18},{18,... | collective-permute-start | bytes 1572872 | tf_op jit(solution)/shard_map/ppermute | solution.py:554
  85.9 8.6 %collective-permute-start.20 = (bf16[1040,128]{1,0:T(8,128)(2,1)S(1)}, bf16[1040,128]{1,0:T(8,128)(2,1)S(1)}, u32[]{:S(2)}, u32[]{:S(2)}) collective-permute-start(bf16[1040,128]{1,0:T(8,128)(2,1)S(1)} %get-tuple-element.82), channel_id=1, source_target_pairs={{0,4},{2,6},{4,0},{6,2},{8,12},{10,14},{12,8},{14,10},{16,20},{18,... | collective-permute-start | bytes 798728 | tf_op jit(solution)/shard_map/ppermute | solution.py:557
  95.6 2.3 %collective-permute-start.21 = (bf16[2,1024,128]{2,1,0:T(8,128)(2,1)S(1)}, bf16[2,1024,128]{2,1,0:T(8,128)(2,1)S(1)}, u32[]{:S(2)}, u32[]{:S(2)}) collective-permute-start(bf16[2,1024,128]{2,1,0:T(8,128)(2,1)S(1)} %get-tuple-element.84), channel_id=1, source_target_pairs={{0,2},{2,0},{4,6},{6,4},{8,10},{10,8},{12,14},{14,12},{16,18},{18,... | collective-permute-start | bytes 1572872 | tf_op jit(solution)/shard_map/ppermute | solution.py:554
  104.6 9.3 %collective-permute-start.22 = (f32[256,128]{1,0:T(8,128)S(1)}, f32[256,128]{1,0:T(8,128)S(1)}, u32[]{:S(2)}, u32[]{:S(2)}) collective-permute-start(f32[256,128]{1,0:T(8,128)S(1)} %get-tuple-element.87.refs_0_), channel_id=1, source_target_pairs={{0,1},{1,0},{2,3},{3,2},{4,5},{5,4},{6,7},{7,6},{8,9},{9,8},{10,11... | collective-permute-start | bytes 393224 | tf_op jit(solution)/shard_map/ppermute | solution.py:638
  (7 other events, 43.3 us)
